TPU v7x, 768 devices: a whole 4x8x12 slice. The times are simulated.
768 devices in a mesh: pair: 32 (over y, x), aux: 24 (over z, core).
Axes of the slice: x: 4, y: 8, z: 12, core: 2. Of those that a mesh axis runs over, the one named last changes fastest.
Arguments:
- amplitudes: bfloat16 [24, 32, 256, 256], P('aux', None, None, 'pair'), may hold values from -4 to 4
- integrals: bfloat16 [24, 32, 2016, 512], P(None, 'pair', 'aux'), may hold values from -1 to 1
- pair_occ: int32 [24, 32, 2], P('aux', 'pair'), may hold values from 0 to 99
- dom_tiles: int32 [24, 32, 2], P('aux', 'pair'), may hold values from 0 to 11, as said below
- dom_mask: int32 [24, 32, 2], P('aux', 'pair'), may hold values 0 or 1
- virt_energy: float32 [1536], replicated, may hold values from 0.3 to 3
- occ_energy: float32 [100], replicated, may hold values from -1.5 to -0.3
Outputs:
- residual: float32 [24, 32, 256, 256], P('aux', 'pair')
Inputs may be any that keep to these rules, and one draw needn't show every extreme that they name: `dom_tiles`: the 2 tile ids of one pair are distinct and ascending.
All inputs are finite; a program needn't handle non-finite values. No bound on the sum of `dom_mask` on one device may be relied on, other than what follows from the above.
Results may differ from a plain program's by a relative error of at most 0.0016.
Values may be sent and summed in bfloat16 or wider, within the bound.
No kernel may reach another device: no remote copies, remote signals or barrier semaphores. Data moves between devices by JAX's collectives and lax.ppermute only.
A program may use at most 64 MiB of HBM per device.

v0:
```python
import jax
import jax.numpy as jnp
from jax import lax
from jax.sharding import PartitionSpec as P

TILE = 128


def domain_terms(block, amps):
    width = amps.shape[-1]
    left = block[..., :width]
    right = block[..., width:]
    first = jnp.einsum("gmqa,gmab->gmqb", left, amps, preferred_element_type=jnp.float32).astype(
        jnp.bfloat16
    )
    second = jnp.einsum("gmqa,gmba->gmqb", left, amps, preferred_element_type=jnp.float32).astype(
        jnp.bfloat16
    )
    direct = jnp.einsum("gmqa,gmqb->gmab", left, right, preferred_element_type=jnp.float32)
    dressed = jnp.einsum("gmqa,gmqb->gmab", left, first, preferred_element_type=jnp.float32)
    mirror = jnp.einsum("gmqa,gmqb->gmab", second, left, preferred_element_type=jnp.float32)
    return direct - dressed - mirror


def on_device(amplitudes, integrals, pair_occ, dom_tiles, dom_mask, virt_energy, occ_energy):
    owned = lax.all_to_all(amplitudes, "pair", split_axis=1, concat_axis=3, tiled=True)
    gathered = lax.all_to_all(integrals, "aux", split_axis=0, concat_axis=2, tiled=True)
    summed = domain_terms(gathered, owned)
    tile_count = virt_energy.shape[0] // TILE
    onehot_tiles = (dom_tiles[..., None] == jnp.arange(tile_count, dtype=jnp.int32)).astype(
        jnp.float32
    )
    table = virt_energy.reshape(tile_count, TILE)
    e_dom = jnp.einsum("gmsn,nt->gmst", onehot_tiles, table, precision=lax.Precision.HIGHEST)
    e_dom = e_dom.reshape(owned.shape[0], owned.shape[1], owned.shape[2])
    onehot_occ = (pair_occ[..., None] == jnp.arange(occ_energy.shape[0], dtype=jnp.int32)).astype(
        jnp.float32
    )
    f_sum = jnp.sum(onehot_occ * occ_energy, axis=(-1, -2))
    delta = e_dom[..., :, None] + e_dom[..., None, :] - f_sum[..., None, None]
    keep = jnp.repeat(dom_mask.astype(jnp.float32), TILE, axis=-1)
    outer = keep[..., :, None] * keep[..., None, :]
    return outer * (summed + delta * owned.astype(jnp.float32))


def solution(mesh):
    return jax.shard_map(
        on_device,
        mesh=mesh,
        in_specs=(
            P("aux", None, None, "pair"),
            P(None, "pair", "aux", None),
            P("aux", "pair", None),
            P("aux", "pair", None),
            P("aux", "pair", None),
            P(),
            P(),
        ),
        out_specs=P("aux", "pair", None, None),
        check_vma=False,
    )
```

profile of v0, /device:TPU:1, one launch (start us, length us, event | category | flops | bytes accessed | tf_op | source)
XLA Modules:
  0.0 119.7 jit_solution(4262751347365015672)
XLA Ops:
  0.0 0.0 copy-start
  0.0 10.6 %all-to-all-start.1 = ((bf16[1,32,256,8]{2,3,0,1:T(8,128)(2,1)}), bf16[1,32,256,8]{2,3,0,1:T(8,128)(2,1)S(1)}, u32[]{:S(2)}, u32[]{:S(2)}) async-start(bf16[1,32,256,8]{2,3,0,1:T(8,128)(2,1)} %bitcast.43), calls=%async_computation.1 | async-start | bytes 262144 | tf_op jit(solution)/shard_map/all_to_all | solution.py:26
  10.6 3.6 %copy.17 = bf16[24,1,84,512]{3,2,1,0:T(8,128)(2,1)} copy(bf16[24,1,84,512]{3,0,2,1:T(8,128)(2,1)} %param.8) | data formatting | bytes 4128768 | tf_op args[1]
  14.2 0.0 copy-start.2
  14.3 0.0 copy-start.3
  14.3 0.0 copy-start.4
  14.3 0.0 copy-start.5
  14.3 5.7 %all-to-all-done.1 = bf16[1,32,256,8]{2,3,0,1:T(8,128)(2,1)S(1)} async-done(((bf16[1,32,256,8]{2,3,0,1:T(8,128)(2,1)}), bf16[1,32,256,8]{2,3,0,1:T(8,128)(2,1)S(1)}, u32[]{:S(2)}, u32[]{:S(2)}) %all-to-all-start.1) | async-done | bytes 131104 | tf_op jit(solution)/shard_map/all_to_all | solution.py:26
  20.0 17.3 %all-to-all-start = ((bf16[24,1,84,512]{3,2,1,0:T(8,128)(2,1)}), bf16[24,1,84,512]{3,2,1,0:T(8,128)(2,1)S(1)}, u32[]{:S(2)}, u32[]{:S(2)}) async-start(bf16[24,1,84,512]{3,2,1,0:T(8,128)(2,1)} %copy.17), calls=%async_computation | async-start | bytes 4325376 | tf_op jit(solution)/shard_map/all_to_all | solution.py:27
  37.2 0.0 copy-done.2
  37.3 0.0 copy-done.3
  37.3 0.7 fusion.12
  38.0 0.0 copy-done
  38.0 0.0 copy-done.4
  38.0 0.2 convolution_bitcast_fusion
  38.2 0.0 copy-done.5
  38.2 0.1 broadcast_bitcast_fusion
  38.3 0.1 copy.20
  38.4 73.9 %all-to-all-done = bf16[24,1,84,512]{3,2,1,0:T(8,128)(2,1)S(1)} async-done(((bf16[24,1,84,512]{3,2,1,0:T(8,128)(2,1)}), bf16[24,1,84,512]{3,2,1,0:T(8,128)(2,1)S(1)}, u32[]{:S(2)}, u32[]{:S(2)}) %all-to-all-start) | async-done | bytes 2064416 | tf_op jit(solution)/shard_map/all_to_all | solution.py:27
  112.2 2.0 %all_to_all.21 = bf16[1,1,2016,512]{3,2,1,0:T(8,128)(2,1)} reshape(bf16[24,1,84,512]{3,2,1,0:T(8,128)(2,1)S(1)} %all-to-all-done) | data formatting | bytes 4128768 | tf_op jit(solution)/shard_map/all_to_all | solution.py:27
  114.2 0.0 copy-start.1
  114.2 2.1 %fusion.8 = f32[256,256]{1,0:T(8,128)S(1)} fusion(bf16[1,1,2016,512]{3,2,1,0:T(8,128)(2,1)} %all_to_all.21), kind=kOutput, calls=%fused_computation.12 | convolution fusion | flops 264241152 | bytes 2326528 | tf_op jit(solution)/shard_map/gmqa,gmqb->gmab/dot_general | solution.py:19
  116.4 0.0 copy-done.1
  116.4 0.9 fusion.7
  117.4 2.3 %fusion.5 = f32[1,1,256,256]{3,2,1,0:T(8,128)} fusion(f32[256,256]{1,0:T(8,128)S(1)} %fusion.7, bf16[1,1,2016,512]{3,2,1,0:T(8,128)(2,1)S(1)} %copy-done.1, bf16[256,256]{1,0:T(8,128)(2,1)S(1)} %copy.20, f32[]{:T(128)} %fusion.12, f32[256]{0:T(256)S(1)} %convolution_bitcast_fusion, f32[256]{0:T(256)S(1)} %broadcast_bitcast_fusion, ...), kind=kOutput, calls=%fused_computation.7 | convolution fusion | flops 529522688 | bytes 2854916 | tf_op jit(solution)/shard_map/gmqa,gmqb->gmab/dot_general | solution.py:21
  (1 shorter events, 0.0 us)
Async XLA Ops:
  0.0 38.0 %copy-start = (f32[1536]{0:T(1024)S(1)}, f32[1536]{0:T(1024)}, u32[]{:S(2)}) copy-start(f32[1536]{0:T(1024)} %param.12) | copy-start | bytes 18436
  0.0 20.0 %all-to-all-start.1 = ((bf16[1,32,256,8]{2,3,0,1:T(8,128)(2,1)}), bf16[1,32,256,8]{2,3,0,1:T(8,128)(2,1)S(1)}, u32[]{:S(2)}, u32[]{:S(2)}) async-start(bf16[1,32,256,8]{2,3,0,1:T(8,128)(2,1)} %bitcast.43), calls=%async_computation.1 | async-start | bytes 262144 | tf_op jit(solution)/shard_map/all_to_all | solution.py:26
  14.2 23.0 %copy-start.2 = (f32[100]{0:T(128)S(1)}, f32[100]{0:T(128)}, u32[]{:S(2)}) copy-start(f32[100]{0:T(128)} %param.13) | copy-start | bytes 1204
  14.3 23.0 %copy-start.3 = (s32[1,1,2]{2,1,0:T(1,128)S(1)}, s32[1,1,2]{2,1,0:T(1,128)}, u32[]{:S(2)}) copy-start(s32[1,1,2]{2,1,0:T(1,128)} %param.9) | copy-start | bytes 28
  14.3 23.8 %copy-start.4 = (s32[1,1,2]{2,1,0:T(1,128)S(1)}, s32[1,1,2]{2,1,0:T(1,128)}, u32[]{:S(2)}) copy-start(s32[1,1,2]{2,1,0:T(1,128)} %param.10) | copy-start | bytes 28
  14.3 23.9 %copy-start.5 = (s32[1,1,2]{2,1,0:T(1,128)S(1)}, s32[1,1,2]{2,1,0:T(1,128)}, u32[]{:S(2)}) copy-start(s32[1,1,2]{2,1,0:T(1,128)} %param.11) | copy-start | bytes 28
  20.0 92.2 %all-to-all-start = ((bf16[24,1,84,512]{3,2,1,0:T(8,128)(2,1)}), bf16[24,1,84,512]{3,2,1,0:T(8,128)(2,1)S(1)}, u32[]{:S(2)}, u32[]{:S(2)}) async-start(bf16[24,1,84,512]{3,2,1,0:T(8,128)(2,1)} %copy.17), calls=%async_computation | async-start | bytes 4325376 | tf_op jit(solution)/shard_map/all_to_all | solution.py:27
  114.2 2.2 %copy-start.1 = (bf16[1,1,2016,512]{3,2,1,0:T(8,128)(2,1)S(1)}, bf16[1,1,2016,512]{3,2,1,0:T(8,128)(2,1)}, u32[]{:S(2)}) copy-start(bf16[1,1,2016,512]{3,2,1,0:T(8,128)(2,1)} %all_to_all.21) | copy-start | bytes 6193156
where the time goes:
time: 120 us
  waiting for transfers between devices  79.6 us (66%)
  starting transfers between devices  27.9 us (23%)
  local copies, waits for them, and re-layouts  5.85 us (5%)
  matrix products  5.53 us (5%)
    all_to_all x1, waiting for transfers between devices, on_device(): lax.all_to_all(integrals, 'aux', split_axis=0, concat_axis=2, tiled=True)  73.9 us
    all_to_all x1, starting transfers between devices, on_device(): lax.all_to_all(integrals, 'aux', split_axis=0, concat_axis=2, tiled=True)  17.3 us
    all_to_all x1, starting transfers between devices, on_device(): lax.all_to_all(amplitudes, 'pair', split_axis=1, concat_axis=3, tiled=True)  10.6 us
    all_to_all x1, waiting for transfers between devices, on_device(): lax.all_to_all(amplitudes, 'pair', split_axis=1, concat_axis=3, tiled=True)  5.73 us
    unnamed x13, local copies, waits for them, and re-layouts  3.67 us
  transfers between devices with their start and end apart: 2, of which 2 were waited for; matrix products, arithmetic and copies ran while one was open for 4% of the time, Pallas kernels for 0%

commit v1 on v0

v1 whole, which is shorter than its diff:
```python
import functools

import jax
import jax.numpy as jnp
from jax import lax
from jax.experimental import pallas as pl
from jax.experimental.pallas import tpu as pltpu
from jax.sharding import PartitionSpec as P

TILE = 128
HOPS = 3
ROWS = 6 * TILE + 8
F32 = jnp.float32
BF16 = jnp.bfloat16


def iotas():
    return (
        lax.broadcasted_iota(jnp.int32, (TILE, TILE), 0),
        lax.broadcasted_iota(jnp.int32, (TILE, TILE), 1),
    )


def packed_sum(blocks, store):
    def product(cols):
        total = None
        for block in blocks:
            term = lax.dot_general(
                block[:, : 2 * TILE],
                block[:, cols * TILE : (cols + 1) * TILE],
                (((0,), (0,)), ((), ())),
                preferred_element_type=F32,
            )
            total = term if total is None else total + term
        return total

    row, col = iotas()
    store(0, product(2))
    store(2 * TILE, product(3))
    g0 = product(0)
    g1 = product(1)
    store(4 * TILE, g1[:TILE])
    store(5 * TILE, jnp.where(row <= col, g0[:TILE], g1[TILE:]))
    diag = jnp.sum(jnp.where(row == col, g1[TILE:], 0.0), axis=0, keepdims=True)
    store(6 * TILE, jnp.broadcast_to(diag, (8, TILE)))


def pack_kernel(idx, own, other, *outs):
    for n, out in enumerate(outs):
        out[0] = own[idx[n]]
        out[1] = other[idx[n]]


def pre_kernel(idx, own, other, out):
    def store(at, value):
        out[0, at : at + value.shape[0], :] = value

    packed_sum([own[0], other[0]], store)


def start_kernel(base, half, *rest):
    out = rest[-1]

    def store(at, value):
        out[at : at + value.shape[0], :] = value + base[at : at + value.shape[0], :]

    blocks = [half[0]]
    for ref in rest[:-1]:
        blocks += [ref[0], ref[1]]
    packed_sum(blocks, store)


def final_kernel(occ_at, tiles, mask, occ, virt, pa, pb, pc, amps_t, out):
    row, col = iotas()

    def part(at, rows):
        return pa[at : at + rows, :] + pb[at : at + rows, :] + pc[at : at + rows, :]

    h = jnp.concatenate([part(0, 2 * TILE), part(2 * TILE, 2 * TILE)], axis=1)
    g01 = part(4 * TILE, TILE)
    fold = part(5 * TILE, TILE)
    diag = part(6 * TILE, 8)[:1]
    above = jnp.where(row < col, fold, 0.0)
    below = jnp.where(row > col, fold, 0.0)
    g00 = jnp.where(row <= col, fold, 0.0) + above.T
    g11 = below + below.T + jnp.where(row == col, diag, 0.0)
    g = jnp.concatenate(
        [jnp.concatenate([g00, g01], axis=1), jnp.concatenate([g01.T, g11], axis=1)], axis=0
    )
    tt = amps_t[...]
    total = h
    rest = g
    for _ in range(3):
        piece = rest.astype(BF16)
        rest = rest - piece.astype(F32)
        total = total - lax.dot_general(
            piece, tt, (((1,), (1,)), ((), ())), preferred_element_type=F32
        )
        total = total - lax.dot_general(
            tt, piece, (((0,), (0,)), ((), ())), preferred_element_type=F32
        )
    f_sum = occ[occ_at[0]] + occ[occ_at[1]]
    t = tt.astype(F32).T
    e_row = [virt[pl.ds(tiles[s], 1), :] for s in range(2)]
    e_col = [jnp.sum(jnp.where(row == col, e, 0.0), axis=1, keepdims=True) for e in e_row]
    keep = [mask[s].astype(F32) for s in range(2)]
    for a in range(2):
        for b in range(2):
            at = (slice(a * TILE, (a + 1) * TILE), slice(b * TILE, (b + 1) * TILE))
            delta = (e_col[a] + e_row[b]) - f_sum
            out[at] = (keep[a] * keep[b]) * (total[at] + delta * t[at])


def on_device(chips, amplitudes, integrals, pair_occ, dom_tiles, dom_mask, virt_energy, occ_energy):
    naux, wide = integrals.shape[2:]
    far = chips // 2
    me = lax.axis_index("aux")
    z, c = me // 2, me % 2
    vmem = pl.BlockSpec(memory_space=pltpu.VMEM)
    smem = pl.BlockSpec(memory_space=pltpu.SMEM)

    def sign(core, stream):
        return 1 - 2 * ((core + stream) % 2)

    def permute(x, stream, hops, cross=False):
        pairs = []
        for chip in range(chips):
            for core in range(2):
                to = (chip + sign(core, stream) * hops) % chips
                pairs.append((chip * 2 + core, to * 2 + (core ^ int(cross))))
        return lax.ppermute(x, "aux", pairs)

    def dest(stream, distance):
        return lax.rem(z + sign(c, stream) * distance + chips, chips)

    by_chip = integrals.reshape(chips, 2, naux, wide)
    other = lax.dynamic_index_in_dim(by_chip, 1 - c, 1, keepdims=False)
    own = lax.dynamic_index_in_dim(by_chip, c, 1, keepdims=False)
    across = lax.rem(z + far, chips)
    half = [
        permute(lax.dynamic_slice_in_dim(own, across, 1, 0), 0, far - HOPS),
        permute(lax.dynamic_slice_in_dim(other, across, 1, 0), 0, far - HOPS, cross=True),
    ]
    other = lax.ppermute(other, "aux", [(i, i ^ 1) for i in range(2 * chips)])

    ways = [(s, d) for d in range(far - 1, HOPS, -1) for s in range(2)]
    idx = jnp.stack([dest(s, d) for s, d in ways]).astype(jnp.int32)
    sends = pl.pallas_call(
        pack_kernel,
        in_specs=[smem, vmem, vmem],
        out_specs=[vmem] * len(ways),
        out_shape=[jax.ShapeDtypeStruct((2, naux, wide), BF16)] * len(ways),
        name="pack_rows",
    )(idx, own, other)
    rows = [[], []]
    for (s, d), x in zip(ways, sends):
        rows[s].append(permute(x, s, d - HOPS))

    near = [(s, d) for d in range(HOPS, 0, -1) for s in range(2)] + [(0, 0)]
    idx = jnp.stack([dest(s, d) for s, d in near]).astype(jnp.int32)
    block = pl.BlockSpec((1, naux, wide), lambda n, at: (at[n], 0, 0))
    local = pl.pallas_call(
        pre_kernel,
        grid_spec=pltpu.PrefetchScalarGridSpec(
            num_scalar_prefetch=1,
            grid=(len(near),),
            in_specs=[block, block],
            out_specs=pl.BlockSpec((1, ROWS, TILE), lambda n, at: (n, 0, 0)),
        ),
        out_shape=jax.ShapeDtypeStruct((len(near), ROWS, TILE), F32),
        name="own_sums",
    )(idx, own, other)

    owned = lax.all_to_all(amplitudes, "pair", split_axis=1, concat_axis=3, tiled=True)
    amps_t = jnp.swapaxes(owned[0, 0], 0, 1)

    sums = []
    for s in range(2):
        sums.append(
            pl.pallas_call(
                start_kernel,
                in_specs=[vmem] * (2 + len(rows[s])),
                out_specs=vmem,
                out_shape=jax.ShapeDtypeStruct((ROWS, TILE), F32),
                name="far_sum",
            )(local[s], half[s], *rows[s])
        )
    for hop in range(HOPS):
        for s in range(2):
            sums[s] = permute(sums[s], s, 1)
            if hop < HOPS - 1:
                sums[s] = sums[s] + local[2 * (hop + 1) + s]

    out = pl.pallas_call(
        final_kernel,
        in_specs=[smem] * 4 + [vmem] * 5,
        out_specs=vmem,
        out_shape=jax.ShapeDtypeStruct((2 * TILE, 2 * TILE), F32),
        name="residual",
    )(
        pair_occ.reshape(-1),
        dom_tiles.reshape(-1),
        dom_mask.reshape(-1),
        occ_energy,
        virt_energy.reshape(-1, TILE),
        sums[0],
        sums[1],
        local[2 * HOPS],
        amps_t,
    )
    return out[None, None]


def solution(mesh):
    return jax.shard_map(
        functools.partial(on_device, mesh.shape["aux"] // 2),
        mesh=mesh,
        in_specs=(
            P("aux", None, None, "pair"),
            P(None, "pair", "aux", None),
            P("aux", "pair", None),
            P("aux", "pair", None),
            P("aux", "pair", None),
            P(),
            P(),
        ),
        out_specs=P("aux", "pair", None, None),
        check_vma=False,
    )
```

time: 120 us -> 132 us (1.10)
  waiting for transfers between devices: 79.6 us -> 17.1 us
  starting transfers between devices: 27.9 us -> 54.3 us
  blocking collectives: 0 us -> 18.9 us
  Pallas kernels: 0 us -> 16.9 us
  local copies, waits for them, and re-layouts: 5.85 us -> 22.4 us
  matrix products: 5.53 us -> 0 us
    all_to_all x2 -> x0, waiting for transfers between devices: 79.6 us -> none  [the longest x1 73.9 us: on_device(): lax.all_to_all(integrals, 'aux', split_axis=0, concat_axis=2, tiled=True)]
    ppermute x0 -> x13, starting transfers between devices: none -> 54.3 us  [the longest x12 41.9 us: permute(): return lax.ppermute(x, 'aux', pairs)]
    all_to_all x2 -> x0, starting transfers between devices: 27.9 us -> none  [the longest x1 17.3 us: on_device(): lax.all_to_all(integrals, 'aux', split_axis=0, concat_axis=2, tiled=True)]
    all_to_all x0 -> x1, blocking collectives: none -> 18.9 us  [on_device(): lax.all_to_all(amplitudes, 'pair', split_axis=1, concat_axis=3, tiled=True)]
    ppermute x0 -> x13, waiting for transfers between devices: none -> 17.1 us  [the longest x12 17.1 us: permute(): return lax.ppermute(x, 'aux', pairs)]
    pallas_call x0 -> x5, Pallas kernels: none -> 16.9 us  [the longest x1 7.04 us: on_device(): pl.pallas_call(pre_kernel, grid_spec=pltpu.PrefetchScalarGridSpec(num_sca...]
    dynamic_slice x0 -> x2, local copies, waits for them, and re-layouts: none -> 5.94 us  [the longest x1 5.57 us: on_device(): other = lax.dynamic_index_in_dim(by_chip, 1 - c, 1, keepdims=False)]
    unnamed x13 -> x24, local copies, waits for them, and re-layouts: 3.67 us -> 9.3 us
  transfers between devices with their start and end apart: 2 -> 13, of which waited for: 2 -> 5; matrix products, arithmetic and copies ran while one was open for 4% -> 6% of each run, Pallas kernels for 0% -> 11%
where the time goes in v1:
time: 132 us; the launch traced here: 131 us
  starting transfers between devices  54.3 us (41%)
  local copies, waits for them, and re-layouts  22.4 us (17%)
  blocking collectives  18.9 us (14%)
  waiting for transfers between devices  17.1 us (13%)
  Pallas kernels  16.9 us (13%)
    ppermute x12, starting transfers between devices, permute(): return lax.ppermute(x, 'aux', pairs)  41.9 us
    all_to_all x1, blocking collectives, on_device(): lax.all_to_all(amplitudes, 'pair', split_axis=1, concat_axis=3, tiled=True)  18.9 us
    ppermute x12, waiting for transfers between devices, permute(): return lax.ppermute(x, 'aux', pairs)  17.1 us
    ppermute x1, starting transfers between devices, on_device(): other = lax.ppermute(other, 'aux', [(i, i ^ 1) for i in range(2 * chips)])  12.4 us
    unnamed x24, local copies, waits for them, and re-layouts  9.3 us
    pallas_call x1, Pallas kernels, on_device(): pl.pallas_call(pre_kernel, grid_spec=pltpu.PrefetchScalarGridSpec(num_sca...  7.04 us
    dynamic_slice x1, local copies, waits for them, and re-layouts, on_device(): other = lax.dynamic_index_in_dim(by_chip, 1 - c, 1, keepdims=False)  5.57 us
    pallas_call x2, Pallas kernels, on_device(): pl.pallas_call(start_kernel, in_specs=[vmem] * (2 + len(rows[s])), out_sp...  4.94 us
  transfers between devices with their start and end apart: 13, of which 5 were waited for; matrix products, arithmetic and copies ran while one was open for 6% of the time, Pallas kernels for 11%

profile of v1, /device:TPU:1, one launch (start us, length us, event | category | flops | bytes accessed | tf_op | source)
XLA Modules:
  0.0 131.0 jit_solution(9612883795152322360)
XLA Ops:
  0.0 4.2 %reshape.22 = bf16[12,2,84,512]{3,1,0,2:T(2,128)(2,1)S(1)} reshape(bf16[24,1,84,512]{3,0,2,1:T(8,128)(2,1)} %param.8) | data formatting | bytes 4128768 | tf_op jit(solution)/shard_map/reshape | solution.py:136
  4.3 5.6 %constant_dynamic-slice_fusion.2 = (bf16[12,1,84,512]{3,1,0,2:T(2,128)(2,1)S(1)}, bf16[12,1,84,512]{3,1,0,2:T(2,128)(2,1)}) fusion(bf16[12,2,84,512]{3,1,0,2:T(2,128)(2,1)S(1)} %reshape.22, s32[]{:T(128)S(6)} %select_n.57, s32[]{:T(128)S(6)} %select_n.56), kind=kLoop, calls=%fused_computation.17 | loop fusion | bytes 4128776 | tf_op jit(solution)/shard_map/jit(dynamic_index_in_dim)/dynamic_slice | solution.py:137
  9.8 1.6 %copy.25 = bf16[12,1,84,512]{3,2,0,1:T(8,128)(2,1)} copy(bf16[12,1,84,512]{3,1,0,2:T(2,128)(2,1)S(1)} %get-tuple-element.22) | data formatting | bytes 2064384
  11.4 12.4 %collective-permute-start = (bf16[12,84,512]{2,1,0:T(8,128)(2,1)}, bf16[12,84,512]{2,1,0:T(8,128)(2,1)S(1)}, u32[]{:S(2)}, u32[]{:S(2)}) collective-permute-start(bf16[12,84,512]{2,1,0:T(8,128)(2,1)} %bitcast.58), channel_id=1, source_target_pairs={{0,1},{1,0},{2,3},{3,2},{4,5},{5,4},{6,7},{7,6},{8,9},{9,8},{10,11... | collective-permute-start | bytes 3096584 | tf_op jit(solution)/shard_map/ppermute | solution.py:144
  23.9 0.4 constant_dynamic-slice_fusion
  24.2 0.6 copy.28
  24.9 5.3 %collective-permute-start.1 = (bf16[1,84,512]{2,1,0:T(8,128)(2,1)}, bf16[1,84,512]{2,1,0:T(8,128)(2,1)}, u32[]{:S(2)}, u32[]{:S(2)}) collective-permute-start(bf16[1,84,512]{2,1,0:T(8,128)(2,1)} %bitcast.61), channel_id=1, source_target_pairs={{0,6},{1,19},{2,8},{3,21},{4,10},{5,23},{6,12},{7,1},{8,14},{9,3},... | collective-permute-start | bytes 258056 | tf_op jit(solution)/shard_map/ppermute | solution.py:131
  30.2 3.2 %collective-permute-start.7 = (bf16[1,84,512]{2,1,0:T(8,128)(2,1)S(1)}, bf16[1,84,512]{2,1,0:T(8,128)(2,1)S(1)}, u32[]{:S(2)}, u32[]{:S(2)}) collective-permute-start(bf16[1,84,512]{2,1,0:T(8,128)(2,1)S(1)} %bitcast.66), channel_id=1, source_target_pairs={{0,7},{1,18},{2,9},{3,20},{4,11},{5,22},{6,13},{7,0},{8,15},{9,2},... | collective-permute-start | bytes 258056 | tf_op jit(solution)/shard_map/ppermute | solution.py:131
  33.5 3.1 %copy.26 = bf16[12,1,84,512]{3,2,0,1:T(8,128)(2,1)} copy(bf16[12,1,84,512]{3,1,0,2:T(2,128)(2,1)} %get-tuple-element.23) | data formatting | bytes 2064384
  36.6 0.7 stack.46.idx
  37.3 0.7 pad_add_fusion.idx
  38.0 0.0 collective-permute-done.other
  38.0 1.0 copy-done.1
  39.0 2.5 %pack_rows.1 = (bf16[2,84,512]{2,1,0:T(8,128)(2,1)}, bf16[2,84,512]{2,1,0:T(8,128)(2,1)}, bf16[2,84,512]{2,1,0:T(8,128)(2,1)}, bf16[2,84,512]{2,1,0:T(8,128)(2,1)}) custom-call(s32[4]{0:T(128)} %pad_add_fusion.idx, bf16[12,84,512]{2,1,0:T(8,128)(2,1)} %bitcast.62, bf16[12,84,512]{2,1,0:T(8,128)(2,1)} %copy-done.1), custom_call_target="tpu_custom_call" | custom-call | tf_op jit(solution)/shard_map/pack_rows/pallas_call | solution.py:148
  41.5 5.3 %collective-permute-start.2 = (bf16[2,84,512]{2,1,0:T(8,128)(2,1)}, bf16[2,84,512]{2,1,0:T(8,128)(2,1)S(1)}, u32[]{:S(2)}, u32[]{:S(2)}) collective-permute-start(bf16[2,84,512]{2,1,0:T(8,128)(2,1)} %get-tuple-element.9), channel_id=1, source_target_pairs={{0,4},{1,21},{2,6},{3,23},{4,8},{5,1},{6,10},{7,3},{8,12},{9,5},{1... | collective-permute-start | bytes 516104 | tf_op jit(solution)/shard_map/ppermute | solution.py:131
  46.8 2.2 %collective-permute-start.3 = (bf16[2,84,512]{2,1,0:T(8,128)(2,1)}, bf16[2,84,512]{2,1,0:T(8,128)(2,1)S(1)}, u32[]{:S(2)}, u32[]{:S(2)}) collective-permute-start(bf16[2,84,512]{2,1,0:T(8,128)(2,1)} %get-tuple-element.10), channel_id=1, source_target_pairs={{0,2},{1,23},{2,4},{3,1},{4,6},{5,3},{6,8},{7,5},{8,10},{9,7},{10,... | collective-permute-start | bytes 516104 | tf_op jit(solution)/shard_map/ppermute | solution.py:131
  49.0 2.8 %collective-permute-start.8 = (bf16[2,84,512]{2,1,0:T(8,128)(2,1)}, bf16[2,84,512]{2,1,0:T(8,128)(2,1)S(1)}, u32[]{:S(2)}, u32[]{:S(2)}) collective-permute-start(bf16[2,84,512]{2,1,0:T(8,128)(2,1)} %get-tuple-element.11), channel_id=1, source_target_pairs={{0,20},{1,5},{2,22},{3,7},{4,0},{5,9},{6,2},{7,11},{8,4},{9,13},{1... | collective-permute-start | bytes 516104 | tf_op jit(solution)/shard_map/ppermute | solution.py:131
  51.8 7.0 %own_sums.1 = f32[7,776,128]{2,1,0:T(8,128)} custom-call(s32[7]{0:T(128)} %stack.46.idx, bf16[12,84,512]{2,1,0:T(8,128)(2,1)} %bitcast.63, bf16[12,84,512]{2,1,0:T(8,128)(2,1)} %copy-done.1), custom_call_target="tpu_custom_call" | custom-call | tf_op jit(solution)/shard_map/own_sums/pallas_call | solution.py:162
  58.8 0.6 copy-done.9
  59.4 2.5 %collective-permute-start.9 = (bf16[2,84,512]{2,1,0:T(8,128)(2,1)}, bf16[2,84,512]{2,1,0:T(8,128)(2,1)S(1)}, u32[]{:S(2)}, u32[]{:S(2)}) collective-permute-start(bf16[2,84,512]{2,1,0:T(8,128)(2,1)} %get-tuple-element.12), channel_id=1, source_target_pairs={{0,22},{1,3},{2,0},{3,5},{4,2},{5,7},{6,4},{7,9},{8,6},{9,11},{10,... | collective-permute-start | bytes 516104 | tf_op jit(solution)/shard_map/ppermute | solution.py:131
  61.9 2.3 %slice_bitcast_fusion = (f32[776,128]{1,0:T(8,128)}, f32[776,128]{1,0:T(8,128)}, f32[776,128]{1,0:T(8,128)}) fusion(f32[7,776,128]{2,1,0:T(8,128)} %own_sums.1), kind=kLoop, calls=%fused_computation.2 | loop fusion | bytes 2383872 | tf_op jit(solution)/shard_map/squeeze | solution.py:208
  64.2 0.0 collective-permute-done.8.rest_0_
  64.2 3.2 %collective-permute-done.9.rest_1_ = bf16[2,84,512]{2,1,0:T(8,128)(2,1)S(1)} collective-permute-done((bf16[2,84,512]{2,1,0:T(8,128)(2,1)}, bf16[2,84,512]{2,1,0:T(8,128)(2,1)S(1)}, u32[]{:S(2)}, u32[]{:S(2)}) %collective-permute-start.9) | collective-permute-done | bytes 172064 | tf_op jit(solution)/shard_map/ppermute | solution.py:131
  67.4 0.7 copy-done.7
  68.1 2.5 %far_sum.3 = f32[776,128]{1,0:T(8,128)} custom-call(f32[776,128]{1,0:T(8,128)} %get-tuple-element.14.base, bf16[1,84,512]{2,1,0:T(8,128)(2,1)} %copy-done.9, bf16[2,84,512]{2,1,0:T(8,128)(2,1)} %copy-done.6, bf16[2,84,512]{2,1,0:T(8,128)(2,1)} %copy-done.7), custom_call_target="tpu_custom_call" | custom-call | tf_op jit(solution)/shard_map/far_sum/pallas_call | solution.py:180
  70.5 1.9 %collective-permute-start.10 = (f32[776,128]{1,0:T(8,128)}, f32[776,128]{1,0:T(8,128)S(1)}, u32[]{:S(2)}, u32[]{:S(2)}) collective-permute-start(f32[776,128]{1,0:T(8,128)} %far_sum.3), channel_id=1, source_target_pairs={{0,22},{1,3},{2,0},{3,5},{4,2},{5,7},{6,4},{7,9},{8,6},{9,11},{10,... | collective-permute-start | bytes 1191944 | tf_op jit(solution)/shard_map/ppermute | solution.py:131
  72.5 0.0 copy-start.4
  72.5 0.0 collective-permute-done.3.rest_1_
  72.5 0.6 copy-done.4
  73.1 0.1 copy-done.5
  73.2 2.5 %far_sum.2 = f32[776,128]{1,0:T(8,128)} custom-call(f32[776,128]{1,0:T(8,128)} %get-tuple-element.15.base, bf16[1,84,512]{2,1,0:T(8,128)(2,1)} %collective-permute-done.1.half, bf16[2,84,512]{2,1,0:T(8,128)(2,1)} %copy-done.4, bf16[2,84,512]{2,1,0:T(8,128)(2,1)} %copy-done.5), custom_call_target="tpu_custom_call" | custom-call | tf_op jit(solution)/shard_map/far_sum/pallas_call | solution.py:180
  75.7 4.7 %collective-permute-start.4 = (f32[776,128]{1,0:T(8,128)}, f32[776,128]{1,0:T(8,128)S(1)}, u32[]{:S(2)}, u32[]{:S(2)}) collective-permute-start(f32[776,128]{1,0:T(8,128)} %far_sum.2), channel_id=1, source_target_pairs={{0,2},{1,23},{2,4},{3,1},{4,6},{5,3},{6,8},{7,5},{8,10},{9,7},{10,... | collective-permute-start | bytes 1191944 | tf_op jit(solution)/shard_map/ppermute | solution.py:131
  80.4 0.1 collective-permute-done.10
  80.5 5.0 %collective-permute-done.4 = f32[776,128]{1,0:T(8,128)S(1)} collective-permute-done((f32[776,128]{1,0:T(8,128)}, f32[776,128]{1,0:T(8,128)S(1)}, u32[]{:S(2)}, u32[]{:S(2)}) %collective-permute-start.4) | collective-permute-done | bytes 397344 | tf_op jit(solution)/shard_map/ppermute | solution.py:131
  85.5 0.1 fusion.1
  85.6 1.9 %collective-permute-start.11 = (f32[776,128]{1,0:T(8,128)S(1)}, f32[776,128]{1,0:T(8,128)S(1)}, u32[]{:S(2)}, u32[]{:S(2)}) collective-permute-start(f32[776,128]{1,0:T(8,128)S(1)} %get-tuple-element.18), channel_id=1, source_target_pairs={{0,22},{1,3},{2,0},{3,5},{4,2},{5,7},{6,4},{7,9},{8,6},{9,11},{10,... | collective-permute-start | bytes 1191944 | tf_op jit(solution)/shard_map/ppermute | solution.py:131
  87.5 4.9 %collective-permute-start.5 = (f32[776,128]{1,0:T(8,128)S(1)}, f32[776,128]{1,0:T(8,128)S(1)}, u32[]{:S(2)}, u32[]{:S(2)}) collective-permute-start(f32[776,128]{1,0:T(8,128)S(1)} %get-tuple-element.19), channel_id=1, source_target_pairs={{0,2},{1,23},{2,4},{3,1},{4,6},{5,3},{6,8},{7,5},{8,10},{9,7},{10,... | collective-permute-start | bytes 1191944 | tf_op jit(solution)/shard_map/ppermute | solution.py:131
  92.4 3.3 %collective-permute-done.11 = f32[776,128]{1,0:T(8,128)S(1)} collective-permute-done((f32[776,128]{1,0:T(8,128)S(1)}, f32[776,128]{1,0:T(8,128)S(1)}, u32[]{:S(2)}, u32[]{:S(2)}) %collective-permute-start.11) | collective-permute-done | bytes 397344 | tf_op jit(solution)/shard_map/ppermute | solution.py:131
  95.7 5.6 %collective-permute-done.5 = f32[776,128]{1,0:T(8,128)S(1)} collective-permute-done((f32[776,128]{1,0:T(8,128)S(1)}, f32[776,128]{1,0:T(8,128)S(1)}, u32[]{:S(2)}, u32[]{:S(2)}) %collective-permute-start.5) | collective-permute-done | bytes 397344 | tf_op jit(solution)/shard_map/ppermute | solution.py:131
  101.3 0.1 fusion
  101.4 1.9 %collective-permute-start.12 = (f32[776,128]{1,0:T(8,128)S(1)}, f32[776,128]{1,0:T(8,128)S(1)}, u32[]{:S(2)}, u32[]{:S(2)}) collective-permute-start(f32[776,128]{1,0:T(8,128)S(1)} %get-tuple-element.16), channel_id=1, source_target_pairs={{0,22},{1,3},{2,0},{3,5},{4,2},{5,7},{6,4},{7,9},{8,6},{9,11},{10,... | collective-permute-start | bytes 1191944 | tf_op jit(solution)/shard_map/ppermute | solution.py:131
  103.3 5.3 %collective-permute-start.6 = (f32[776,128]{1,0:T(8,128)S(1)}, f32[776,128]{1,0:T(8,128)S(1)}, u32[]{:S(2)}, u32[]{:S(2)}) collective-permute-start(f32[776,128]{1,0:T(8,128)S(1)} %get-tuple-element.17), channel_id=1, source_target_pairs={{0,2},{1,23},{2,4},{3,1},{4,6},{5,3},{6,8},{7,5},{8,10},{9,7},{10,... | collective-permute-start | bytes 1191944 | tf_op jit(solution)/shard_map/ppermute | solution.py:131
  108.7 18.9 %all_to_all.15 = bf16[1,32,256,8]{2,3,0,1:T(8,128)(2,1)} all-to-all(bf16[1,32,256,8]{2,3,0,1:T(8,128)(2,1)S(1)} %bitcast.65), channel_id=1, replica_groups=mesh['pair'=32,'aux'=24] {'pair'}, dimensions={1} | all-to-all | bytes 262144 | tf_op jit(solution)/shard_map/all_to_all | solution.py:174
  127.6 0.0 collective-permute-done.12.pb
  127.6 0.0 collective-permute-done.6.pa
  127.6 0.8 copy-done.2
  128.4 0.1 copy-done.3
  128.5 2.5 %residual.1 = f32[256,256]{1,0:T(8,128)} custom-call(s32[2]{0:T(128)} %bitcast.68, s32[2]{0:T(128)} %bitcast.69, s32[2]{0:T(128)} %bitcast.70, f32[100]{0:T(128)} %occ.1, f32[12,128]{1,0:T(8,128)} %bitcast.67, f32[776,128]{1,0:T(8,128)} %copy-done.3, f32[776,128]{1,0:T(8,128)} %copy-done.2, f32[776,128]{1,0:T(8,128)} %get-tuple-element.13.pc, ...), custom_call_target="tpu_custom_call" | custom-call | tf_op jit(solution)/shard_map/residual/pallas_call | solution.py:194
  (16 shorter events, 0.0 us)
Async XLA Ops:
  11.4 26.6 %collective-permute-start = (bf16[12,84,512]{2,1,0:T(8,128)(2,1)}, bf16[12,84,512]{2,1,0:T(8,128)(2,1)S(1)}, u32[]{:S(2)}, u32[]{:S(2)}) collective-permute-start(bf16[12,84,512]{2,1,0:T(8,128)(2,1)} %bitcast.58), channel_id=1, source_target_pairs={{0,1},{1,0},{2,3},{3,2},{4,5},{5,4},{6,7},{7,6},{8,9},{9,8},{10,11... | collective-permute-start | bytes 3096584 | tf_op jit(solution)/shard_map/ppermute | solution.py:144
  24.9 47.6 %collective-permute-start.1 = (bf16[1,84,512]{2,1,0:T(8,128)(2,1)}, bf16[1,84,512]{2,1,0:T(8,128)(2,1)}, u32[]{:S(2)}, u32[]{:S(2)}) collective-permute-start(bf16[1,84,512]{2,1,0:T(8,128)(2,1)} %bitcast.61), channel_id=1, source_target_pairs={{0,6},{1,19},{2,8},{3,21},{4,10},{5,23},{6,12},{7,1},{8,14},{9,3},... | collective-permute-start | bytes 258056 | tf_op jit(solution)/shard_map/ppermute | solution.py:131
  30.2 28.6 %collective-permute-start.7 = (bf16[1,84,512]{2,1,0:T(8,128)(2,1)S(1)}, bf16[1,84,512]{2,1,0:T(8,128)(2,1)S(1)}, u32[]{:S(2)}, u32[]{:S(2)}) collective-permute-start(bf16[1,84,512]{2,1,0:T(8,128)(2,1)S(1)} %bitcast.66), channel_id=1, source_target_pairs={{0,7},{1,18},{2,9},{3,20},{4,11},{5,22},{6,13},{7,0},{8,15},{9,2},... | collective-permute-start | bytes 258056 | tf_op jit(solution)/shard_map/ppermute | solution.py:131
  38.0 1.0 copy-start.1
  41.5 31.0 %collective-permute-start.2 = (bf16[2,84,512]{2,1,0:T(8,128)(2,1)}, bf16[2,84,512]{2,1,0:T(8,128)(2,1)S(1)}, u32[]{:S(2)}, u32[]{:S(2)}) collective-permute-start(bf16[2,84,512]{2,1,0:T(8,128)(2,1)} %get-tuple-element.9), channel_id=1, source_target_pairs={{0,4},{1,21},{2,6},{3,23},{4,8},{5,1},{6,10},{7,3},{8,12},{9,5},{1... | collective-permute-start | bytes 516104 | tf_op jit(solution)/shard_map/ppermute | solution.py:131
  46.8 25.7 %collective-permute-start.3 = (bf16[2,84,512]{2,1,0:T(8,128)(2,1)}, bf16[2,84,512]{2,1,0:T(8,128)(2,1)S(1)}, u32[]{:S(2)}, u32[]{:S(2)}) collective-permute-start(bf16[2,84,512]{2,1,0:T(8,128)(2,1)} %get-tuple-element.10), channel_id=1, source_target_pairs={{0,2},{1,23},{2,4},{3,1},{4,6},{5,3},{6,8},{7,5},{8,10},{9,7},{10,... | collective-permute-start | bytes 516104 | tf_op jit(solution)/shard_map/ppermute | solution.py:131
  49.0 15.3 %collective-permute-start.8 = (bf16[2,84,512]{2,1,0:T(8,128)(2,1)}, bf16[2,84,512]{2,1,0:T(8,128)(2,1)S(1)}, u32[]{:S(2)}, u32[]{:S(2)}) collective-permute-start(bf16[2,84,512]{2,1,0:T(8,128)(2,1)} %get-tuple-element.11), channel_id=1, source_target_pairs={{0,20},{1,5},{2,22},{3,7},{4,0},{5,9},{6,2},{7,11},{8,4},{9,13},{1... | collective-permute-start | bytes 516104 | tf_op jit(solution)/shard_map/ppermute | solution.py:131
  58.8 0.6 copy-start.9
  59.4 26.0 %copy-start = (f32[7,776,128]{2,1,0:T(8,128)S(1)}, f32[7,776,128]{2,1,0:T(8,128)}, u32[]{:S(2)}) copy-start(f32[7,776,128]{2,1,0:T(8,128)} %own_sums.1) | copy-start | bytes 8343556
  59.4 7.9 %collective-permute-start.9 = (bf16[2,84,512]{2,1,0:T(8,128)(2,1)}, bf16[2,84,512]{2,1,0:T(8,128)(2,1)S(1)}, u32[]{:S(2)}, u32[]{:S(2)}) collective-permute-start(bf16[2,84,512]{2,1,0:T(8,128)(2,1)} %get-tuple-element.12), channel_id=1, source_target_pairs={{0,22},{1,3},{2,0},{3,5},{4,2},{5,7},{6,4},{7,9},{8,6},{9,11},{10,... | collective-permute-start | bytes 516104 | tf_op jit(solution)/shard_map/ppermute | solution.py:131
  64.2 3.2 %copy-start.6 = (bf16[2,84,512]{2,1,0:T(8,128)(2,1)}, bf16[2,84,512]{2,1,0:T(8,128)(2,1)S(1)}, u32[]{:S(2)}) copy-start(bf16[2,84,512]{2,1,0:T(8,128)(2,1)S(1)} %collective-permute-done.8.rest_0_) | copy-start | bytes 516100
  67.4 0.7 copy-start.7
  70.5 10.0 %collective-permute-start.10 = (f32[776,128]{1,0:T(8,128)}, f32[776,128]{1,0:T(8,128)S(1)}, u32[]{:S(2)}, u32[]{:S(2)}) collective-permute-start(f32[776,128]{1,0:T(8,128)} %far_sum.3), channel_id=1, source_target_pairs={{0,22},{1,3},{2,0},{3,5},{4,2},{5,7},{6,4},{7,9},{8,6},{9,11},{10,... | collective-permute-start | bytes 1191944 | tf_op jit(solution)/shard_map/ppermute | solution.py:131
  72.5 0.7 copy-start.4
  72.5 0.7 copy-start.5
  75.7 33.0 %copy-start.8 = (bf16[1,32,256,8]{2,3,1,0:T(8,128)(2,1)S(1)}, bf16[1,32,256,8]{2,3,1,0:T(8,128)(2,1)}, u32[]{:S(2)}) copy-start(bf16[1,32,256,8]{2,3,1,0:T(8,128)(2,1)} %param.7) | copy-start | bytes 393220
  75.7 9.8 %collective-permute-start.4 = (f32[776,128]{1,0:T(8,128)}, f32[776,128]{1,0:T(8,128)S(1)}, u32[]{:S(2)}, u32[]{:S(2)}) collective-permute-start(f32[776,128]{1,0:T(8,128)} %far_sum.2), channel_id=1, source_target_pairs={{0,2},{1,23},{2,4},{3,1},{4,6},{5,3},{6,8},{7,5},{8,10},{9,7},{10,... | collective-permute-start | bytes 1191944 | tf_op jit(solution)/shard_map/ppermute | solution.py:131
  85.6 10.1 %collective-permute-start.11 = (f32[776,128]{1,0:T(8,128)S(1)}, f32[776,128]{1,0:T(8,128)S(1)}, u32[]{:S(2)}, u32[]{:S(2)}) collective-permute-start(f32[776,128]{1,0:T(8,128)S(1)} %get-tuple-element.18), channel_id=1, source_target_pairs={{0,22},{1,3},{2,0},{3,5},{4,2},{5,7},{6,4},{7,9},{8,6},{9,11},{10,... | collective-permute-start | bytes 1191944 | tf_op jit(solution)/shard_map/ppermute | solution.py:131
  87.5 13.8 %collective-permute-start.5 = (f32[776,128]{1,0:T(8,128)S(1)}, f32[776,128]{1,0:T(8,128)S(1)}, u32[]{:S(2)}, u32[]{:S(2)}) collective-permute-start(f32[776,128]{1,0:T(8,128)S(1)} %get-tuple-element.19), channel_id=1, source_target_pairs={{0,2},{1,23},{2,4},{3,1},{4,6},{5,3},{6,8},{7,5},{8,10},{9,7},{10,... | collective-permute-start | bytes 1191944 | tf_op jit(solution)/shard_map/ppermute | solution.py:131
  101.4 26.2 %collective-permute-start.12 = (f32[776,128]{1,0:T(8,128)S(1)}, f32[776,128]{1,0:T(8,128)S(1)}, u32[]{:S(2)}, u32[]{:S(2)}) collective-permute-start(f32[776,128]{1,0:T(8,128)S(1)} %get-tuple-element.16), channel_id=1, source_target_pairs={{0,22},{1,3},{2,0},{3,5},{4,2},{5,7},{6,4},{7,9},{8,6},{9,11},{10,... | collective-permute-start | bytes 1191944 | tf_op jit(solution)/shard_map/ppermute | solution.py:131
  103.3 24.3 %collective-permute-start.6 = (f32[776,128]{1,0:T(8,128)S(1)}, f32[776,128]{1,0:T(8,128)S(1)}, u32[]{:S(2)}, u32[]{:S(2)}) collective-permute-start(f32[776,128]{1,0:T(8,128)S(1)} %get-tuple-element.17), channel_id=1, source_target_pairs={{0,2},{1,23},{2,4},{3,1},{4,6},{5,3},{6,8},{7,5},{8,10},{9,7},{10,... | collective-permute-start | bytes 1191944 | tf_op jit(solution)/shard_map/ppermute | solution.py:131
  127.6 0.8 copy-start.2
  127.6 0.9 copy-start.3

commit v2 on v0

v2 whole, which is shorter than its diff:
```python
import functools

import jax
import jax.numpy as jnp
from jax import lax
from jax.experimental import pallas as pl
from jax.experimental.pallas import tpu as pltpu
from jax.sharding import PartitionSpec as P

TILE = 128
HOPS = 3
H_ROWS, G_ROWS = 4 * TILE, 2 * TILE
DIAG = H_ROWS + G_ROWS
H_EXP, G_EXP = DIAG + 1, DIAG + 2
ROWS = DIAG + 16
F32 = jnp.float32
BF16 = jnp.bfloat16
F16 = jnp.float16


def sign(core, stream):
    return 1 - 2 * ((core + stream) % 2)


def here():
    me = lax.axis_index("aux")
    return lax.div(me, 2), lax.rem(me, 2)


def dest(chips, stream, distance):
    z, c = here()
    return lax.rem(z + sign(c, stream) * distance + chips, chips)


def iotas():
    return (
        lax.broadcasted_iota(jnp.int32, (TILE, TILE), 0),
        lax.broadcasted_iota(jnp.int32, (TILE, TILE), 1),
    )


def exponent(*parts):
    top = None
    for part in parts:
        high = jnp.max(jnp.abs(part), axis=0, keepdims=True)
        top = high if top is None else jnp.maximum(top, high)
    top = jnp.max(top, axis=1, keepdims=True)
    power = 14.0 - jnp.floor(jnp.log2(jnp.maximum(top, 1e-30)))
    return jnp.broadcast_to(power, (1, TILE))


def packed_sum(blocks, out):
    total = None
    for block in blocks:
        term = lax.dot_general(
            block[:, : 2 * TILE], block, (((0,), (0,)), ((), ())), preferred_element_type=F32
        )
        total = term if total is None else total + term
    row, col = iotas()
    g00, g01 = total[:TILE, :TILE], total[:TILE, TILE : 2 * TILE]
    g11 = total[TILE:, TILE : 2 * TILE]
    h0, h1 = total[:, 2 * TILE : 3 * TILE], total[:, 3 * TILE :]
    fold = jnp.where(row <= col, g00, g11)
    diag = jnp.sum(jnp.where(row == col, g11, 0.0), axis=0, keepdims=True)
    out[: 2 * TILE] = h0
    out[2 * TILE : H_ROWS] = h1
    out[H_ROWS : H_ROWS + TILE] = g01
    out[H_ROWS + TILE : DIAG] = fold
    lines = lax.broadcasted_iota(jnp.int32, (ROWS - DIAG, TILE), 0)
    rest = jnp.where(lines == 0, diag, 0.0)
    rest = jnp.where(lines == H_EXP - DIAG, exponent(h0, h1), rest)
    out[DIAG:] = jnp.where(lines == G_EXP - DIAG, exponent(g01, fold, diag), rest)


def scales(e_h, e_g):
    row = lax.broadcasted_iota(jnp.int32, (ROWS, TILE), 0)
    return row, jnp.where(row < H_ROWS, jnp.exp2(e_h), jnp.exp2(e_g))


def encode(x, e_h, e_g):
    row, scale = scales(e_h, e_g)
    tail = jnp.where(row == H_EXP, e_h, e_g)
    return jnp.where(row <= DIAG, x * scale, tail).astype(F16)


def decode(x):
    x = x.astype(F32)
    e_h, e_g = x[H_EXP : H_EXP + 1], x[G_EXP : G_EXP + 1]
    return x * scales(-e_h, -e_g)[1], e_h, e_g


def split_kernel(chips, ints, out):
    c = here()[1]
    for chip in range(chips):
        out[chip] = ints[2 * chip + 1 - c]


def pack_kernel(chips, ways, ints, other, *outs):
    c = here()[1]
    for (s, d), out in zip(ways, outs):
        to = dest(chips, s, d)
        out[0] = ints[2 * to + c]
        out[1] = other[to]


def own_kernel(chips, near, ints, other, *outs):
    c = here()[1]
    for (s, d), out in zip(near, outs):
        to = dest(chips, s, d)
        packed_sum([ints[2 * to + c], other[to]], out)


def far_kernel(chips, stream, ints, other, *rest):
    c = here()[1]
    to = dest(chips, stream, HOPS)
    blocks = [ints[2 * to + c], other[to]]
    for ref in rest[:-1]:
        blocks += [ref[0], ref[1]]
    packed_sum(blocks, rest[-1])


def final_kernel(occ_at, tiles, mask, occ, virt, sums, amps_t, out):
    row, col = iotas()
    h = jnp.concatenate([sums[: 2 * TILE], sums[2 * TILE : H_ROWS]], axis=1)
    g01 = sums[H_ROWS : H_ROWS + TILE]
    fold = sums[H_ROWS + TILE : DIAG]
    diag = sums[DIAG : DIAG + 8][:1]
    above = jnp.where(row < col, fold, 0.0)
    below = jnp.where(row > col, fold, 0.0)
    g00 = jnp.where(row <= col, fold, 0.0) + above.T
    g11 = below + below.T + jnp.where(row == col, diag, 0.0)
    g = jnp.concatenate(
        [jnp.concatenate([g00, g01], axis=1), jnp.concatenate([g01.T, g11], axis=1)], axis=0
    )
    tt = amps_t[...]
    total = h
    rest = g
    for _ in range(3):
        piece = rest.astype(BF16)
        rest = rest - piece.astype(F32)
        total = total - lax.dot_general(
            piece, tt, (((1,), (1,)), ((), ())), preferred_element_type=F32
        )
        total = total - lax.dot_general(
            tt, piece, (((0,), (0,)), ((), ())), preferred_element_type=F32
        )
    f_sum = occ[occ_at[0]] + occ[occ_at[1]]
    t = tt.astype(F32).T
    e_row = [virt[pl.ds(tiles[s], 1), :] for s in range(2)]
    e_col = [jnp.sum(jnp.where(row == col, e, 0.0), axis=1, keepdims=True) for e in e_row]
    keep = [mask[s].astype(F32) for s in range(2)]
    for a in range(2):
        for b in range(2):
            at = (slice(a * TILE, (a + 1) * TILE), slice(b * TILE, (b + 1) * TILE))
            delta = (e_col[a] + e_row[b]) - f_sum
            out[at] = (keep[a] * keep[b]) * (total[at] + delta * t[at])


def on_device(chips, amplitudes, integrals, pair_occ, dom_tiles, dom_mask, virt_energy, occ_energy):
    naux, wide = integrals.shape[2:]
    far = chips // 2
    vmem = pl.BlockSpec(memory_space=pltpu.VMEM)
    smem = pl.BlockSpec(memory_space=pltpu.SMEM)

    def call(kernel, n_in, shapes, name, small=0):
        return pl.pallas_call(
            kernel,
            in_specs=[smem] * small + [vmem] * n_in,
            out_specs=[vmem] * len(shapes),
            out_shape=[jax.ShapeDtypeStruct(*s) for s in shapes],
            compiler_params=pltpu.CompilerParams(vmem_limit_bytes=24 << 20),
            name=name,
        )

    def permute(x, stream, hops):
        pairs = []
        for chip in range(chips):
            for core in range(2):
                to = (chip + sign(core, stream) * hops) % chips
                pairs.append((chip * 2 + core, to * 2 + core))
        return lax.ppermute(x, "aux", pairs)

    owned = lax.all_to_all(amplitudes, "pair", split_axis=1, concat_axis=3, tiled=True)

    ints = integrals[:, 0]
    (other,) = call(
        functools.partial(split_kernel, chips), 1, [((chips, naux, wide), BF16)], "split_cores"
    )(ints)
    other = lax.ppermute(other, "aux", [(i, i ^ 1) for i in range(2 * chips)])

    ways = [(s, d) for d in range(far, HOPS, -1) for s in range(2) if d < far or s == 0]
    sends = call(
        functools.partial(pack_kernel, chips, ways),
        2,
        [((2, naux, wide), BF16)] * len(ways),
        "pack_rows",
    )(ints, other)
    rows = [[], []]
    for (s, d), x in zip(ways, sends):
        rows[s].append(permute(x, s, d - HOPS))

    near = [(s, d) for d in range(HOPS - 1, 0, -1) for s in range(2)] + [(0, 0)]
    local = call(
        functools.partial(own_kernel, chips, near),
        2,
        [((ROWS, TILE), F32)] * len(near),
        "own_sums",
    )(ints, other)

    rows[1][-1], owned = lax.optimization_barrier((rows[1][-1], owned))
    amps_t = jnp.swapaxes(owned[0, 0], 0, 1)

    moving = []
    for s in range(2):
        (x,) = call(
            functools.partial(far_kernel, chips, s), 2 + len(rows[s]), [((ROWS, TILE), F32)], "far_sum"
        )(ints, other, *rows[s])
        moving.append(
            permute(encode(x, x[H_EXP : H_EXP + 1], x[G_EXP : G_EXP + 1]), s, 1)
        )
    for hop in range(1, HOPS):
        for s in range(2):
            x, e_h, e_g = decode(moving[s])
            mine = local[2 * (hop - 1) + s]
            e_h = jnp.minimum(e_h, mine[H_EXP : H_EXP + 1]) - 1.0
            e_g = jnp.minimum(e_g, mine[G_EXP : G_EXP + 1]) - 1.0
            x = encode(x + mine, e_h, e_g)
            moving[s] = permute(x, s, 1)
            if s == 0:
                moving[1] = lax.optimization_barrier((moving[1], x))[0]
    sums = decode(moving[0])[0] + decode(moving[1])[0] + local[-1]

    (out,) = call(final_kernel, 3, [((2 * TILE, 2 * TILE), F32)], "residual", 4)(
        pair_occ.reshape(-1),
        dom_tiles.reshape(-1),
        dom_mask.reshape(-1),
        occ_energy,
        virt_energy.reshape(-1, TILE),
        sums,
        amps_t,
    )
    return out[None, None]


def solution(mesh):
    return jax.shard_map(
        functools.partial(on_device, mesh.shape["aux"] // 2),
        mesh=mesh,
        in_specs=(
            P("aux", None, None, "pair"),
            P(None, "pair", "aux", None),
            P("aux", "pair", None),
            P("aux", "pair", None),
            P("aux", "pair", None),
            P(),
            P(),
        ),
        out_specs=P("aux", "pair", None, None),
        check_vma=False,
    )
```

time: 120 us -> 106 us (0.88)
  the two profiles are of different devices: /device:TPU:1 before, /device:TPU:2 now
where the time goes in v2:
time: 106 us
  starting transfers between devices  59.8 us (56%)
  waiting for transfers between devices  25.4 us (24%)
  Pallas kernels  7.12 us (7%)
  other arithmetic  6.75 us (6%)
  local copies, waits for them, and re-layouts  6.13 us (6%)
    ppermute x11, starting transfers between devices, permute(): return lax.ppermute(x, 'aux', pairs)  44.8 us
    ppermute x11, waiting for transfers between devices, permute(): return lax.ppermute(x, 'aux', pairs)  25.4 us
    all_to_all x1, starting transfers between devices, on_device(): lax.all_to_all(amplitudes, 'pair', split_axis=1, concat_axis=3, tiled=True)  13.1 us
    unnamed x43, local copies, waits for them, and re-layouts  6.13 us
    convert_element_type x5, other arithmetic, encode(): return jnp.where(row <= DIAG, x * scale, tail).astype(F16)  5.27 us
    pallas_call x2, Pallas kernels, on_device(): call(functools.partial(far_kernel, chips, s), 2 + len(rows[s]), [((ROWS,...  2.42 us
  transfers between devices with their start and end apart: 13, of which 7 were waited for; matrix products, arithmetic and copies ran while one was open for 2% of the time, Pallas kernels for 4%

profile of v2, /device:TPU:2, one launch (start us, length us, event | category | flops | bytes accessed | tf_op | source)
XLA Modules:
  0.0 105.8 jit_solution(16742722603402785121)
XLA Ops:
  0.0 2.3 %copy.12 = bf16[24,1,84,512]{3,2,0,1:T(8,128)(2,1)S(1)} copy(bf16[24,1,84,512]{3,0,2,1:T(8,128)(2,1)} %param.8) | data formatting | bytes 4128768 | tf_op args[1]
  2.3 1.1 %split_cores.1 = bf16[12,84,512]{2,1,0:T(8,128)(2,1)} custom-call(bf16[24,84,512]{2,1,0:T(8,128)(2,1)S(1)} %bitcast.81), custom_call_target="tpu_custom_call" | custom-call | tf_op jit(solution)/shard_map/split_cores/pallas_call | solution.py:186
  3.4 1.9 %collective-permute-start = (bf16[12,84,512]{2,1,0:T(8,128)(2,1)}, bf16[12,84,512]{2,1,0:T(8,128)(2,1)S(1)}, u32[]{:S(2)}, u32[]{:S(2)}) collective-permute-start(bf16[12,84,512]{2,1,0:T(8,128)(2,1)} %split_cores.1), channel_id=1, source_target_pairs={{0,1},{1,0},{2,3},{3,2},{4,5},{5,4},{6,7},{7,6},{8,9},{9,8},{10,11... | collective-permute-start | bytes 3096584 | tf_op jit(solution)/shard_map/ppermute | solution.py:189
  5.3 13.1 %all-to-all-start = ((bf16[1,32,256,8]{2,3,0,1:T(8,128)(2,1)}), bf16[1,32,256,8]{2,3,0,1:T(8,128)(2,1)S(1)}, u32[]{:S(2)}, u32[]{:S(2)}) async-start(bf16[1,32,256,8]{2,3,0,1:T(8,128)(2,1)} %bitcast.23), calls=%async_computation | async-start | bytes 262144 | tf_op jit(solution)/shard_map/all_to_all | solution.py:183
  18.4 0.0 collective-permute-done.other
  18.4 0.8 pack_rows.1
  19.2 5.1 %collective-permute-start.1 = (bf16[2,84,512]{2,1,0:T(8,128)(2,1)S(1)}, bf16[2,84,512]{2,1,0:T(8,128)(2,1)S(1)}, u32[]{:S(2)}, u32[]{:S(2)}) collective-permute-start(bf16[2,84,512]{2,1,0:T(8,128)(2,1)S(1)} %get-tuple-element.19), channel_id=1, source_target_pairs={{0,6},{1,19},{2,8},{3,21},{4,10},{5,23},{6,12},{7,1},{8,14},{9,3},... | collective-permute-start | bytes 516104 | tf_op jit(solution)/shard_map/ppermute | solution.py:181
  24.3 7.3 %collective-permute-start.2 = (bf16[2,84,512]{2,1,0:T(8,128)(2,1)S(1)}, bf16[2,84,512]{2,1,0:T(8,128)(2,1)S(1)}, u32[]{:S(2)}, u32[]{:S(2)}) collective-permute-start(bf16[2,84,512]{2,1,0:T(8,128)(2,1)S(1)} %get-tuple-element.20), channel_id=1, source_target_pairs={{0,4},{1,21},{2,6},{3,23},{4,8},{5,1},{6,10},{7,3},{8,12},{9,5},{1... | collective-permute-start | bytes 516104 | tf_op jit(solution)/shard_map/ppermute | solution.py:181
  31.6 4.3 %collective-permute-start.3 = (bf16[2,84,512]{2,1,0:T(8,128)(2,1)S(1)}, bf16[2,84,512]{2,1,0:T(8,128)(2,1)S(1)}, u32[]{:S(2)}, u32[]{:S(2)}) collective-permute-start(bf16[2,84,512]{2,1,0:T(8,128)(2,1)S(1)} %get-tuple-element.21), channel_id=1, source_target_pairs={{0,2},{1,23},{2,4},{3,1},{4,6},{5,3},{6,8},{7,5},{8,10},{9,7},{10,... | collective-permute-start | bytes 516104 | tf_op jit(solution)/shard_map/ppermute | solution.py:181
  35.9 0.0 collective-permute-done.1.rest_0_
  36.0 6.3 %collective-permute-done.2.rest_1_ = bf16[2,84,512]{2,1,0:T(8,128)(2,1)S(1)} collective-permute-done((bf16[2,84,512]{2,1,0:T(8,128)(2,1)S(1)}, bf16[2,84,512]{2,1,0:T(8,128)(2,1)S(1)}, u32[]{:S(2)}, u32[]{:S(2)}) %collective-permute-start.2) | collective-permute-done | bytes 172064 | tf_op jit(solution)/shard_map/ppermute | solution.py:181
  42.3 1.8 %collective-permute-done.3.rest_2_ = bf16[2,84,512]{2,1,0:T(8,128)(2,1)S(1)} collective-permute-done((bf16[2,84,512]{2,1,0:T(8,128)(2,1)S(1)}, bf16[2,84,512]{2,1,0:T(8,128)(2,1)S(1)}, u32[]{:S(2)}, u32[]{:S(2)}) %collective-permute-start.3) | collective-permute-done | bytes 172064 | tf_op jit(solution)/shard_map/ppermute | solution.py:181
  44.1 0.8 far_sum.2
  45.0 1.4 %select_convert_fusion.5 = f16[784,128]{1,0:T(8,128)(2,1)} fusion(f32[784,128]{1,0:T(8,128)S(1)} %far_sum.2, f32[128]{0:T(128)S(1)} %get-tuple-element.71, f32[128]{0:T(128)S(1)} %get-tuple-element.70, f32[128]{0:T(128)S(1)} %get-tuple-element.72, f32[128]{0:T(128)S(1)} %get-tuple-element.69, pred[784]{0:T(1024)(128)(4,1)S(1)} %get-tuple-element.79, ...), kind=kLoop, calls=%fused_computation.7 | loop fusion | flops 501760 | bytes 606512 | tf_op jit(solution)/shard_map/convert_element_type | solution.py:83
  46.3 2.4 %collective-permute-start.4 = (f16[784,128]{1,0:T(8,128)(2,1)}, f16[784,128]{1,0:T(8,128)(2,1)}, u32[]{:S(2)}, u32[]{:S(2)}) collective-permute-start(f16[784,128]{1,0:T(8,128)(2,1)} %select_convert_fusion.5), channel_id=1, source_target_pairs={{0,2},{1,23},{2,4},{3,1},{4,6},{5,3},{6,8},{7,5},{8,10},{9,7},{10,... | collective-permute-start | bytes 602120 | tf_op jit(solution)/shard_map/ppermute | solution.py:181
  48.8 4.6 %collective-permute-start.8 = (bf16[2,84,512]{2,1,0:T(8,128)(2,1)}, bf16[2,84,512]{2,1,0:T(8,128)(2,1)S(1)}, u32[]{:S(2)}, u32[]{:S(2)}) collective-permute-start(bf16[2,84,512]{2,1,0:T(8,128)(2,1)} %get-tuple-element.25), channel_id=1, source_target_pairs={{0,22},{1,3},{2,0},{3,5},{4,2},{5,7},{6,4},{7,9},{8,6},{9,11},{10,... | collective-permute-start | bytes 516104 | tf_op jit(solution)/shard_map/ppermute | solution.py:181
  53.4 3.1 %collective-permute-start.7 = (bf16[2,84,512]{2,1,0:T(8,128)(2,1)}, bf16[2,84,512]{2,1,0:T(8,128)(2,1)}, u32[]{:S(2)}, u32[]{:S(2)}) collective-permute-start(bf16[2,84,512]{2,1,0:T(8,128)(2,1)} %get-tuple-element.24), channel_id=1, source_target_pairs={{0,20},{1,5},{2,22},{3,7},{4,0},{5,9},{6,2},{7,11},{8,4},{9,13},{1... | collective-permute-start | bytes 516104 | tf_op jit(solution)/shard_map/ppermute | solution.py:181
  56.5 1.0 own_sums.1
  57.5 0.8 copy-done
  58.3 0.8 copy-done.2
  59.0 0.8 copy-done.4
  59.8 0.7 copy-done.6
  60.6 0.7 copy-done.8
  61.3 0.0 all-to-all-done
  61.4 1.8 %collective-permute-done.7.rest_0_ = bf16[2,84,512]{2,1,0:T(8,128)(2,1)} collective-permute-done((bf16[2,84,512]{2,1,0:T(8,128)(2,1)}, bf16[2,84,512]{2,1,0:T(8,128)(2,1)}, u32[]{:S(2)}, u32[]{:S(2)}) %collective-permute-start.7) | collective-permute-done | bytes 172064 | tf_op jit(solution)/shard_map/ppermute | solution.py:181
  63.2 1.6 %far_sum.3 = f32[784,128]{1,0:T(8,128)S(1)} custom-call(bf16[24,84,512]{2,1,0:T(8,128)(2,1)S(1)} %bitcast.85, bf16[12,84,512]{2,1,0:T(8,128)(2,1)S(1)} %collective-permute-done.other, bf16[2,84,512]{2,1,0:T(8,128)(2,1)} %collective-permute-done.7.rest_0_, bf16[2,84,512]{2,1,0:T(8,128)(2,1)S(1)} %collective-permute-done.8.rest_1_), custom_call_target="tpu_custom_call" | custom-call | tf_op jit(solution)/shard_map/far_sum/pallas_call | solution.py:215
  64.8 0.0 collective-permute-done.4
  64.8 1.0 convert_element_type.37
  65.9 1.6 %select_convert_fusion.4 = f16[784,128]{1,0:T(8,128)(2,1)S(1)} fusion(f32[784,128]{1,0:T(8,128)S(1)} %copy-done.7, f32[128]{0:T(128)S(1)} %bitcast.96, f32[128]{0:T(128)S(1)} %bitcast.95, f32[128]{0:T(128)S(1)} %get-tuple-element.55, f32[128]{0:T(128)S(1)} %get-tuple-element.45, f32[128]{0:T(128)S(1)} %get-tuple-element.68, f32[128]{0:T(128)S(1)} %get-tuple-element.67, ...), kind=kLoop, calls=%fused_computation.6 | loop fusion | flops 903168 | bytes 808240 | tf_op jit(solution)/shard_map/convert_element_type | solution.py:83
  67.5 1.9 %collective-permute-start.5 = (f16[784,128]{1,0:T(8,128)(2,1)S(1)}, f16[784,128]{1,0:T(8,128)(2,1)S(1)}, u32[]{:S(2)}, u32[]{:S(2)}) collective-permute-start(f16[784,128]{1,0:T(8,128)(2,1)S(1)} %select_convert_fusion.4), channel_id=1, source_target_pairs={{0,2},{1,23},{2,4},{3,1},{4,6},{5,3},{6,8},{7,5},{8,10},{9,7},{10,... | collective-permute-start | bytes 602120 | tf_op jit(solution)/shard_map/ppermute | solution.py:181
  69.4 6.9 %collective-permute-done.5 = f16[784,128]{1,0:T(8,128)(2,1)S(1)} collective-permute-done((f16[784,128]{1,0:T(8,128)(2,1)S(1)}, f16[784,128]{1,0:T(8,128)(2,1)S(1)}, u32[]{:S(2)}, u32[]{:S(2)}) %collective-permute-start.5) | collective-permute-done | bytes 200736 | tf_op jit(solution)/shard_map/ppermute | solution.py:181
  76.4 0.8 select_convert_fusion.3
  77.2 2.3 %collective-permute-start.9 = (f16[784,128]{1,0:T(8,128)(2,1)S(1)}, f16[784,128]{1,0:T(8,128)(2,1)S(1)}, u32[]{:S(2)}, u32[]{:S(2)}) collective-permute-start(f16[784,128]{1,0:T(8,128)(2,1)S(1)} %get-tuple-element.78), channel_id=1, source_target_pairs={{0,22},{1,3},{2,0},{3,5},{4,2},{5,7},{6,4},{7,9},{8,6},{9,11},{10,... | collective-permute-start | bytes 602120 | tf_op jit(solution)/shard_map/ppermute | solution.py:181
  79.5 3.7 %collective-permute-start.6 = (f16[784,128]{1,0:T(8,128)(2,1)S(1)}, f16[784,128]{1,0:T(8,128)(2,1)S(1)}, u32[]{:S(2)}, u32[]{:S(2)}) collective-permute-start(f16[784,128]{1,0:T(8,128)(2,1)S(1)} %get-tuple-element.77), channel_id=1, source_target_pairs={{0,2},{1,23},{2,4},{3,1},{4,6},{5,3},{6,8},{7,5},{8,10},{9,7},{10,... | collective-permute-start | bytes 602120 | tf_op jit(solution)/shard_map/ppermute | solution.py:181
  83.2 2.2 %collective-permute-done.9 = f16[784,128]{1,0:T(8,128)(2,1)S(1)} collective-permute-done((f16[784,128]{1,0:T(8,128)(2,1)S(1)}, f16[784,128]{1,0:T(8,128)(2,1)S(1)}, u32[]{:S(2)}, u32[]{:S(2)}) %collective-permute-start.9) | collective-permute-done | bytes 200736 | tf_op jit(solution)/shard_map/ppermute | solution.py:181
  85.4 0.7 select_convert_fusion.1
  86.2 0.0 copy-start.10
  86.2 0.0 copy-start.11
  86.2 0.0 copy-start.12
  86.2 0.0 copy-start.13
  86.2 0.0 copy-start.14
  86.3 4.6 %collective-permute-start.10 = (f16[784,128]{1,0:T(8,128)(2,1)S(1)}, f16[784,128]{1,0:T(8,128)(2,1)S(1)}, u32[]{:S(2)}, u32[]{:S(2)}) collective-permute-start(f16[784,128]{1,0:T(8,128)(2,1)S(1)} %select_convert_fusion.1), channel_id=1, source_target_pairs={{0,22},{1,3},{2,0},{3,5},{4,2},{5,7},{6,4},{7,9},{8,6},{9,11},{10,... | collective-permute-start | bytes 602120 | tf_op jit(solution)/shard_map/ppermute | solution.py:181
  90.9 3.2 %collective-permute-done.10 = f16[784,128]{1,0:T(8,128)(2,1)S(1)} collective-permute-done((f16[784,128]{1,0:T(8,128)(2,1)S(1)}, f16[784,128]{1,0:T(8,128)(2,1)S(1)}, u32[]{:S(2)}, u32[]{:S(2)}) %collective-permute-start.10) | collective-permute-done | bytes 200736 | tf_op jit(solution)/shard_map/ppermute | solution.py:181
  94.1 0.8 select_convert_fusion
  94.9 5.6 %collective-permute-start.11 = (f16[784,128]{1,0:T(8,128)(2,1)S(1)}, f16[784,128]{1,0:T(8,128)(2,1)S(1)}, u32[]{:S(2)}, u32[]{:S(2)}) collective-permute-start(f16[784,128]{1,0:T(8,128)(2,1)S(1)} %select_convert_fusion), channel_id=1, source_target_pairs={{0,22},{1,3},{2,0},{3,5},{4,2},{5,7},{6,4},{7,9},{8,6},{9,11},{10,... | collective-permute-start | bytes 602120 | tf_op jit(solution)/shard_map/ppermute | solution.py:181
  100.5 3.2 %collective-permute-done.11 = f16[784,128]{1,0:T(8,128)(2,1)S(1)} collective-permute-done((f16[784,128]{1,0:T(8,128)(2,1)S(1)}, f16[784,128]{1,0:T(8,128)(2,1)S(1)}, u32[]{:S(2)}, u32[]{:S(2)}) %collective-permute-start.11) | collective-permute-done | bytes 200736 | tf_op jit(solution)/shard_map/ppermute | solution.py:181
  103.7 0.2 add_add_fusion.sums
  104.0 1.8 %residual.1 = f32[256,256]{1,0:T(8,128)} custom-call(s32[2]{0:T(128)S(1)} %bitcast.88, s32[2]{0:T(128)S(1)} %bitcast.89, s32[2]{0:T(128)S(1)} %bitcast.90, f32[100]{0:T(128)S(1)} %copy-done.14, f32[12,128]{1,0:T(8,128)S(1)} %bitcast.87, f32[784,128]{1,0:T(8,128)S(1)} %add_add_fusion.sums, bf16[256,256]{1,0:T(8,128)(2,1)S(1)} %bitcast.86), custom_call_target="tpu_custom_call" | custom-call | tf_op jit(solution)/shard_map/residual/pallas_call | solution.py:233
  (49 shorter events, 0.3 us)
Async XLA Ops:
  3.4 15.0 %collective-permute-start = (bf16[12,84,512]{2,1,0:T(8,128)(2,1)}, bf16[12,84,512]{2,1,0:T(8,128)(2,1)S(1)}, u32[]{:S(2)}, u32[]{:S(2)}) collective-permute-start(bf16[12,84,512]{2,1,0:T(8,128)(2,1)} %split_cores.1), channel_id=1, source_target_pairs={{0,1},{1,0},{2,3},{3,2},{4,5},{5,4},{6,7},{7,6},{8,9},{9,8},{10,11... | collective-permute-start | bytes 3096584 | tf_op jit(solution)/shard_map/ppermute | solution.py:189
  5.3 56.0 %all-to-all-start = ((bf16[1,32,256,8]{2,3,0,1:T(8,128)(2,1)}), bf16[1,32,256,8]{2,3,0,1:T(8,128)(2,1)S(1)}, u32[]{:S(2)}, u32[]{:S(2)}) async-start(bf16[1,32,256,8]{2,3,0,1:T(8,128)(2,1)} %bitcast.23), calls=%async_computation | async-start | bytes 262144 | tf_op jit(solution)/shard_map/all_to_all | solution.py:183
  19.2 16.7 %collective-permute-start.1 = (bf16[2,84,512]{2,1,0:T(8,128)(2,1)S(1)}, bf16[2,84,512]{2,1,0:T(8,128)(2,1)S(1)}, u32[]{:S(2)}, u32[]{:S(2)}) collective-permute-start(bf16[2,84,512]{2,1,0:T(8,128)(2,1)S(1)} %get-tuple-element.19), channel_id=1, source_target_pairs={{0,6},{1,19},{2,8},{3,21},{4,10},{5,23},{6,12},{7,1},{8,14},{9,3},... | collective-permute-start | bytes 516104 | tf_op jit(solution)/shard_map/ppermute | solution.py:181
  24.3 18.0 %collective-permute-start.2 = (bf16[2,84,512]{2,1,0:T(8,128)(2,1)S(1)}, bf16[2,84,512]{2,1,0:T(8,128)(2,1)S(1)}, u32[]{:S(2)}, u32[]{:S(2)}) collective-permute-start(bf16[2,84,512]{2,1,0:T(8,128)(2,1)S(1)} %get-tuple-element.20), channel_id=1, source_target_pairs={{0,4},{1,21},{2,6},{3,23},{4,8},{5,1},{6,10},{7,3},{8,12},{9,5},{1... | collective-permute-start | bytes 516104 | tf_op jit(solution)/shard_map/ppermute | solution.py:181
  31.6 12.5 %collective-permute-start.3 = (bf16[2,84,512]{2,1,0:T(8,128)(2,1)S(1)}, bf16[2,84,512]{2,1,0:T(8,128)(2,1)S(1)}, u32[]{:S(2)}, u32[]{:S(2)}) collective-permute-start(bf16[2,84,512]{2,1,0:T(8,128)(2,1)S(1)} %get-tuple-element.21), channel_id=1, source_target_pairs={{0,2},{1,23},{2,4},{3,1},{4,6},{5,3},{6,8},{7,5},{8,10},{9,7},{10,... | collective-permute-start | bytes 516104 | tf_op jit(solution)/shard_map/ppermute | solution.py:181
  35.9 9.1 %copy-start.19 = (pred[784]{0:T(1024)(128)(4,1)}, pred[784]{0:T(1024)(128)(4,1)S(1)}, u32[]{:S(2)}) copy-start(pred[784]{0:T(1024)(128)(4,1)S(1)} %iota_compare_fusion.2) | copy-start | bytes 2356
  35.9 9.0 %copy-start.15 = (pred[784]{0:T(1024)(128)(4,1)}, pred[784]{0:T(1024)(128)(4,1)S(1)}, u32[]{:S(2)}) copy-start(pred[784]{0:T(1024)(128)(4,1)S(1)} %get-tuple-element.80) | copy-start | bytes 2356
  35.9 9.0 %copy-start.17 = (pred[784]{0:T(1024)(128)(4,1)}, pred[784]{0:T(1024)(128)(4,1)S(1)}, u32[]{:S(2)}) copy-start(pred[784]{0:T(1024)(128)(4,1)S(1)} %get-tuple-element.79) | copy-start | bytes 2356
  46.3 18.4 %collective-permute-start.4 = (f16[784,128]{1,0:T(8,128)(2,1)}, f16[784,128]{1,0:T(8,128)(2,1)}, u32[]{:S(2)}, u32[]{:S(2)}) collective-permute-start(f16[784,128]{1,0:T(8,128)(2,1)} %select_convert_fusion.5), channel_id=1, source_target_pairs={{0,2},{1,23},{2,4},{3,1},{4,6},{5,3},{6,8},{7,5},{8,10},{9,7},{10,... | collective-permute-start | bytes 602120 | tf_op jit(solution)/shard_map/ppermute | solution.py:181
  48.8 12.5 %collective-permute-start.8 = (bf16[2,84,512]{2,1,0:T(8,128)(2,1)}, bf16[2,84,512]{2,1,0:T(8,128)(2,1)S(1)}, u32[]{:S(2)}, u32[]{:S(2)}) collective-permute-start(bf16[2,84,512]{2,1,0:T(8,128)(2,1)} %get-tuple-element.25), channel_id=1, source_target_pairs={{0,22},{1,3},{2,0},{3,5},{4,2},{5,7},{6,4},{7,9},{8,6},{9,11},{10,... | collective-permute-start | bytes 516104 | tf_op jit(solution)/shard_map/ppermute | solution.py:181
  53.4 9.8 %collective-permute-start.7 = (bf16[2,84,512]{2,1,0:T(8,128)(2,1)}, bf16[2,84,512]{2,1,0:T(8,128)(2,1)}, u32[]{:S(2)}, u32[]{:S(2)}) collective-permute-start(bf16[2,84,512]{2,1,0:T(8,128)(2,1)} %get-tuple-element.24), channel_id=1, source_target_pairs={{0,20},{1,5},{2,22},{3,7},{4,0},{5,9},{6,2},{7,11},{8,4},{9,13},{1... | collective-permute-start | bytes 516104 | tf_op jit(solution)/shard_map/ppermute | solution.py:181
  57.5 0.8 copy-start
  58.3 0.8 copy-start.2
  59.0 0.8 copy-start.4
  59.8 0.7 copy-start.6
  60.6 0.7 copy-start.8
  61.3 4.5 %copy-start.7 = (f32[784,128]{1,0:T(8,128)S(1)}, f32[784,128]{1,0:T(8,128)}, u32[]{:S(2)}) copy-start(f32[784,128]{1,0:T(8,128)} %copy-done.6) | copy-start | bytes 1204228
  61.3 4.5 %copy-start.16 = (pred[784]{0:T(1024)(128)(4,1)S(1)}, pred[784]{0:T(1024)(128)(4,1)}, u32[]{:S(2)}) copy-start(pred[784]{0:T(1024)(128)(4,1)} %copy-done.15) | copy-start | bytes 2356
  61.3 4.5 %copy-start.18 = (pred[784]{0:T(1024)(128)(4,1)S(1)}, pred[784]{0:T(1024)(128)(4,1)}, u32[]{:S(2)}) copy-start(pred[784]{0:T(1024)(128)(4,1)} %copy-done.17) | copy-start | bytes 2356
  61.3 4.5 %copy-start.20 = (pred[784]{0:T(1024)(128)(4,1)S(1)}, pred[784]{0:T(1024)(128)(4,1)}, u32[]{:S(2)}) copy-start(pred[784]{0:T(1024)(128)(4,1)} %copy-done.19) | copy-start | bytes 2356
  61.3 15.0 %copy-start.5 = (f32[784,128]{1,0:T(8,128)S(1)}, f32[784,128]{1,0:T(8,128)}, u32[]{:S(2)}) copy-start(f32[784,128]{1,0:T(8,128)} %copy-done.4) | copy-start | bytes 1204228
  64.8 20.6 %copy-start.3 = (f32[784,128]{1,0:T(8,128)S(1)}, f32[784,128]{1,0:T(8,128)}, u32[]{:S(2)}) copy-start(f32[784,128]{1,0:T(8,128)} %copy-done.2) | copy-start | bytes 1204228
  67.5 8.8 %collective-permute-start.5 = (f16[784,128]{1,0:T(8,128)(2,1)S(1)}, f16[784,128]{1,0:T(8,128)(2,1)S(1)}, u32[]{:S(2)}, u32[]{:S(2)}) collective-permute-start(f16[784,128]{1,0:T(8,128)(2,1)S(1)} %select_convert_fusion.4), channel_id=1, source_target_pairs={{0,2},{1,23},{2,4},{3,1},{4,6},{5,3},{6,8},{7,5},{8,10},{9,7},{10,... | collective-permute-start | bytes 602120 | tf_op jit(solution)/shard_map/ppermute | solution.py:181
  76.3 17.7 %copy-start.1 = (f32[784,128]{1,0:T(8,128)S(1)}, f32[784,128]{1,0:T(8,128)}, u32[]{:S(2)}) copy-start(f32[784,128]{1,0:T(8,128)} %copy-done) | copy-start | bytes 1204228
  77.2 26.6 %copy-start.9 = (f32[784,128]{1,0:T(8,128)S(1)}, f32[784,128]{1,0:T(8,128)}, u32[]{:S(2)}) copy-start(f32[784,128]{1,0:T(8,128)} %copy-done.8) | copy-start | bytes 1204228
  77.2 8.2 %collective-permute-start.9 = (f16[784,128]{1,0:T(8,128)(2,1)S(1)}, f16[784,128]{1,0:T(8,128)(2,1)S(1)}, u32[]{:S(2)}, u32[]{:S(2)}) collective-permute-start(f16[784,128]{1,0:T(8,128)(2,1)S(1)} %get-tuple-element.78), channel_id=1, source_target_pairs={{0,22},{1,3},{2,0},{3,5},{4,2},{5,7},{6,4},{7,9},{8,6},{9,11},{10,... | collective-permute-start | bytes 602120 | tf_op jit(solution)/shard_map/ppermute | solution.py:181
  79.5 11.4 %collective-permute-start.6 = (f16[784,128]{1,0:T(8,128)(2,1)S(1)}, f16[784,128]{1,0:T(8,128)(2,1)S(1)}, u32[]{:S(2)}, u32[]{:S(2)}) collective-permute-start(f16[784,128]{1,0:T(8,128)(2,1)S(1)} %get-tuple-element.77), channel_id=1, source_target_pairs={{0,2},{1,23},{2,4},{3,1},{4,6},{5,3},{6,8},{7,5},{8,10},{9,7},{10,... | collective-permute-start | bytes 602120 | tf_op jit(solution)/shard_map/ppermute | solution.py:181
  86.2 17.8 %copy-start.10 = (f32[1536]{0:T(1024)S(1)}, f32[1536]{0:T(1024)}, u32[]{:S(2)}) copy-start(f32[1536]{0:T(1024)} %param.12) | copy-start | bytes 18436
  86.2 17.8 %copy-start.11 = (s32[1,1,2]{2,1,0:T(1,128)S(1)}, s32[1,1,2]{2,1,0:T(1,128)}, u32[]{:S(2)}) copy-start(s32[1,1,2]{2,1,0:T(1,128)} %param.9) | copy-start | bytes 28
  86.2 17.8 %copy-start.12 = (s32[1,1,2]{2,1,0:T(1,128)S(1)}, s32[1,1,2]{2,1,0:T(1,128)}, u32[]{:S(2)}) copy-start(s32[1,1,2]{2,1,0:T(1,128)} %param.10) | copy-start | bytes 28
  86.2 17.8 %copy-start.13 = (s32[1,1,2]{2,1,0:T(1,128)S(1)}, s32[1,1,2]{2,1,0:T(1,128)}, u32[]{:S(2)}) copy-start(s32[1,1,2]{2,1,0:T(1,128)} %param.11) | copy-start | bytes 28
  86.2 17.8 %copy-start.14 = (f32[100]{0:T(128)S(1)}, f32[100]{0:T(128)}, u32[]{:S(2)}) copy-start(f32[100]{0:T(128)} %occ.1) | copy-start | bytes 1204
  86.3 7.8 %collective-permute-start.10 = (f16[784,128]{1,0:T(8,128)(2,1)S(1)}, f16[784,128]{1,0:T(8,128)(2,1)S(1)}, u32[]{:S(2)}, u32[]{:S(2)}) collective-permute-start(f16[784,128]{1,0:T(8,128)(2,1)S(1)} %select_convert_fusion.1), channel_id=1, source_target_pairs={{0,22},{1,3},{2,0},{3,5},{4,2},{5,7},{6,4},{7,9},{8,6},{9,11},{10,... | collective-permute-start | bytes 602120 | tf_op jit(solution)/shard_map/ppermute | solution.py:181
  94.9 8.8 %collective-permute-start.11 = (f16[784,128]{1,0:T(8,128)(2,1)S(1)}, f16[784,128]{1,0:T(8,128)(2,1)S(1)}, u32[]{:S(2)}, u32[]{:S(2)}) collective-permute-start(f16[784,128]{1,0:T(8,128)(2,1)S(1)} %select_convert_fusion), channel_id=1, source_target_pairs={{0,22},{1,3},{2,0},{3,5},{4,2},{5,7},{6,4},{7,9},{8,6},{9,11},{10,... | collective-permute-start | bytes 602120 | tf_op jit(solution)/shard_map/ppermute | solution.py:181

commit v3 on v2

--- a/solution.py
+++ b/solution.py
@@ -18,18 +18,15 @@
 F16 = jnp.float16
 
 
-def sign(core, stream):
-    return 1 - 2 * ((core + stream) % 2)
-
-
 def here():
     me = lax.axis_index("aux")
-    return lax.div(me, 2), lax.rem(me, 2)
-
-
-def dest(chips, stream, distance):
-    z, c = here()
-    return lax.rem(z + sign(c, stream) * distance + chips, chips)
+    c = lax.rem(me, 2)
+    return lax.div(me, 2), c, 1 - 2 * c
+
+
+def toward(chips, distance):
+    z, _, way = here()
+    return lax.rem(z + way * distance + chips, chips)
 
 
 def iotas():
@@ -49,7 +46,7 @@
     return jnp.broadcast_to(power, (1, TILE))
 
 
-def packed_sum(blocks, out):
+def packed_sum(blocks, out, scaled=False):
     total = None
     for block in blocks:
         term = lax.dot_general(
@@ -62,14 +59,18 @@
     h0, h1 = total[:, 2 * TILE : 3 * TILE], total[:, 3 * TILE :]
     fold = jnp.where(row <= col, g00, g11)
     diag = jnp.sum(jnp.where(row == col, g11, 0.0), axis=0, keepdims=True)
+    e_h, e_g = exponent(h0, h1), exponent(g01, fold, diag)
+    if scaled:
+        by_h, by_g = jnp.exp2(e_h), jnp.exp2(e_g)
+        h0, h1, g01, fold, diag = h0 * by_h, h1 * by_h, g01 * by_g, fold * by_g, diag * by_g
     out[: 2 * TILE] = h0
     out[2 * TILE : H_ROWS] = h1
     out[H_ROWS : H_ROWS + TILE] = g01
     out[H_ROWS + TILE : DIAG] = fold
     lines = lax.broadcasted_iota(jnp.int32, (ROWS - DIAG, TILE), 0)
     rest = jnp.where(lines == 0, diag, 0.0)
-    rest = jnp.where(lines == H_EXP - DIAG, exponent(h0, h1), rest)
-    out[DIAG:] = jnp.where(lines == G_EXP - DIAG, exponent(g01, fold, diag), rest)
+    rest = jnp.where(lines == H_EXP - DIAG, e_h, rest)
+    out[DIAG:] = jnp.where(lines == G_EXP - DIAG, e_g, rest)
 
 
 def scales(e_h, e_g):
@@ -90,33 +91,48 @@
 
 
 def split_kernel(chips, ints, out):
+    z, c, _ = here()
+    near = chips // 2 - 1
+    for d in range(1, near + 1):
+        to = toward(chips, -d)
+        out[2 * d - 2] = ints[2 * to + 1 - c]
+        out[2 * d - 1] = ints[2 * to + c]
+    out[2 * near] = ints[2 * lax.rem(z + near + 1, chips) + 1 - c]
+    out[2 * near + 1] = ints[2 * z + 1 - c]
+
+
+def chip_rows(chips, ints, other, distance, mine):
     c = here()[1]
-    for chip in range(chips):
-        out[chip] = ints[2 * chip + 1 - c]
-
-
-def pack_kernel(chips, ways, ints, other, *outs):
-    c = here()[1]
-    for (s, d), out in zip(ways, outs):
-        to = dest(chips, s, d)
-        out[0] = ints[2 * to + c]
-        out[1] = other[to]
-
-
-def own_kernel(chips, near, ints, other, *outs):
-    c = here()[1]
-    for (s, d), out in zip(near, outs):
-        to = dest(chips, s, d)
-        packed_sum([ints[2 * to + c], other[to]], out)
-
-
-def far_kernel(chips, stream, ints, other, *rest):
-    c = here()[1]
-    to = dest(chips, stream, HOPS)
-    blocks = [ints[2 * to + c], other[to]]
+    near = chips // 2 - 1
+    if distance == 0:
+        at = 2 * near + 1
+    elif distance > near:
+        at = 2 * near
+    else:
+        at = 2 * distance - 1 - int(mine)
+    return [ints[2 * toward(chips, distance) + (c if mine else 1 - c)], other[at]]
+
+
+def pack_kernel(chips, distances, ints, other, *outs):
+    for d, out in zip(distances, outs):
+        rows = chip_rows(chips, ints, other, d, True)
+        if d < chips // 2:
+            rows += chip_rows(chips, ints, other, d, False)
+        for n, row in enumerate(rows):
+            out[n] = row
+
+
+def own_kernel(chips, wanted, ints, other, *outs):
+    for (d, mine), out in zip(wanted, outs):
+        packed_sum(chip_rows(chips, ints, other, d, mine), out)
+
+
+def far_kernel(chips, mine, ints, other, *rest):
+    blocks = chip_rows(chips, ints, other, HOPS, mine)
     for ref in rest[:-1]:
-        blocks += [ref[0], ref[1]]
-    packed_sum(blocks, rest[-1])
+        at = 0 if mine else 2
+        blocks += [ref[at], ref[at + 1]]
+    packed_sum(blocks, rest[-1], scaled=True)
 
 
 def final_kernel(occ_at, tiles, mask, occ, virt, sums, amps_t, out):
@@ -172,13 +188,21 @@
             name=name,
         )
 
-    def permute(x, stream, hops):
+    def permute(x, hops, cross=False):
         pairs = []
         for chip in range(chips):
             for core in range(2):
-                to = (chip + sign(core, stream) * hops) % chips
-                pairs.append((chip * 2 + core, to * 2 + core))
+                to = (chip + (1 - 2 * core) * hops) % chips
+                pairs.append((chip * 2 + core, to * 2 + (core ^ int(cross))))
         return lax.ppermute(x, "aux", pairs)
+
+    def summed(wanted, other):
+        return call(
+            functools.partial(own_kernel, chips, wanted),
+            2,
+            [((ROWS, TILE), F32)] * len(wanted),
+            "own_sums",
+        )(ints, other)
 
     owned = lax.all_to_all(amplitudes, "pair", split_axis=1, concat_axis=3, tiled=True)
 
@@ -188,47 +212,40 @@
     )(ints)
     other = lax.ppermute(other, "aux", [(i, i ^ 1) for i in range(2 * chips)])
 
-    ways = [(s, d) for d in range(far, HOPS, -1) for s in range(2) if d < far or s == 0]
+    distances = list(range(far, HOPS, -1))
     sends = call(
-        functools.partial(pack_kernel, chips, ways),
+        functools.partial(pack_kernel, chips, distances),
         2,
-        [((2, naux, wide), BF16)] * len(ways),
+        [((2 if d == far else 4, naux, wide), BF16) for d in distances],
         "pack_rows",
     )(ints, other)
-    rows = [[], []]
-    for (s, d), x in zip(ways, sends):
-        rows[s].append(permute(x, s, d - HOPS))
-
-    near = [(s, d) for d in range(HOPS - 1, 0, -1) for s in range(2)] + [(0, 0)]
-    local = call(
-        functools.partial(own_kernel, chips, near),
-        2,
-        [((ROWS, TILE), F32)] * len(near),
-        "own_sums",
-    )(ints, other)
-
-    rows[1][-1], owned = lax.optimization_barrier((rows[1][-1], owned))
+    rows = [permute(x, d - HOPS) for d, x in zip(distances, sends)]
+    rows[-1], owned = lax.optimization_barrier((rows[-1], owned))
     amps_t = jnp.swapaxes(owned[0, 0], 0, 1)
 
     moving = []
-    for s in range(2):
+    for mine in (True, False):
         (x,) = call(
-            functools.partial(far_kernel, chips, s), 2 + len(rows[s]), [((ROWS, TILE), F32)], "far_sum"
-        )(ints, other, *rows[s])
-        moving.append(
-            permute(encode(x, x[H_EXP : H_EXP + 1], x[G_EXP : G_EXP + 1]), s, 1)
-        )
-    for hop in range(1, HOPS):
-        for s in range(2):
-            x, e_h, e_g = decode(moving[s])
-            mine = local[2 * (hop - 1) + s]
-            e_h = jnp.minimum(e_h, mine[H_EXP : H_EXP + 1]) - 1.0
-            e_g = jnp.minimum(e_g, mine[G_EXP : G_EXP + 1]) - 1.0
-            x = encode(x + mine, e_h, e_g)
-            moving[s] = permute(x, s, 1)
-            if s == 0:
+            functools.partial(far_kernel, chips, mine),
+            2 + len(rows[0 if mine else 1 :]),
+            [((ROWS, TILE), F32)],
+            "far_sum",
+        )(ints, other, *rows[0 if mine else 1 :])
+        x = x.astype(F16)
+        moving.append(permute(x, 1, HOPS == 1 and not mine))
+    for d in range(HOPS - 1, 0, -1):
+        local = summed([(d, True), (d, False)], lax.optimization_barrier((other, x))[0])
+        for n in range(2):
+            x, e_h, e_g = decode(moving[n])
+            own = local[n]
+            e_h = jnp.minimum(e_h, own[H_EXP : H_EXP + 1]) - 1.0
+            e_g = jnp.minimum(e_g, own[G_EXP : G_EXP + 1]) - 1.0
+            x = encode(x + own, e_h, e_g)
+            moving[n] = permute(x, 1, d == 1 and n == 1)
+            if n == 0:
                 moving[1] = lax.optimization_barrier((moving[1], x))[0]
-    sums = decode(moving[0])[0] + decode(moving[1])[0] + local[-1]
+    (local,) = summed([(0, True)], lax.optimization_barrier((other, x))[0])
+    sums = decode(moving[0])[0] + decode(moving[1])[0] + local
 
     (out,) = call(final_kernel, 3, [((2 * TILE, 2 * TILE), F32)], "residual", 4)(
         pair_occ.reshape(-1),

time: 106 us -> 83.9 us (0.79)
  the two profiles are of different devices: /device:TPU:2 before, /device:TPU:1 now
where the time goes in v3:
time: 83.9 us; the launch traced here: 83.4 us
  starting transfers between devices  57.1 us (68%)
  waiting for transfers between devices  11.4 us (14%)
  Pallas kernels  8.05 us (10%)
  other arithmetic  3.54 us (4%)
  local copies, waits for them, and re-layouts  2.95 us (4%)
    ppermute x9, starting transfers between devices, permute(): return lax.ppermute(x, 'aux', pairs)  34.9 us
    ppermute x1, starting transfers between devices, on_device(): other = lax.ppermute(other, 'aux', [(i, i ^ 1) for i in range(2 * chips)])  12.4 us
    all_to_all x1, starting transfers between devices, on_device(): lax.all_to_all(amplitudes, 'pair', split_axis=1, concat_axis=3, tiled=True)  9.69 us
    all_to_all x1, waiting for transfers between devices, on_device(): lax.all_to_all(amplitudes, 'pair', split_axis=1, concat_axis=3, tiled=True)  6.23 us
    pallas_call x2, Pallas kernels, on_device(): call(functools.partial(far_kernel, chips, mine), 2 + len(rows[0 if mine e...  3.76 us
    convert_element_type x4, other arithmetic, encode(): return jnp.where(row <= DIAG, x * scale, tail).astype(F16)  2.99 us
    unnamed x13, local copies, waits for them, and re-layouts  2.95 us
    ppermute x9, waiting for transfers between devices, permute(): return lax.ppermute(x, 'aux', pairs)  2.88 us
  transfers between devices with their start and end apart: 11, of which 3 were waited for; matrix products, arithmetic and copies ran while one was open for 4% of the time, Pallas kernels for 4%

profile of v3, /device:TPU:1, one launch (start us, length us, event | category | flops | bytes accessed | tf_op | source)
XLA Modules:
  0.0 83.4 jit_solution(6105588245213231164)
XLA Ops:
  0.0 2.3 %copy.12 = bf16[24,1,84,512]{3,2,0,1:T(8,128)(2,1)S(1)} copy(bf16[24,1,84,512]{3,0,2,1:T(8,128)(2,1)} %param.8) | data formatting | bytes 4128768 | tf_op args[1]
  2.3 0.1 split_cores.1
  2.4 12.4 %collective-permute-start = (bf16[12,84,512]{2,1,0:T(8,128)(2,1)S(1)}, bf16[12,84,512]{2,1,0:T(8,128)(2,1)S(1)}, u32[]{:S(2)}, u32[]{:S(2)}) collective-permute-start(bf16[12,84,512]{2,1,0:T(8,128)(2,1)S(1)} %split_cores.1), channel_id=1, source_target_pairs={{0,1},{1,0},{2,3},{3,2},{4,5},{5,4},{6,7},{7,6},{8,9},{9,8},{10,11... | collective-permute-start | bytes 3096584 | tf_op jit(solution)/shard_map/ppermute | solution.py:213
  14.8 2.3 %collective-permute-done.other = bf16[12,84,512]{2,1,0:T(8,128)(2,1)S(1)} collective-permute-done((bf16[12,84,512]{2,1,0:T(8,128)(2,1)S(1)}, bf16[12,84,512]{2,1,0:T(8,128)(2,1)S(1)}, u32[]{:S(2)}, u32[]{:S(2)}) %collective-permute-start) | collective-permute-done | bytes 1032224 | tf_op jit(solution)/shard_map/ppermute | solution.py:213
  17.1 0.9 %pack_rows.1 = (bf16[2,84,512]{2,1,0:T(8,128)(2,1)S(1)}, bf16[4,84,512]{2,1,0:T(8,128)(2,1)}, bf16[4,84,512]{2,1,0:T(8,128)(2,1)}) custom-call(bf16[24,84,512]{2,1,0:T(8,128)(2,1)S(1)} %bitcast.66, bf16[12,84,512]{2,1,0:T(8,128)(2,1)S(1)} %collective-permute-done.other), custom_call_target="tpu_custom_call" | custom-call | tf_op jit(solution)/shard_map/pack_rows/pallas_call | solution.py:216
  18.0 0.0 copy-start.5
  18.0 0.7 copy-done.5
  18.7 5.3 %collective-permute-start.3 = (bf16[4,84,512]{2,1,0:T(8,128)(2,1)}, bf16[4,84,512]{2,1,0:T(8,128)(2,1)}, u32[]{:S(2)}, u32[]{:S(2)}) collective-permute-start(bf16[4,84,512]{2,1,0:T(8,128)(2,1)} %get-tuple-element.21), channel_id=1, source_target_pairs={{0,2},{1,23},{2,4},{3,1},{4,6},{5,3},{6,8},{7,5},{8,10},{9,7},{10,... | collective-permute-start | bytes 1032200 | tf_op jit(solution)/shard_map/ppermute | solution.py:197
  24.0 2.2 %collective-permute-start.2 = (bf16[4,84,512]{2,1,0:T(8,128)(2,1)}, bf16[4,84,512]{2,1,0:T(8,128)(2,1)}, u32[]{:S(2)}, u32[]{:S(2)}) collective-permute-start(bf16[4,84,512]{2,1,0:T(8,128)(2,1)} %get-tuple-element.20), channel_id=1, source_target_pairs={{0,4},{1,21},{2,6},{3,23},{4,8},{5,1},{6,10},{7,3},{8,12},{9,5},{1... | collective-permute-start | bytes 1032200 | tf_op jit(solution)/shard_map/ppermute | solution.py:197
  26.2 9.7 %all-to-all-start = ((bf16[1,32,256,8]{2,3,0,1:T(8,128)(2,1)}), bf16[1,32,256,8]{2,3,0,1:T(8,128)(2,1)S(1)}, u32[]{:S(2)}, u32[]{:S(2)}) async-start(bf16[1,32,256,8]{2,3,0,1:T(8,128)(2,1)} %bitcast.5), calls=%async_computation | async-start | bytes 262144 | tf_op jit(solution)/shard_map/all_to_all | solution.py:207
  35.9 3.1 %collective-permute-start.1 = (bf16[2,84,512]{2,1,0:T(8,128)(2,1)}, bf16[2,84,512]{2,1,0:T(8,128)(2,1)S(1)}, u32[]{:S(2)}, u32[]{:S(2)}) collective-permute-start(bf16[2,84,512]{2,1,0:T(8,128)(2,1)} %copy-done.5), channel_id=1, source_target_pairs={{0,6},{1,19},{2,8},{3,21},{4,10},{5,23},{6,12},{7,1},{8,14},{9,3},... | collective-permute-start | bytes 516104 | tf_op jit(solution)/shard_map/ppermute | solution.py:197
  39.0 6.2 %all-to-all-done = bf16[1,32,256,8]{2,3,0,1:T(8,128)(2,1)S(1)} async-done(((bf16[1,32,256,8]{2,3,0,1:T(8,128)(2,1)}), bf16[1,32,256,8]{2,3,0,1:T(8,128)(2,1)S(1)}, u32[]{:S(2)}, u32[]{:S(2)}) %all-to-all-start) | async-done | bytes 131104 | tf_op jit(solution)/shard_map/all_to_all | solution.py:207
  45.2 0.0 collective-permute-done.3.rest_2_.rest_1_
  45.2 0.0 collective-permute-done.1.rest_0_
  45.2 0.0 collective-permute-done.2.rest_1_.rest_0_
  45.2 1.9 %far_sum.2 = f32[784,128]{1,0:T(8,128)S(1)} custom-call(bf16[24,84,512]{2,1,0:T(8,128)(2,1)S(1)} %bitcast.67, bf16[12,84,512]{2,1,0:T(8,128)(2,1)S(1)} %collective-permute-done.other, bf16[2,84,512]{2,1,0:T(8,128)(2,1)S(1)} %collective-permute-done.1.rest_0_, bf16[4,84,512]{2,1,0:T(8,128)(2,1)} %collective-permute-done.2.rest_1_.rest_0_, ...), custom_call_target="tpu_custom_call" | custom-call | tf_op jit(solution)/shard_map/far_sum/pallas_call | solution.py:228
  47.2 5.3 %collective-permute-start.4 = (f16[784,128]{1,0:T(8,128)(2,1)S(1)}, f16[784,128]{1,0:T(8,128)(2,1)S(1)}, u32[]{:S(2)}, u32[]{:S(2)}) collective-permute-start(f16[784,128]{1,0:T(8,128)(2,1)S(1)} %convert_element_type.36), channel_id=1, source_target_pairs={{0,2},{1,23},{2,4},{3,1},{4,6},{5,3},{6,8},{7,5},{8,10},{9,7},{10,... | collective-permute-start | bytes 602120 | tf_op jit(solution)/shard_map/ppermute | solution.py:197
  52.6 1.8 %far_sum.3 = f32[784,128]{1,0:T(8,128)S(1)} custom-call(bf16[24,84,512]{2,1,0:T(8,128)(2,1)S(1)} %bitcast.68, bf16[12,84,512]{2,1,0:T(8,128)(2,1)S(1)} %collective-permute-done.other, bf16[4,84,512]{2,1,0:T(8,128)(2,1)} %collective-permute-done.2.rest_1_.rest_0_, bf16[4,84,512]{2,1,0:T(8,128)(2,1)} %collective-permute-done.3.rest_2_.rest_1_), custom_call_target="tpu_custom_call" | custom-call | tf_op jit(solution)/shard_map/far_sum/pallas_call | solution.py:228
  54.4 4.0 %collective-permute-start.6 = (f16[784,128]{1,0:T(8,128)(2,1)S(1)}, f16[784,128]{1,0:T(8,128)(2,1)S(1)}, u32[]{:S(2)}, u32[]{:S(2)}) collective-permute-start(f16[784,128]{1,0:T(8,128)(2,1)S(1)} %convert_element_type.38), channel_id=1, source_target_pairs={{0,2},{1,23},{2,4},{3,1},{4,6},{5,3},{6,8},{7,5},{8,10},{9,7},{10,... | collective-permute-start | bytes 602120 | tf_op jit(solution)/shard_map/ppermute | solution.py:197
  58.4 0.5 own_sums.3
  59.0 0.0 collective-permute-done.4
  59.0 0.7 select_convert_fusion.3
  59.8 1.9 %collective-permute-start.5 = (f16[784,128]{1,0:T(8,128)(2,1)S(1)}, f16[784,128]{1,0:T(8,128)(2,1)S(1)}, u32[]{:S(2)}, u32[]{:S(2)}) collective-permute-start(f16[784,128]{1,0:T(8,128)(2,1)S(1)} %select_convert_fusion.3), channel_id=1, source_target_pairs={{0,2},{1,23},{2,4},{3,1},{4,6},{5,3},{6,8},{7,5},{8,10},{9,7},{10,... | collective-permute-start | bytes 602120 | tf_op jit(solution)/shard_map/ppermute | solution.py:197
  61.7 0.0 collective-permute-done.6
  61.8 0.7 select_convert_fusion.2
  62.5 4.3 %collective-permute-start.8 = (f16[784,128]{1,0:T(8,128)(2,1)S(1)}, f16[784,128]{1,0:T(8,128)(2,1)S(1)}, u32[]{:S(2)}, u32[]{:S(2)}) collective-permute-start(f16[784,128]{1,0:T(8,128)(2,1)S(1)} %select_convert_fusion.2), channel_id=1, source_target_pairs={{0,2},{1,23},{2,4},{3,1},{4,6},{5,3},{6,8},{7,5},{8,10},{9,7},{10,... | collective-permute-start | bytes 602120 | tf_op jit(solution)/shard_map/ppermute | solution.py:197
  66.9 0.5 own_sums.4
  67.4 0.0 collective-permute-done.5
  67.5 0.8 select_convert_fusion.1
  68.3 1.9 %collective-permute-start.7 = (f16[784,128]{1,0:T(8,128)(2,1)S(1)}, f16[784,128]{1,0:T(8,128)(2,1)S(1)}, u32[]{:S(2)}, u32[]{:S(2)}) collective-permute-start(f16[784,128]{1,0:T(8,128)(2,1)S(1)} %select_convert_fusion.1), channel_id=1, source_target_pairs={{0,2},{1,23},{2,4},{3,1},{4,6},{5,3},{6,8},{7,5},{8,10},{9,7},{10,... | collective-permute-start | bytes 602120 | tf_op jit(solution)/shard_map/ppermute | solution.py:197
  70.2 0.0 collective-permute-done.8
  70.3 0.7 select_convert_fusion
  71.0 6.9 %collective-permute-start.9 = (f16[784,128]{1,0:T(8,128)(2,1)S(1)}, f16[784,128]{1,0:T(8,128)(2,1)S(1)}, u32[]{:S(2)}, u32[]{:S(2)}) collective-permute-start(f16[784,128]{1,0:T(8,128)(2,1)S(1)} %select_convert_fusion), channel_id=1, source_target_pairs={{0,3},{1,22},{2,5},{3,0},{4,7},{5,2},{6,9},{7,4},{8,11},{9,6},{10,... | collective-permute-start | bytes 602120 | tf_op jit(solution)/shard_map/ppermute | solution.py:197
  77.9 0.4 own_sums.5
  78.3 0.0 copy-start
  78.3 0.0 copy-start.1
  78.3 0.0 copy-start.2
  78.4 0.0 copy-start.3
  78.4 0.0 copy-start.4
  78.4 0.0 collective-permute-done.7
  78.4 2.9 %collective-permute-done.9 = f16[784,128]{1,0:T(8,128)(2,1)S(1)} collective-permute-done((f16[784,128]{1,0:T(8,128)(2,1)S(1)}, f16[784,128]{1,0:T(8,128)(2,1)S(1)}, u32[]{:S(2)}, u32[]{:S(2)}) %collective-permute-start.9) | collective-permute-done | bytes 200736 | tf_op jit(solution)/shard_map/ppermute | solution.py:197
  81.4 0.2 add_add_fusion.sums
  81.6 0.0 copy-done
  81.6 0.0 copy-done.1
  81.6 0.0 copy-done.2
  81.6 0.0 copy-done.3
  81.6 0.0 copy-done.4
  81.6 1.8 %residual.1 = f32[256,256]{1,0:T(8,128)} custom-call(s32[2]{0:T(128)S(1)} %bitcast.74, s32[2]{0:T(128)S(1)} %bitcast.75, s32[2]{0:T(128)S(1)} %bitcast.76, f32[100]{0:T(128)S(1)} %copy-done.4, f32[12,128]{1,0:T(8,128)S(1)} %bitcast.73, f32[784,128]{1,0:T(8,128)S(1)} %add_add_fusion.sums, bf16[256,256]{1,0:T(8,128)(2,1)S(1)} %bitcast.72), custom_call_target="tpu_custom_call" | custom-call | tf_op jit(solution)/shard_map/residual/pallas_call | solution.py:250
  (16 shorter events, 0.3 us)
Async XLA Ops:
  2.4 14.7 %collective-permute-start = (bf16[12,84,512]{2,1,0:T(8,128)(2,1)S(1)}, bf16[12,84,512]{2,1,0:T(8,128)(2,1)S(1)}, u32[]{:S(2)}, u32[]{:S(2)}) collective-permute-start(bf16[12,84,512]{2,1,0:T(8,128)(2,1)S(1)} %split_cores.1), channel_id=1, source_target_pairs={{0,1},{1,0},{2,3},{3,2},{4,5},{5,4},{6,7},{7,6},{8,9},{9,8},{10,11... | collective-permute-start | bytes 3096584 | tf_op jit(solution)/shard_map/ppermute | solution.py:213
  18.0 0.7 copy-start.5
  18.7 26.5 %collective-permute-start.3 = (bf16[4,84,512]{2,1,0:T(8,128)(2,1)}, bf16[4,84,512]{2,1,0:T(8,128)(2,1)}, u32[]{:S(2)}, u32[]{:S(2)}) collective-permute-start(bf16[4,84,512]{2,1,0:T(8,128)(2,1)} %get-tuple-element.21), channel_id=1, source_target_pairs={{0,2},{1,23},{2,4},{3,1},{4,6},{5,3},{6,8},{7,5},{8,10},{9,7},{10,... | collective-permute-start | bytes 1032200 | tf_op jit(solution)/shard_map/ppermute | solution.py:197
  24.0 21.2 %collective-permute-start.2 = (bf16[4,84,512]{2,1,0:T(8,128)(2,1)}, bf16[4,84,512]{2,1,0:T(8,128)(2,1)}, u32[]{:S(2)}, u32[]{:S(2)}) collective-permute-start(bf16[4,84,512]{2,1,0:T(8,128)(2,1)} %get-tuple-element.20), channel_id=1, source_target_pairs={{0,4},{1,21},{2,6},{3,23},{4,8},{5,1},{6,10},{7,3},{8,12},{9,5},{1... | collective-permute-start | bytes 1032200 | tf_op jit(solution)/shard_map/ppermute | solution.py:197
  26.2 19.0 %all-to-all-start = ((bf16[1,32,256,8]{2,3,0,1:T(8,128)(2,1)}), bf16[1,32,256,8]{2,3,0,1:T(8,128)(2,1)S(1)}, u32[]{:S(2)}, u32[]{:S(2)}) async-start(bf16[1,32,256,8]{2,3,0,1:T(8,128)(2,1)} %bitcast.5), calls=%async_computation | async-start | bytes 262144 | tf_op jit(solution)/shard_map/all_to_all | solution.py:207
  35.9 9.4 %collective-permute-start.1 = (bf16[2,84,512]{2,1,0:T(8,128)(2,1)}, bf16[2,84,512]{2,1,0:T(8,128)(2,1)S(1)}, u32[]{:S(2)}, u32[]{:S(2)}) collective-permute-start(bf16[2,84,512]{2,1,0:T(8,128)(2,1)} %copy-done.5), channel_id=1, source_target_pairs={{0,6},{1,19},{2,8},{3,21},{4,10},{5,23},{6,12},{7,1},{8,14},{9,3},... | collective-permute-start | bytes 516104 | tf_op jit(solution)/shard_map/ppermute | solution.py:197
  47.2 11.7 %collective-permute-start.4 = (f16[784,128]{1,0:T(8,128)(2,1)S(1)}, f16[784,128]{1,0:T(8,128)(2,1)S(1)}, u32[]{:S(2)}, u32[]{:S(2)}) collective-permute-start(f16[784,128]{1,0:T(8,128)(2,1)S(1)} %convert_element_type.36), channel_id=1, source_target_pairs={{0,2},{1,23},{2,4},{3,1},{4,6},{5,3},{6,8},{7,5},{8,10},{9,7},{10,... | collective-permute-start | bytes 602120 | tf_op jit(solution)/shard_map/ppermute | solution.py:197
  54.4 7.3 %collective-permute-start.6 = (f16[784,128]{1,0:T(8,128)(2,1)S(1)}, f16[784,128]{1,0:T(8,128)(2,1)S(1)}, u32[]{:S(2)}, u32[]{:S(2)}) collective-permute-start(f16[784,128]{1,0:T(8,128)(2,1)S(1)} %convert_element_type.38), channel_id=1, source_target_pairs={{0,2},{1,23},{2,4},{3,1},{4,6},{5,3},{6,8},{7,5},{8,10},{9,7},{10,... | collective-permute-start | bytes 602120 | tf_op jit(solution)/shard_map/ppermute | solution.py:197
  59.8 7.7 %collective-permute-start.5 = (f16[784,128]{1,0:T(8,128)(2,1)S(1)}, f16[784,128]{1,0:T(8,128)(2,1)S(1)}, u32[]{:S(2)}, u32[]{:S(2)}) collective-permute-start(f16[784,128]{1,0:T(8,128)(2,1)S(1)} %select_convert_fusion.3), channel_id=1, source_target_pairs={{0,2},{1,23},{2,4},{3,1},{4,6},{5,3},{6,8},{7,5},{8,10},{9,7},{10,... | collective-permute-start | bytes 602120 | tf_op jit(solution)/shard_map/ppermute | solution.py:197
  62.5 7.7 %collective-permute-start.8 = (f16[784,128]{1,0:T(8,128)(2,1)S(1)}, f16[784,128]{1,0:T(8,128)(2,1)S(1)}, u32[]{:S(2)}, u32[]{:S(2)}) collective-permute-start(f16[784,128]{1,0:T(8,128)(2,1)S(1)} %select_convert_fusion.2), channel_id=1, source_target_pairs={{0,2},{1,23},{2,4},{3,1},{4,6},{5,3},{6,8},{7,5},{8,10},{9,7},{10,... | collective-permute-start | bytes 602120 | tf_op jit(solution)/shard_map/ppermute | solution.py:197
  68.3 10.1 %collective-permute-start.7 = (f16[784,128]{1,0:T(8,128)(2,1)S(1)}, f16[784,128]{1,0:T(8,128)(2,1)S(1)}, u32[]{:S(2)}, u32[]{:S(2)}) collective-permute-start(f16[784,128]{1,0:T(8,128)(2,1)S(1)} %select_convert_fusion.1), channel_id=1, source_target_pairs={{0,2},{1,23},{2,4},{3,1},{4,6},{5,3},{6,8},{7,5},{8,10},{9,7},{10,... | collective-permute-start | bytes 602120 | tf_op jit(solution)/shard_map/ppermute | solution.py:197
  71.0 10.3 %collective-permute-start.9 = (f16[784,128]{1,0:T(8,128)(2,1)S(1)}, f16[784,128]{1,0:T(8,128)(2,1)S(1)}, u32[]{:S(2)}, u32[]{:S(2)}) collective-permute-start(f16[784,128]{1,0:T(8,128)(2,1)S(1)} %select_convert_fusion), channel_id=1, source_target_pairs={{0,3},{1,22},{2,5},{3,0},{4,7},{5,2},{6,9},{7,4},{8,11},{9,6},{10,... | collective-permute-start | bytes 602120 | tf_op jit(solution)/shard_map/ppermute | solution.py:197
  78.3 3.3 %copy-start = (f32[1536]{0:T(1024)S(1)}, f32[1536]{0:T(1024)}, u32[]{:S(2)}) copy-start(f32[1536]{0:T(1024)} %param.12) | copy-start | bytes 18436
  78.3 3.3 %copy-start.1 = (s32[1,1,2]{2,1,0:T(1,128)S(1)}, s32[1,1,2]{2,1,0:T(1,128)}, u32[]{:S(2)}) copy-start(s32[1,1,2]{2,1,0:T(1,128)} %param.9) | copy-start | bytes 28
  78.3 3.3 %copy-start.2 = (s32[1,1,2]{2,1,0:T(1,128)S(1)}, s32[1,1,2]{2,1,0:T(1,128)}, u32[]{:S(2)}) copy-start(s32[1,1,2]{2,1,0:T(1,128)} %param.10) | copy-start | bytes 28
  78.4 3.3 %copy-start.3 = (s32[1,1,2]{2,1,0:T(1,128)S(1)}, s32[1,1,2]{2,1,0:T(1,128)}, u32[]{:S(2)}) copy-start(s32[1,1,2]{2,1,0:T(1,128)} %param.11) | copy-start | bytes 28
  78.4 3.3 %copy-start.4 = (f32[100]{0:T(128)S(1)}, f32[100]{0:T(128)}, u32[]{:S(2)}) copy-start(f32[100]{0:T(128)} %occ.1) | copy-start | bytes 1204

commit v4 on v3

--- a/solution.py
+++ b/solution.py
@@ -8,7 +8,7 @@
 from jax.sharding import PartitionSpec as P
 
 TILE = 128
-HOPS = 3
+FIRST, SECOND = 4, 2
 H_ROWS, G_ROWS = 4 * TILE, 2 * TILE
 DIAG = H_ROWS + G_ROWS
 H_EXP, G_EXP = DIAG + 1, DIAG + 2
@@ -74,20 +74,27 @@
 
 
 def scales(e_h, e_g):
-    row = lax.broadcasted_iota(jnp.int32, (ROWS, TILE), 0)
+    row = lax.broadcasted_iota(jnp.int32, (1, ROWS, TILE), 1)
     return row, jnp.where(row < H_ROWS, jnp.exp2(e_h), jnp.exp2(e_g))
 
 
-def encode(x, e_h, e_g):
+def exponents(x):
+    return x[:, H_EXP : H_EXP + 1], x[:, G_EXP : G_EXP + 1]
+
+
+def decode(x):
+    x = x.astype(F32)
+    e_h, e_g = exponents(x)
+    return x * scales(-e_h, -e_g)[1], e_h, e_g
+
+
+def add_on(x, own):
+    x, e_h, e_g = decode(x)
+    own_h, own_g = exponents(own)
+    e_h, e_g = jnp.minimum(e_h, own_h) - 1.0, jnp.minimum(e_g, own_g) - 1.0
     row, scale = scales(e_h, e_g)
     tail = jnp.where(row == H_EXP, e_h, e_g)
-    return jnp.where(row <= DIAG, x * scale, tail).astype(F16)
-
-
-def decode(x):
-    x = x.astype(F32)
-    e_h, e_g = x[H_EXP : H_EXP + 1], x[G_EXP : G_EXP + 1]
-    return x * scales(-e_h, -e_g)[1], e_h, e_g
+    return jnp.where(row <= DIAG, (x + own) * scale, tail).astype(F16)
 
 
 def split_kernel(chips, ints, out):
@@ -113,26 +120,20 @@
     return [ints[2 * toward(chips, distance) + (c if mine else 1 - c)], other[at]]
 
 
-def pack_kernel(chips, distances, ints, other, *outs):
-    for d, out in zip(distances, outs):
-        rows = chip_rows(chips, ints, other, d, True)
-        if d < chips // 2:
-            rows += chip_rows(chips, ints, other, d, False)
-        for n, row in enumerate(rows):
+def pack_kernel(chips, wanted, ints, other, *outs):
+    for group, out in zip(wanted, outs):
+        for n, row in enumerate(sum((chip_rows(chips, ints, other, *w) for w in group), [])):
             out[n] = row
 
 
-def own_kernel(chips, wanted, ints, other, *outs):
-    for (d, mine), out in zip(wanted, outs):
-        packed_sum(chip_rows(chips, ints, other, d, mine), out)
-
-
-def far_kernel(chips, mine, ints, other, *rest):
-    blocks = chip_rows(chips, ints, other, HOPS, mine)
-    for ref in rest[:-1]:
-        at = 0 if mine else 2
-        blocks += [ref[at], ref[at + 1]]
-    packed_sum(blocks, rest[-1], scaled=True)
+def stop_kernel(chips, stop, owners, picks, scaled, ints, other, *rest):
+    received, out = rest[:-1], rest[-1]
+    for n, mine in enumerate(owners):
+        blocks = chip_rows(chips, ints, other, stop, mine)
+        for at, ref in picks:
+            if at[n] is not None:
+                blocks += [received[ref][at[n]], received[ref][at[n] + 1]]
+        packed_sum(blocks, out.at[n], scaled)
 
 
 def final_kernel(occ_at, tiles, mask, occ, virt, sums, amps_t, out):
@@ -184,7 +185,7 @@
             in_specs=[smem] * small + [vmem] * n_in,
             out_specs=[vmem] * len(shapes),
             out_shape=[jax.ShapeDtypeStruct(*s) for s in shapes],
-            compiler_params=pltpu.CompilerParams(vmem_limit_bytes=24 << 20),
+            compiler_params=pltpu.CompilerParams(vmem_limit_bytes=8 << 20),
             name=name,
         )
 
@@ -196,15 +197,27 @@
                 pairs.append((chip * 2 + core, to * 2 + (core ^ int(cross))))
         return lax.ppermute(x, "aux", pairs)
 
-    def summed(wanted, other):
+    def pack(wanted, other):
         return call(
-            functools.partial(own_kernel, chips, wanted),
+            functools.partial(pack_kernel, chips, wanted),
             2,
-            [((ROWS, TILE), F32)] * len(wanted),
-            "own_sums",
+            [((2 * len(group), naux, wide), BF16) for group in wanted],
+            "pack_rows",
         )(ints, other)
 
-    owned = lax.all_to_all(amplitudes, "pair", split_axis=1, concat_axis=3, tiled=True)
+    def stop_sums(stop, owners, picks, scaled, other, received):
+        return call(
+            functools.partial(stop_kernel, chips, stop, owners, picks, scaled),
+            2 + len(received),
+            [((len(owners), ROWS, TILE), F32)],
+            "stop_sums",
+        )(ints, other, *received)[0]
+
+    def pairs_at(d):
+        return [(d, True)] if d == far else [(d, True), (d, False)]
+
+    owned = lax.all_gather(jnp.swapaxes(amplitudes[0], 1, 2), "pair")
+    owned = lax.dynamic_index_in_dim(owned, lax.axis_index("pair"), 1, keepdims=False)
 
     ints = integrals[:, 0]
     (other,) = call(
@@ -212,40 +225,35 @@
     )(ints)
     other = lax.ppermute(other, "aux", [(i, i ^ 1) for i in range(2 * chips)])
 
-    distances = list(range(far, HOPS, -1))
-    sends = call(
-        functools.partial(pack_kernel, chips, distances),
-        2,
-        [((2 if d == far else 4, naux, wide), BF16) for d in distances],
-        "pack_rows",
-    )(ints, other)
-    rows = [permute(x, d - HOPS) for d, x in zip(distances, sends)]
-    rows[-1], owned = lax.optimization_barrier((rows[-1], owned))
-    amps_t = jnp.swapaxes(owned[0, 0], 0, 1)
-
-    moving = []
-    for mine in (True, False):
-        (x,) = call(
-            functools.partial(far_kernel, chips, mine),
-            2 + len(rows[0 if mine else 1 :]),
-            [((ROWS, TILE), F32)],
-            "far_sum",
-        )(ints, other, *rows[0 if mine else 1 :])
-        x = x.astype(F16)
-        moving.append(permute(x, 1, HOPS == 1 and not mine))
-    for d in range(HOPS - 1, 0, -1):
-        local = summed([(d, True), (d, False)], lax.optimization_barrier((other, x))[0])
-        for n in range(2):
-            x, e_h, e_g = decode(moving[n])
-            own = local[n]
-            e_h = jnp.minimum(e_h, own[H_EXP : H_EXP + 1]) - 1.0
-            e_g = jnp.minimum(e_g, own[G_EXP : G_EXP + 1]) - 1.0
-            x = encode(x + own, e_h, e_g)
-            moving[n] = permute(x, 1, d == 1 and n == 1)
-            if n == 0:
-                moving[1] = lax.optimization_barrier((moving[1], x))[0]
-    (local,) = summed([(0, True)], lax.optimization_barrier((other, x))[0])
-    sums = decode(moving[0])[0] + decode(moving[1])[0] + local
+    to_first = list(range(far, FIRST, -1))
+    to_second = list(range(FIRST - 1, SECOND, -1))
+    to_owner = list(range(SECOND - 1, 0, -1))
+    sends = pack([pairs_at(d) for d in to_first], other)
+    first_rows = [permute(x, d - FIRST) for d, x in zip(to_first, sends)]
+    gate = lax.optimization_barrier((other, *sends))[0]
+    sends = pack([pairs_at(d) for d in to_second], gate)
+    second_rows = [permute(x, d - SECOND) for d, x in zip(to_second, sends)]
+
+    picks = [((0, None) if d == far else (0, 2), at) for at, d in enumerate(to_first)]
+    x = stop_sums(FIRST, (True, False), picks, True, other, first_rows).astype(F16)
+    x, *second_rows = lax.optimization_barrier((x, *second_rows))
+    moving = permute(x, FIRST - SECOND)
+
+    gate = lax.optimization_barrier((other, x))[0]
+    sends = pack([[(d, mine)] for d in to_owner for mine in (True, False)], gate)
+    ways = [(d, n == 1) for d in to_owner for n in range(2)]
+    owner_rows = [permute(x, *way) for way, x in zip(ways, sends)]
+    picks = [((0, 2), at) for at in range(len(to_second))]
+    local = stop_sums(SECOND, (True, False), picks, False, gate, second_rows)
+    last = [add_on(moving[n : n + 1], local[n : n + 1])[0] for n in range(2)]
+    *last, owner_rows = lax.optimization_barrier((*last, owner_rows))
+    moving = [permute(last[n], SECOND, n == 1) for n in range(2)]
+
+    gate = lax.optimization_barrier((other, last[1]))[0]
+    picks = [((0,), at) for at in range(len(owner_rows))]
+    local = stop_sums(0, (True,), picks, False, gate, owner_rows)
+    sums = (decode(moving[0][None])[0] + decode(moving[1][None])[0] + local)[0]
+    amps_t = owned.reshape(2 * TILE, 2 * TILE)
 
     (out,) = call(final_kernel, 3, [((2 * TILE, 2 * TILE), F32)], "residual", 4)(
         pair_occ.reshape(-1),

time: 83.9 us -> 121 us (1.44)
  the two profiles are of different devices: /device:TPU:1 before, /device:TPU:8 now
where the time goes in v4:
time: 121 us; the launch traced here: 120 us
  waiting for transfers between devices  58.1 us (48%)
  starting transfers between devices  35.4 us (29%)
  between operations  13.7 us (11%)
  local copies, waits for them, and re-layouts  4.8 us (4%)
  Pallas kernels  4.48 us (4%)
  other arithmetic  3.76 us (3%)
    ppermute x8, starting transfers between devices, permute(): return lax.ppermute(x, 'aux', pairs)  33.5 us
    all_gather x1, waiting for transfers between devices, on_device(): owned = lax.all_gather(jnp.swapaxes(amplitudes[0], 1, 2), 'pair')  30.2 us
    ppermute x8, waiting for transfers between devices, permute(): return lax.ppermute(x, 'aux', pairs)  24.5 us
    unnamed x15, local copies, waits for them, and re-layouts  3.89 us
    ppermute x1, waiting for transfers between devices, on_device(): other = lax.ppermute(other, 'aux', [(i, i ^ 1) for i in range(2 * chips)])  2.67 us
    pallas_call x3, Pallas kernels, stop_sums(): call(functools.partial(stop_kernel, chips, stop, owners, picks, scaled),...  2.5 us
  transfers between devices with their start and end apart: 10, of which 8 were waited for; matrix products, arithmetic and copies ran while one was open for 5% of the time, Pallas kernels for 2%

profile of v4, /device:TPU:8, one launch (start us, length us, event | category | flops | bytes accessed | tf_op | source)
XLA Modules:
  0.0 120.2 jit_solution(16972858001482596737)
XLA Ops:
  6.5 0.0 all-gather.3.cloned.1.call-start
  6.5 0.7 all-gather.3.cloned.1.call-update
  7.3 2.3 %copy.14 = bf16[24,1,84,512]{3,2,0,1:T(8,128)(2,1)S(1)} copy(bf16[24,1,84,512]{3,0,2,1:T(8,128)(2,1)} %param.8) | data formatting | bytes 4128768 | tf_op args[1]
  9.5 0.1 split_cores.1
  9.6 1.9 %collective-permute-start = (bf16[12,84,512]{2,1,0:T(8,128)(2,1)S(1)}, bf16[12,84,512]{2,1,0:T(8,128)(2,1)S(1)}, u32[]{:S(2)}, u32[]{:S(2)}) collective-permute-start(bf16[12,84,512]{2,1,0:T(8,128)(2,1)S(1)} %split_cores.1), channel_id=1, source_target_pairs={{0,1},{1,0},{2,3},{3,2},{4,5},{5,4},{6,7},{7,6},{8,9},{9,8},{10,11... | collective-permute-start | bytes 3096584 | tf_op jit(solution)/shard_map/ppermute | solution.py:226
  11.6 2.7 %collective-permute-done.other = bf16[12,84,512]{2,1,0:T(8,128)(2,1)S(1)} collective-permute-done((bf16[12,84,512]{2,1,0:T(8,128)(2,1)S(1)}, bf16[12,84,512]{2,1,0:T(8,128)(2,1)S(1)}, u32[]{:S(2)}, u32[]{:S(2)}) %collective-permute-start) | collective-permute-done | bytes 1032224 | tf_op jit(solution)/shard_map/ppermute | solution.py:226
  14.3 4.3 %collective-permute-start.2 = (bf16[4,84,512]{2,1,0:T(8,128)(2,1)S(1)}, bf16[4,84,512]{2,1,0:T(8,128)(2,1)S(1)}, u32[]{:S(2)}, u32[]{:S(2)}) collective-permute-start(bf16[4,84,512]{2,1,0:T(8,128)(2,1)S(1)} %get-tuple-element.19), channel_id=1, source_target_pairs={{0,2},{1,23},{2,4},{3,1},{4,6},{5,3},{6,8},{7,5},{8,10},{9,7},{10,... | collective-permute-start | bytes 1032200 | tf_op jit(solution)/shard_map/ppermute | solution.py:198
  18.6 4.3 %collective-permute-start.3 = (bf16[4,84,512]{2,1,0:T(8,128)(2,1)S(1)}, bf16[4,84,512]{2,1,0:T(8,128)(2,1)S(1)}, u32[]{:S(2)}, u32[]{:S(2)}) collective-permute-start(bf16[4,84,512]{2,1,0:T(8,128)(2,1)S(1)} %pack_rows.4), channel_id=1, source_target_pairs={{0,2},{1,23},{2,4},{3,1},{4,6},{5,3},{6,8},{7,5},{8,10},{9,7},{10,... | collective-permute-start | bytes 1032200 | tf_op jit(solution)/shard_map/ppermute | solution.py:198
  22.9 7.3 %collective-permute-start.1 = (bf16[2,84,512]{2,1,0:T(8,128)(2,1)S(1)}, bf16[2,84,512]{2,1,0:T(8,128)(2,1)S(1)}, u32[]{:S(2)}, u32[]{:S(2)}) collective-permute-start(bf16[2,84,512]{2,1,0:T(8,128)(2,1)S(1)} %get-tuple-element.18), channel_id=1, source_target_pairs={{0,4},{1,21},{2,6},{3,23},{4,8},{5,1},{6,10},{7,3},{8,12},{9,5},{1... | collective-permute-start | bytes 516104 | tf_op jit(solution)/shard_map/ppermute | solution.py:198
  30.2 11.4 %collective-permute-done.1.rest_0_ = bf16[2,84,512]{2,1,0:T(8,128)(2,1)S(1)} collective-permute-done((bf16[2,84,512]{2,1,0:T(8,128)(2,1)S(1)}, bf16[2,84,512]{2,1,0:T(8,128)(2,1)S(1)}, u32[]{:S(2)}, u32[]{:S(2)}) %collective-permute-start.1) | collective-permute-done | bytes 172064 | tf_op jit(solution)/shard_map/ppermute | solution.py:198
  41.6 0.0 collective-permute-done.2.rest_1_
  41.6 1.0 stop_sums.3
  42.7 0.1 convert_element_type.27
  42.7 0.0 collective-permute-done.3.rest_0_
  42.7 1.9 %collective-permute-start.4 = (f16[2,784,128]{2,1,0:T(8,128)(2,1)S(1)}, f16[2,784,128]{2,1,0:T(8,128)(2,1)S(1)}, u32[]{:S(2)}, u32[]{:S(2)}) collective-permute-start(f16[2,784,128]{2,1,0:T(8,128)(2,1)S(1)} %convert_element_type.27), channel_id=1, source_target_pairs={{0,4},{1,21},{2,6},{3,23},{4,8},{5,1},{6,10},{7,3},{8,12},{9,5},{1... | collective-permute-start | bytes 1204232 | tf_op jit(solution)/shard_map/ppermute | solution.py:198
  44.7 0.8 stop_sums.4
  45.5 3.7 %collective-permute-start.5 = (bf16[2,84,512]{2,1,0:T(8,128)(2,1)S(1)}, bf16[2,84,512]{2,1,0:T(8,128)(2,1)S(1)}, u32[]{:S(2)}, u32[]{:S(2)}) collective-permute-start(bf16[2,84,512]{2,1,0:T(8,128)(2,1)S(1)} %get-tuple-element.24), channel_id=1, source_target_pairs={{0,2},{1,23},{2,4},{3,1},{4,6},{5,3},{6,8},{7,5},{8,10},{9,7},{10,... | collective-permute-start | bytes 516104 | tf_op jit(solution)/shard_map/ppermute | solution.py:198
  49.3 4.6 %collective-permute-start.6 = (bf16[2,84,512]{2,1,0:T(8,128)(2,1)S(1)}, bf16[2,84,512]{2,1,0:T(8,128)(2,1)S(1)}, u32[]{:S(2)}, u32[]{:S(2)}) collective-permute-start(bf16[2,84,512]{2,1,0:T(8,128)(2,1)S(1)} %get-tuple-element.25), channel_id=1, source_target_pairs={{0,3},{1,22},{2,5},{3,0},{4,7},{5,2},{6,9},{7,4},{8,11},{9,6},{10,... | collective-permute-start | bytes 516104 | tf_op jit(solution)/shard_map/ppermute | solution.py:198
  53.9 5.1 %collective-permute-done.4 = f16[2,784,128]{2,1,0:T(8,128)(2,1)S(1)} collective-permute-done((f16[2,784,128]{2,1,0:T(8,128)(2,1)S(1)}, f16[2,784,128]{2,1,0:T(8,128)(2,1)S(1)}, u32[]{:S(2)}, u32[]{:S(2)}) %collective-permute-start.4) | collective-permute-done | bytes 401440 | tf_op jit(solution)/shard_map/ppermute | solution.py:198
  59.0 0.1 slice_convert_fusion
  59.1 1.5 %fusion.11 = (f16[784,128]{1,0:T(8,128)(2,1)}, f16[784,128]{1,0:T(8,128)(2,1)}) fusion(f32[2,784,128]{2,1,0:T(8,128)S(1)} %stop_sums.4, f32[128]{0:T(128)S(1)} %bitcast.74, f32[128]{0:T(128)S(1)} %bitcast.73, f32[128]{0:T(128)S(1)} %get-tuple-element.41, f32[128]{0:T(128)S(1)} %get-tuple-element.31, f32[128]{0:T(128)S(1)} %get-tuple-element.56, ...), kind=kLoop, calls=%fused_computation.18 | loop fusion | flops 1806336 | bytes 1614128 | tf_op jit(solution)/shard_map/squeeze | solution.py:248
  60.6 0.3 collective-permute-done.5.rest_0_
  60.8 0.1 collective-permute-done.6.rest_1_
  61.0 0.0 copy-start
  61.0 0.7 copy-done
  61.7 2.4 %collective-permute-start.8 = (f16[784,128]{1,0:T(8,128)(2,1)}, f16[784,128]{1,0:T(8,128)(2,1)}, u32[]{:S(2)}, u32[]{:S(2)}) collective-permute-start(f16[784,128]{1,0:T(8,128)(2,1)} %get-tuple-element.27), channel_id=1, source_target_pairs={{0,5},{1,20},{2,7},{3,22},{4,9},{5,0},{6,11},{7,2},{8,13},{9,4},{1... | collective-permute-start | bytes 602120 | tf_op jit(solution)/shard_map/ppermute | solution.py:198
  64.0 5.0 %collective-permute-start.7 = (f16[784,128]{1,0:T(8,128)(2,1)}, f16[784,128]{1,0:T(8,128)(2,1)S(1)}, u32[]{:S(2)}, u32[]{:S(2)}) collective-permute-start(f16[784,128]{1,0:T(8,128)(2,1)} %get-tuple-element.26), channel_id=1, source_target_pairs={{0,4},{1,21},{2,6},{3,23},{4,8},{5,1},{6,10},{7,3},{8,12},{9,5},{1... | collective-permute-start | bytes 602120 | tf_op jit(solution)/shard_map/ppermute | solution.py:198
  69.0 0.0 copy-start.1
  69.0 0.9 copy-done.1
  69.9 0.7 stop_sums.5
  70.6 0.0 copy-start.2
  70.6 0.0 copy-start.3
  70.6 0.0 copy-start.4
  70.6 0.0 copy-start.5
  70.7 0.0 copy-start.6
  70.7 1.3 %collective-permute-done.8 = f16[784,128]{1,0:T(8,128)(2,1)} collective-permute-done((f16[784,128]{1,0:T(8,128)(2,1)}, f16[784,128]{1,0:T(8,128)(2,1)}, u32[]{:S(2)}, u32[]{:S(2)}) %collective-permute-start.8) | collective-permute-done | bytes 200736 | tf_op jit(solution)/shard_map/ppermute | solution.py:198
  72.0 1.0 convert_bitcast_fusion
  73.0 6.2 %collective-permute-done.7 = f16[784,128]{1,0:T(8,128)(2,1)S(1)} collective-permute-done((f16[784,128]{1,0:T(8,128)(2,1)}, f16[784,128]{1,0:T(8,128)(2,1)S(1)}, u32[]{:S(2)}, u32[]{:S(2)}) %collective-permute-start.7) | collective-permute-done | bytes 200736 | tf_op jit(solution)/shard_map/ppermute | solution.py:198
  79.2 1.2 fusion.3.sums
  80.4 30.2 %all-gather.3.cloned.1.call-done = bf16[1024,8,256]{2,1,0:T(8,128)(2,1)} async-done(((bf16[32,8,256]{2,1,0:T(8,128)(2,1)}), bf16[1024,8,256]{2,1,0:T(8,128)(2,1)}) %all-gather.3.cloned.1.call-update) | async-done | bytes 4194320 | tf_op jit(solution)/shard_map/all_gather | solution.py:219
  110.6 0.9 dynamic-slice_bitcast_fusion.amps_t
  111.5 0.0 copy-done.2
  111.5 0.0 copy-done.3
  111.5 0.0 copy-done.4
  111.5 0.0 copy-done.5
  111.6 0.0 copy-done.6
  111.6 1.8 %residual.1 = f32[256,256]{1,0:T(8,128)} custom-call(s32[2]{0:T(128)S(1)} %bitcast.68, s32[2]{0:T(128)S(1)} %bitcast.69, s32[2]{0:T(128)S(1)} %bitcast.70, f32[100]{0:T(128)S(1)} %copy-done.6, f32[12,128]{1,0:T(8,128)S(1)} %bitcast.67, f32[784,128]{1,0:T(8,128)S(1)} %fusion.3.sums, bf16[256,256]{1,0:T(8,128)(2,1)S(1)} %dynamic-slice_bitcast_fusion.amps_t), custom_call_target="tpu_custom_call" | custom-call | tf_op jit(solution)/shard_map/residual/pallas_call | solution.py:258
  (9 shorter events, 0.2 us)
Async XLA Ops:
  6.5 104.1 %all-gather.3.cloned.1.call-start = ((), (), s32[]{:S(2)}) async-start(), calls=%async_computation | async-start | bytes 4325376 | tf_op jit(solution)/shard_map/all_gather | solution.py:219
  9.6 4.6 %collective-permute-start = (bf16[12,84,512]{2,1,0:T(8,128)(2,1)S(1)}, bf16[12,84,512]{2,1,0:T(8,128)(2,1)S(1)}, u32[]{:S(2)}, u32[]{:S(2)}) collective-permute-start(bf16[12,84,512]{2,1,0:T(8,128)(2,1)S(1)} %split_cores.1), channel_id=1, source_target_pairs={{0,1},{1,0},{2,3},{3,2},{4,5},{5,4},{6,7},{7,6},{8,9},{9,8},{10,11... | collective-permute-start | bytes 3096584 | tf_op jit(solution)/shard_map/ppermute | solution.py:226
  14.3 27.4 %collective-permute-start.2 = (bf16[4,84,512]{2,1,0:T(8,128)(2,1)S(1)}, bf16[4,84,512]{2,1,0:T(8,128)(2,1)S(1)}, u32[]{:S(2)}, u32[]{:S(2)}) collective-permute-start(bf16[4,84,512]{2,1,0:T(8,128)(2,1)S(1)} %get-tuple-element.19), channel_id=1, source_target_pairs={{0,2},{1,23},{2,4},{3,1},{4,6},{5,3},{6,8},{7,5},{8,10},{9,7},{10,... | collective-permute-start | bytes 1032200 | tf_op jit(solution)/shard_map/ppermute | solution.py:198
  18.6 24.1 %collective-permute-start.3 = (bf16[4,84,512]{2,1,0:T(8,128)(2,1)S(1)}, bf16[4,84,512]{2,1,0:T(8,128)(2,1)S(1)}, u32[]{:S(2)}, u32[]{:S(2)}) collective-permute-start(bf16[4,84,512]{2,1,0:T(8,128)(2,1)S(1)} %pack_rows.4), channel_id=1, source_target_pairs={{0,2},{1,23},{2,4},{3,1},{4,6},{5,3},{6,8},{7,5},{8,10},{9,7},{10,... | collective-permute-start | bytes 1032200 | tf_op jit(solution)/shard_map/ppermute | solution.py:198
  22.9 18.7 %collective-permute-start.1 = (bf16[2,84,512]{2,1,0:T(8,128)(2,1)S(1)}, bf16[2,84,512]{2,1,0:T(8,128)(2,1)S(1)}, u32[]{:S(2)}, u32[]{:S(2)}) collective-permute-start(bf16[2,84,512]{2,1,0:T(8,128)(2,1)S(1)} %get-tuple-element.18), channel_id=1, source_target_pairs={{0,4},{1,21},{2,6},{3,23},{4,8},{5,1},{6,10},{7,3},{8,12},{9,5},{1... | collective-permute-start | bytes 516104 | tf_op jit(solution)/shard_map/ppermute | solution.py:198
  42.7 16.3 %collective-permute-start.4 = (f16[2,784,128]{2,1,0:T(8,128)(2,1)S(1)}, f16[2,784,128]{2,1,0:T(8,128)(2,1)S(1)}, u32[]{:S(2)}, u32[]{:S(2)}) collective-permute-start(f16[2,784,128]{2,1,0:T(8,128)(2,1)S(1)} %convert_element_type.27), channel_id=1, source_target_pairs={{0,4},{1,21},{2,6},{3,23},{4,8},{5,1},{6,10},{7,3},{8,12},{9,5},{1... | collective-permute-start | bytes 1204232 | tf_op jit(solution)/shard_map/ppermute | solution.py:198
  45.5 15.3 %collective-permute-start.5 = (bf16[2,84,512]{2,1,0:T(8,128)(2,1)S(1)}, bf16[2,84,512]{2,1,0:T(8,128)(2,1)S(1)}, u32[]{:S(2)}, u32[]{:S(2)}) collective-permute-start(bf16[2,84,512]{2,1,0:T(8,128)(2,1)S(1)} %get-tuple-element.24), channel_id=1, source_target_pairs={{0,2},{1,23},{2,4},{3,1},{4,6},{5,3},{6,8},{7,5},{8,10},{9,7},{10,... | collective-permute-start | bytes 516104 | tf_op jit(solution)/shard_map/ppermute | solution.py:198
  49.3 11.7 %collective-permute-start.6 = (bf16[2,84,512]{2,1,0:T(8,128)(2,1)S(1)}, bf16[2,84,512]{2,1,0:T(8,128)(2,1)S(1)}, u32[]{:S(2)}, u32[]{:S(2)}) collective-permute-start(bf16[2,84,512]{2,1,0:T(8,128)(2,1)S(1)} %get-tuple-element.25), channel_id=1, source_target_pairs={{0,3},{1,22},{2,5},{3,0},{4,7},{5,2},{6,9},{7,4},{8,11},{9,6},{10,... | collective-permute-start | bytes 516104 | tf_op jit(solution)/shard_map/ppermute | solution.py:198
  61.0 0.7 copy-start
  61.7 10.4 %collective-permute-start.8 = (f16[784,128]{1,0:T(8,128)(2,1)}, f16[784,128]{1,0:T(8,128)(2,1)}, u32[]{:S(2)}, u32[]{:S(2)}) collective-permute-start(f16[784,128]{1,0:T(8,128)(2,1)} %get-tuple-element.27), channel_id=1, source_target_pairs={{0,5},{1,20},{2,7},{3,22},{4,9},{5,0},{6,11},{7,2},{8,13},{9,4},{1... | collective-permute-start | bytes 602120 | tf_op jit(solution)/shard_map/ppermute | solution.py:198
  64.0 15.1 %collective-permute-start.7 = (f16[784,128]{1,0:T(8,128)(2,1)}, f16[784,128]{1,0:T(8,128)(2,1)S(1)}, u32[]{:S(2)}, u32[]{:S(2)}) collective-permute-start(f16[784,128]{1,0:T(8,128)(2,1)} %get-tuple-element.26), channel_id=1, source_target_pairs={{0,4},{1,21},{2,6},{3,23},{4,8},{5,1},{6,10},{7,3},{8,12},{9,5},{1... | collective-permute-start | bytes 602120 | tf_op jit(solution)/shard_map/ppermute | solution.py:198
  69.0 0.9 copy-start.1
  70.6 40.9 %copy-start.2 = (f32[1536]{0:T(1024)S(1)}, f32[1536]{0:T(1024)}, u32[]{:S(2)}) copy-start(f32[1536]{0:T(1024)} %param.12) | copy-start | bytes 18436
  70.6 40.9 %copy-start.3 = (s32[1,1,2]{2,1,0:T(1,128)S(1)}, s32[1,1,2]{2,1,0:T(1,128)}, u32[]{:S(2)}) copy-start(s32[1,1,2]{2,1,0:T(1,128)} %param.9) | copy-start | bytes 28
  70.6 40.9 %copy-start.4 = (s32[1,1,2]{2,1,0:T(1,128)S(1)}, s32[1,1,2]{2,1,0:T(1,128)}, u32[]{:S(2)}) copy-start(s32[1,1,2]{2,1,0:T(1,128)} %param.10) | copy-start | bytes 28
  70.6 40.9 %copy-start.5 = (s32[1,1,2]{2,1,0:T(1,128)S(1)}, s32[1,1,2]{2,1,0:T(1,128)}, u32[]{:S(2)}) copy-start(s32[1,1,2]{2,1,0:T(1,128)} %param.11) | copy-start | bytes 28
  70.7 40.9 %copy-start.6 = (f32[100]{0:T(128)S(1)}, f32[100]{0:T(128)}, u32[]{:S(2)}) copy-start(f32[100]{0:T(128)} %occ.1) | copy-start | bytes 1204
Sparse Core Ops, SparseCore 0:
  11.1 99.4 all-gather.2

commit v5 on v4

--- a/solution.py
+++ b/solution.py
@@ -216,8 +216,6 @@
     def pairs_at(d):
         return [(d, True)] if d == far else [(d, True), (d, False)]
 
-    owned = lax.all_gather(jnp.swapaxes(amplitudes[0], 1, 2), "pair")
-    owned = lax.dynamic_index_in_dim(owned, lax.axis_index("pair"), 1, keepdims=False)
 
     ints = integrals[:, 0]
     (other,) = call(
@@ -230,13 +228,13 @@
     to_owner = list(range(SECOND - 1, 0, -1))
     sends = pack([pairs_at(d) for d in to_first], other)
     first_rows = [permute(x, d - FIRST) for d, x in zip(to_first, sends)]
-    gate = lax.optimization_barrier((other, *sends))[0]
+    owned = lax.all_to_all(amplitudes, "pair", split_axis=1, concat_axis=3, tiled=True)
+    gate, owned, *first_rows = lax.optimization_barrier((other, owned, *first_rows))
     sends = pack([pairs_at(d) for d in to_second], gate)
     second_rows = [permute(x, d - SECOND) for d, x in zip(to_second, sends)]
 
     picks = [((0, None) if d == far else (0, 2), at) for at, d in enumerate(to_first)]
     x = stop_sums(FIRST, (True, False), picks, True, other, first_rows).astype(F16)
-    x, *second_rows = lax.optimization_barrier((x, *second_rows))
     moving = permute(x, FIRST - SECOND)
 
     gate = lax.optimization_barrier((other, x))[0]
@@ -253,7 +251,7 @@
     picks = [((0,), at) for at in range(len(owner_rows))]
     local = stop_sums(0, (True,), picks, False, gate, owner_rows)
     sums = (decode(moving[0][None])[0] + decode(moving[1][None])[0] + local)[0]
-    amps_t = owned.reshape(2 * TILE, 2 * TILE)
+    amps_t = jnp.swapaxes(owned[0, 0], 0, 1)
 
     (out,) = call(final_kernel, 3, [((2 * TILE, 2 * TILE), F32)], "residual", 4)(
         pair_occ.reshape(-1),

time: 121 us -> 85.7 us (0.71)
  the two profiles are of different devices: /device:TPU:8 before, /device:TPU:1 now
where the time goes in v5:
time: 85.7 us; the launch traced here: 85.2 us
  starting transfers between devices  49 us (57%)
  waiting for transfers between devices  25.6 us (30%)
  Pallas kernels  6.21 us (7%)
  local copies, waits for them, and re-layouts  2.95 us (3%)
  other arithmetic  1.24 us (1%)
    ppermute x8, starting transfers between devices, permute(): return lax.ppermute(x, 'aux', pairs)  26.9 us
    ppermute x8, waiting for transfers between devices, permute(): return lax.ppermute(x, 'aux', pairs)  16.1 us
    ppermute x1, starting transfers between devices, on_device(): other = lax.ppermute(other, 'aux', [(i, i ^ 1) for i in range(2 * chips)])  12.4 us
    all_to_all x1, starting transfers between devices, on_device(): lax.all_to_all(amplitudes, 'pair', split_axis=1, concat_axis=3, tiled=True)  9.68 us
    all_to_all x1, waiting for transfers between devices, on_device(): lax.all_to_all(amplitudes, 'pair', split_axis=1, concat_axis=3, tiled=True)  7.17 us
    pallas_call x3, Pallas kernels, stop_sums(): call(functools.partial(stop_kernel, chips, stop, owners, picks, scaled),...  3.49 us
    unnamed x13, local copies, waits for them, and re-layouts  2.95 us
    ppermute x1, waiting for transfers between devices, on_device(): other = lax.ppermute(other, 'aux', [(i, i ^ 1) for i in range(2 * chips)])  2.31 us
  transfers between devices with their start and end apart: 10, of which 6 were waited for; matrix products, arithmetic and copies ran while one was open for 1% of the time, Pallas kernels for 2%

profile of v5, /device:TPU:1, one launch (start us, length us, event | category | flops | bytes accessed | tf_op | source)
XLA Modules:
  0.0 85.2 jit_solution(11384190581171626929)
XLA Ops:
  0.0 2.3 %copy.12 = bf16[24,1,84,512]{3,2,0,1:T(8,128)(2,1)S(1)} copy(bf16[24,1,84,512]{3,0,2,1:T(8,128)(2,1)} %param.8) | data formatting | bytes 4128768 | tf_op args[1]
  2.3 0.1 split_cores.1
  2.4 12.4 %collective-permute-start = (bf16[12,84,512]{2,1,0:T(8,128)(2,1)S(1)}, bf16[12,84,512]{2,1,0:T(8,128)(2,1)S(1)}, u32[]{:S(2)}, u32[]{:S(2)}) collective-permute-start(bf16[12,84,512]{2,1,0:T(8,128)(2,1)S(1)} %split_cores.1), channel_id=1, source_target_pairs={{0,1},{1,0},{2,3},{3,2},{4,5},{5,4},{6,7},{7,6},{8,9},{9,8},{10,11... | collective-permute-start | bytes 3096584 | tf_op jit(solution)/shard_map/ppermute | solution.py:224
  14.8 2.3 %collective-permute-done.other = bf16[12,84,512]{2,1,0:T(8,128)(2,1)S(1)} collective-permute-done((bf16[12,84,512]{2,1,0:T(8,128)(2,1)S(1)}, bf16[12,84,512]{2,1,0:T(8,128)(2,1)S(1)}, u32[]{:S(2)}, u32[]{:S(2)}) %collective-permute-start) | collective-permute-done | bytes 1032224 | tf_op jit(solution)/shard_map/ppermute | solution.py:224
  17.1 0.8 pack_rows.3
  17.9 0.0 copy-start.5
  17.9 0.7 copy-done.5
  18.6 5.3 %collective-permute-start.2 = (bf16[4,84,512]{2,1,0:T(8,128)(2,1)}, bf16[4,84,512]{2,1,0:T(8,128)(2,1)}, u32[]{:S(2)}, u32[]{:S(2)}) collective-permute-start(bf16[4,84,512]{2,1,0:T(8,128)(2,1)} %get-tuple-element.20), channel_id=1, source_target_pairs={{0,2},{1,23},{2,4},{3,1},{4,6},{5,3},{6,8},{7,5},{8,10},{9,7},{10,... | collective-permute-start | bytes 1032200 | tf_op jit(solution)/shard_map/ppermute | solution.py:198
  23.9 9.7 %all-to-all-start = ((bf16[1,32,256,8]{2,3,0,1:T(8,128)(2,1)}), bf16[1,32,256,8]{2,3,0,1:T(8,128)(2,1)S(1)}, u32[]{:S(2)}, u32[]{:S(2)}) async-start(bf16[1,32,256,8]{2,3,0,1:T(8,128)(2,1)} %bitcast.5), calls=%async_computation | async-start | bytes 262144 | tf_op jit(solution)/shard_map/all_to_all | solution.py:231
  33.6 2.2 %collective-permute-start.1 = (bf16[2,84,512]{2,1,0:T(8,128)(2,1)}, bf16[2,84,512]{2,1,0:T(8,128)(2,1)S(1)}, u32[]{:S(2)}, u32[]{:S(2)}) collective-permute-start(bf16[2,84,512]{2,1,0:T(8,128)(2,1)} %copy-done.5), channel_id=1, source_target_pairs={{0,4},{1,21},{2,6},{3,23},{4,8},{5,1},{6,10},{7,3},{8,12},{9,5},{1... | collective-permute-start | bytes 516104 | tf_op jit(solution)/shard_map/ppermute | solution.py:198
  35.7 7.2 %all-to-all-done = bf16[1,32,256,8]{2,3,0,1:T(8,128)(2,1)S(1)} async-done(((bf16[1,32,256,8]{2,3,0,1:T(8,128)(2,1)}), bf16[1,32,256,8]{2,3,0,1:T(8,128)(2,1)S(1)}, u32[]{:S(2)}, u32[]{:S(2)}) %all-to-all-start) | async-done | bytes 131104 | tf_op jit(solution)/shard_map/all_to_all | solution.py:231
  42.9 0.0 collective-permute-done.1.rest_0_
  42.9 0.0 collective-permute-done.2.rest_1_
  42.9 2.0 %stop_sums.3 = f32[2,784,128]{2,1,0:T(8,128)S(1)} custom-call(bf16[24,84,512]{2,1,0:T(8,128)(2,1)S(1)} %bitcast.63, bf16[12,84,512]{2,1,0:T(8,128)(2,1)S(1)} %collective-permute-done.other, bf16[2,84,512]{2,1,0:T(8,128)(2,1)S(1)} %collective-permute-done.1.rest_0_, bf16[4,84,512]{2,1,0:T(8,128)(2,1)} %collective-permute-done.2.rest_1_), custom_call_target="tpu_custom_call" | custom-call | tf_op jit(solution)/shard_map/stop_sums/pallas_call | solution.py:209
  44.9 0.1 convert_element_type.27
  45.0 2.6 %collective-permute-start.3 = (f16[2,784,128]{2,1,0:T(8,128)(2,1)S(1)}, f16[2,784,128]{2,1,0:T(8,128)(2,1)S(1)}, u32[]{:S(2)}, u32[]{:S(2)}) collective-permute-start(f16[2,784,128]{2,1,0:T(8,128)(2,1)S(1)} %convert_element_type.27), channel_id=1, source_target_pairs={{0,4},{1,21},{2,6},{3,23},{4,8},{5,1},{6,10},{7,3},{8,12},{9,5},{1... | collective-permute-start | bytes 1204232 | tf_op jit(solution)/shard_map/ppermute | solution.py:198
  47.7 2.9 %collective-permute-start.4 = (bf16[4,84,512]{2,1,0:T(8,128)(2,1)S(1)}, bf16[4,84,512]{2,1,0:T(8,128)(2,1)S(1)}, u32[]{:S(2)}, u32[]{:S(2)}) collective-permute-start(bf16[4,84,512]{2,1,0:T(8,128)(2,1)S(1)} %pack_rows.4), channel_id=1, source_target_pairs={{0,2},{1,23},{2,4},{3,1},{4,6},{5,3},{6,8},{7,5},{8,10},{9,7},{10,... | collective-permute-start | bytes 1032200 | tf_op jit(solution)/shard_map/ppermute | solution.py:198
  50.7 2.2 %collective-permute-start.5 = (bf16[2,84,512]{2,1,0:T(8,128)(2,1)S(1)}, bf16[2,84,512]{2,1,0:T(8,128)(2,1)S(1)}, u32[]{:S(2)}, u32[]{:S(2)}) collective-permute-start(bf16[2,84,512]{2,1,0:T(8,128)(2,1)S(1)} %get-tuple-element.25), channel_id=1, source_target_pairs={{0,2},{1,23},{2,4},{3,1},{4,6},{5,3},{6,8},{7,5},{8,10},{9,7},{10,... | collective-permute-start | bytes 516104 | tf_op jit(solution)/shard_map/ppermute | solution.py:198
  52.9 3.0 %collective-permute-start.6 = (bf16[2,84,512]{2,1,0:T(8,128)(2,1)S(1)}, bf16[2,84,512]{2,1,0:T(8,128)(2,1)S(1)}, u32[]{:S(2)}, u32[]{:S(2)}) collective-permute-start(bf16[2,84,512]{2,1,0:T(8,128)(2,1)S(1)} %get-tuple-element.26), channel_id=1, source_target_pairs={{0,3},{1,22},{2,5},{3,0},{4,7},{5,2},{6,9},{7,4},{8,11},{9,6},{10,... | collective-permute-start | bytes 516104 | tf_op jit(solution)/shard_map/ppermute | solution.py:198
  55.9 7.6 %collective-permute-done.4.rest_0_ = bf16[4,84,512]{2,1,0:T(8,128)(2,1)S(1)} collective-permute-done((bf16[4,84,512]{2,1,0:T(8,128)(2,1)S(1)}, bf16[4,84,512]{2,1,0:T(8,128)(2,1)S(1)}, u32[]{:S(2)}, u32[]{:S(2)}) %collective-permute-start.4) | collective-permute-done | bytes 344096 | tf_op jit(solution)/shard_map/ppermute | solution.py:198
  63.5 0.8 stop_sums.4
  64.3 0.0 collective-permute-done.3
  64.3 0.1 slice_convert_fusion
  64.4 0.8 fusion.11
  65.2 0.0 collective-permute-done.5.rest_0_
  65.2 1.4 %collective-permute-done.6.rest_1_ = bf16[2,84,512]{2,1,0:T(8,128)(2,1)S(1)} collective-permute-done((bf16[2,84,512]{2,1,0:T(8,128)(2,1)S(1)}, bf16[2,84,512]{2,1,0:T(8,128)(2,1)S(1)}, u32[]{:S(2)}, u32[]{:S(2)}) %collective-permute-start.6) | collective-permute-done | bytes 172064 | tf_op jit(solution)/shard_map/ppermute | solution.py:198
  66.6 4.6 %collective-permute-start.7 = (f16[784,128]{1,0:T(8,128)(2,1)S(1)}, f16[784,128]{1,0:T(8,128)(2,1)S(1)}, u32[]{:S(2)}, u32[]{:S(2)}) collective-permute-start(f16[784,128]{1,0:T(8,128)(2,1)S(1)} %get-tuple-element.27), channel_id=1, source_target_pairs={{0,4},{1,21},{2,6},{3,23},{4,8},{5,1},{6,10},{7,3},{8,12},{9,5},{1... | collective-permute-start | bytes 602120 | tf_op jit(solution)/shard_map/ppermute | solution.py:198
  71.2 4.1 %collective-permute-start.8 = (f16[784,128]{1,0:T(8,128)(2,1)S(1)}, f16[784,128]{1,0:T(8,128)(2,1)S(1)}, u32[]{:S(2)}, u32[]{:S(2)}) collective-permute-start(f16[784,128]{1,0:T(8,128)(2,1)S(1)} %get-tuple-element.28), channel_id=1, source_target_pairs={{0,5},{1,20},{2,7},{3,22},{4,9},{5,0},{6,11},{7,2},{8,13},{9,4},{1... | collective-permute-start | bytes 602120 | tf_op jit(solution)/shard_map/ppermute | solution.py:198
  75.3 0.7 stop_sums.5
  76.0 0.0 copy-start
  76.0 0.0 copy-start.1
  76.0 0.0 copy-start.2
  76.0 0.0 copy-start.3
  76.0 0.0 copy-start.4
  76.0 0.5 collective-permute-done.7
  76.5 6.6 %collective-permute-done.8 = f16[784,128]{1,0:T(8,128)(2,1)S(1)} collective-permute-done((f16[784,128]{1,0:T(8,128)(2,1)S(1)}, f16[784,128]{1,0:T(8,128)(2,1)S(1)}, u32[]{:S(2)}, u32[]{:S(2)}) %collective-permute-start.8) | collective-permute-done | bytes 200736 | tf_op jit(solution)/shard_map/ppermute | solution.py:198
  83.2 0.2 fusion.3.sums
  83.4 0.0 copy-done
  83.4 0.0 copy-done.1
  83.4 0.0 copy-done.2
  83.4 0.0 copy-done.3
  83.4 0.0 copy-done.4
  83.4 1.8 %residual.1 = f32[256,256]{1,0:T(8,128)} custom-call(s32[2]{0:T(128)S(1)} %bitcast.70, s32[2]{0:T(128)S(1)} %bitcast.71, s32[2]{0:T(128)S(1)} %bitcast.72, f32[100]{0:T(128)S(1)} %copy-done.4, f32[12,128]{1,0:T(8,128)S(1)} %bitcast.69, f32[784,128]{1,0:T(8,128)S(1)} %fusion.3.sums, bf16[256,256]{1,0:T(8,128)(2,1)S(1)} %bitcast.68), custom_call_target="tpu_custom_call" | custom-call | tf_op jit(solution)/shard_map/residual/pallas_call | solution.py:256
  (9 shorter events, 0.2 us)
Async XLA Ops:
  2.4 14.7 %collective-permute-start = (bf16[12,84,512]{2,1,0:T(8,128)(2,1)S(1)}, bf16[12,84,512]{2,1,0:T(8,128)(2,1)S(1)}, u32[]{:S(2)}, u32[]{:S(2)}) collective-permute-start(bf16[12,84,512]{2,1,0:T(8,128)(2,1)S(1)} %split_cores.1), channel_id=1, source_target_pairs={{0,1},{1,0},{2,3},{3,2},{4,5},{5,4},{6,7},{7,6},{8,9},{9,8},{10,11... | collective-permute-start | bytes 3096584 | tf_op jit(solution)/shard_map/ppermute | solution.py:224
  17.9 0.7 copy-start.5
  18.6 24.3 %collective-permute-start.2 = (bf16[4,84,512]{2,1,0:T(8,128)(2,1)}, bf16[4,84,512]{2,1,0:T(8,128)(2,1)}, u32[]{:S(2)}, u32[]{:S(2)}) collective-permute-start(bf16[4,84,512]{2,1,0:T(8,128)(2,1)} %get-tuple-element.20), channel_id=1, source_target_pairs={{0,2},{1,23},{2,4},{3,1},{4,6},{5,3},{6,8},{7,5},{8,10},{9,7},{10,... | collective-permute-start | bytes 1032200 | tf_op jit(solution)/shard_map/ppermute | solution.py:198
  23.9 19.0 %all-to-all-start = ((bf16[1,32,256,8]{2,3,0,1:T(8,128)(2,1)}), bf16[1,32,256,8]{2,3,0,1:T(8,128)(2,1)S(1)}, u32[]{:S(2)}, u32[]{:S(2)}) async-start(bf16[1,32,256,8]{2,3,0,1:T(8,128)(2,1)} %bitcast.5), calls=%async_computation | async-start | bytes 262144 | tf_op jit(solution)/shard_map/all_to_all | solution.py:231
  33.6 9.3 %collective-permute-start.1 = (bf16[2,84,512]{2,1,0:T(8,128)(2,1)}, bf16[2,84,512]{2,1,0:T(8,128)(2,1)S(1)}, u32[]{:S(2)}, u32[]{:S(2)}) collective-permute-start(bf16[2,84,512]{2,1,0:T(8,128)(2,1)} %copy-done.5), channel_id=1, source_target_pairs={{0,4},{1,21},{2,6},{3,23},{4,8},{5,1},{6,10},{7,3},{8,12},{9,5},{1... | collective-permute-start | bytes 516104 | tf_op jit(solution)/shard_map/ppermute | solution.py:198
  45.0 19.3 %collective-permute-start.3 = (f16[2,784,128]{2,1,0:T(8,128)(2,1)S(1)}, f16[2,784,128]{2,1,0:T(8,128)(2,1)S(1)}, u32[]{:S(2)}, u32[]{:S(2)}) collective-permute-start(f16[2,784,128]{2,1,0:T(8,128)(2,1)S(1)} %convert_element_type.27), channel_id=1, source_target_pairs={{0,4},{1,21},{2,6},{3,23},{4,8},{5,1},{6,10},{7,3},{8,12},{9,5},{1... | collective-permute-start | bytes 1204232 | tf_op jit(solution)/shard_map/ppermute | solution.py:198
  47.7 15.8 %collective-permute-start.4 = (bf16[4,84,512]{2,1,0:T(8,128)(2,1)S(1)}, bf16[4,84,512]{2,1,0:T(8,128)(2,1)S(1)}, u32[]{:S(2)}, u32[]{:S(2)}) collective-permute-start(bf16[4,84,512]{2,1,0:T(8,128)(2,1)S(1)} %pack_rows.4), channel_id=1, source_target_pairs={{0,2},{1,23},{2,4},{3,1},{4,6},{5,3},{6,8},{7,5},{8,10},{9,7},{10,... | collective-permute-start | bytes 1032200 | tf_op jit(solution)/shard_map/ppermute | solution.py:198
  50.7 14.5 %collective-permute-start.5 = (bf16[2,84,512]{2,1,0:T(8,128)(2,1)S(1)}, bf16[2,84,512]{2,1,0:T(8,128)(2,1)S(1)}, u32[]{:S(2)}, u32[]{:S(2)}) collective-permute-start(bf16[2,84,512]{2,1,0:T(8,128)(2,1)S(1)} %get-tuple-element.25), channel_id=1, source_target_pairs={{0,2},{1,23},{2,4},{3,1},{4,6},{5,3},{6,8},{7,5},{8,10},{9,7},{10,... | collective-permute-start | bytes 516104 | tf_op jit(solution)/shard_map/ppermute | solution.py:198
  52.9 13.8 %collective-permute-start.6 = (bf16[2,84,512]{2,1,0:T(8,128)(2,1)S(1)}, bf16[2,84,512]{2,1,0:T(8,128)(2,1)S(1)}, u32[]{:S(2)}, u32[]{:S(2)}) collective-permute-start(bf16[2,84,512]{2,1,0:T(8,128)(2,1)S(1)} %get-tuple-element.26), channel_id=1, source_target_pairs={{0,3},{1,22},{2,5},{3,0},{4,7},{5,2},{6,9},{7,4},{8,11},{9,6},{10,... | collective-permute-start | bytes 516104 | tf_op jit(solution)/shard_map/ppermute | solution.py:198
  66.6 9.8 %collective-permute-start.7 = (f16[784,128]{1,0:T(8,128)(2,1)S(1)}, f16[784,128]{1,0:T(8,128)(2,1)S(1)}, u32[]{:S(2)}, u32[]{:S(2)}) collective-permute-start(f16[784,128]{1,0:T(8,128)(2,1)S(1)} %get-tuple-element.27), channel_id=1, source_target_pairs={{0,4},{1,21},{2,6},{3,23},{4,8},{5,1},{6,10},{7,3},{8,12},{9,5},{1... | collective-permute-start | bytes 602120 | tf_op jit(solution)/shard_map/ppermute | solution.py:198
  71.2 11.9 %collective-permute-start.8 = (f16[784,128]{1,0:T(8,128)(2,1)S(1)}, f16[784,128]{1,0:T(8,128)(2,1)S(1)}, u32[]{:S(2)}, u32[]{:S(2)}) collective-permute-start(f16[784,128]{1,0:T(8,128)(2,1)S(1)} %get-tuple-element.28), channel_id=1, source_target_pairs={{0,5},{1,20},{2,7},{3,22},{4,9},{5,0},{6,11},{7,2},{8,13},{9,4},{1... | collective-permute-start | bytes 602120 | tf_op jit(solution)/shard_map/ppermute | solution.py:198
  76.0 7.4 %copy-start = (f32[1536]{0:T(1024)S(1)}, f32[1536]{0:T(1024)}, u32[]{:S(2)}) copy-start(f32[1536]{0:T(1024)} %param.12) | copy-start | bytes 18436
  76.0 7.4 %copy-start.1 = (s32[1,1,2]{2,1,0:T(1,128)S(1)}, s32[1,1,2]{2,1,0:T(1,128)}, u32[]{:S(2)}) copy-start(s32[1,1,2]{2,1,0:T(1,128)} %param.9) | copy-start | bytes 28
  76.0 7.4 %copy-start.2 = (s32[1,1,2]{2,1,0:T(1,128)S(1)}, s32[1,1,2]{2,1,0:T(1,128)}, u32[]{:S(2)}) copy-start(s32[1,1,2]{2,1,0:T(1,128)} %param.10) | copy-start | bytes 28
  76.0 7.4 %copy-start.3 = (s32[1,1,2]{2,1,0:T(1,128)S(1)}, s32[1,1,2]{2,1,0:T(1,128)}, u32[]{:S(2)}) copy-start(s32[1,1,2]{2,1,0:T(1,128)} %param.11) | copy-start | bytes 28
  76.0 7.4 %copy-start.4 = (f32[100]{0:T(128)S(1)}, f32[100]{0:T(128)}, u32[]{:S(2)}) copy-start(f32[100]{0:T(128)} %occ.1) | copy-start | bytes 1204

commit v6 on v5

--- a/solution.py
+++ b/solution.py
@@ -228,13 +228,15 @@
     to_owner = list(range(SECOND - 1, 0, -1))
     sends = pack([pairs_at(d) for d in to_first], other)
     first_rows = [permute(x, d - FIRST) for d, x in zip(to_first, sends)]
-    owned = lax.all_to_all(amplitudes, "pair", split_axis=1, concat_axis=3, tiled=True)
-    gate, owned, *first_rows = lax.optimization_barrier((other, owned, *first_rows))
+    gate = lax.optimization_barrier((other, *sends))[0]
     sends = pack([pairs_at(d) for d in to_second], gate)
     second_rows = [permute(x, d - SECOND) for d, x in zip(to_second, sends)]
+    amplitudes, first_rows[0] = lax.optimization_barrier((amplitudes, first_rows[0]))
+    owned = lax.all_to_all(amplitudes, "pair", split_axis=1, concat_axis=3, tiled=True)
 
     picks = [((0, None) if d == far else (0, 2), at) for at, d in enumerate(to_first)]
     x = stop_sums(FIRST, (True, False), picks, True, other, first_rows).astype(F16)
+    x, *second_rows = lax.optimization_barrier((x, *second_rows))
     moving = permute(x, FIRST - SECOND)
 
     gate = lax.optimization_barrier((other, x))[0]
@@ -242,6 +244,7 @@
     ways = [(d, n == 1) for d in to_owner for n in range(2)]
     owner_rows = [permute(x, *way) for way, x in zip(ways, sends)]
     picks = [((0, 2), at) for at in range(len(to_second))]
+    gate, owned = lax.optimization_barrier((gate, owned))
     local = stop_sums(SECOND, (True, False), picks, False, gate, second_rows)
     last = [add_on(moving[n : n + 1], local[n : n + 1])[0] for n in range(2)]
     *last, owner_rows = lax.optimization_barrier((*last, owner_rows))

time: 85.7 us -> 83.4 us (0.973)
  waiting for transfers between devices: 25.6 us -> 17 us
  other arithmetic: 1.24 us -> 5.1 us
  local copies, waits for them, and re-layouts: 2.95 us -> 4.04 us
    all_to_all x1, waiting for transfers between devices: 7.17 us -> 1.92 us  [on_device(): lax.all_to_all(amplitudes, 'pair', split_axis=1, concat_axis=3, tiled=True)]
    ppermute x8, waiting for transfers between devices: 16.1 us -> 12.8 us  [permute(): return lax.ppermute(x, 'aux', pairs)]
    unnamed x13 -> x21, local copies, waits for them, and re-layouts: 2.95 us -> 4.04 us
    convert_element_type x3, other arithmetic: 0.11 us -> 1.14 us  [decode(): x = x.astype(F32)]
    squeeze x1, other arithmetic: 0.79 us -> 1.71 us  [on_device(): last = [add_on(moving[n:n + 1], local[n:n + 1])[0] for n in range(2)]]
    ppermute x8, starting transfers between devices: 26.9 us -> 27.7 us  [permute(): return lax.ppermute(x, 'aux', pairs)]
  transfers between devices with their start and end apart: 10 -> 10, of which waited for: 6 -> 5; matrix products, arithmetic and copies ran while one was open for 1% -> 6% of each run, Pallas kernels for 2% -> 5%
where the time goes in v6:
time: 83.4 us; the launch traced here: 82.4 us
  starting transfers between devices  49.8 us (60%)
  waiting for transfers between devices  17 us (20%)
  Pallas kernels  6.12 us (7%)
  other arithmetic  5.1 us (6%)
  local copies, waits for them, and re-layouts  4.04 us (5%)
    ppermute x8, starting transfers between devices, permute(): return lax.ppermute(x, 'aux', pairs)  27.7 us
    ppermute x8, waiting for transfers between devices, permute(): return lax.ppermute(x, 'aux', pairs)  12.8 us
    ppermute x1, starting transfers between devices, on_device(): other = lax.ppermute(other, 'aux', [(i, i ^ 1) for i in range(2 * chips)])  12.4 us
    all_to_all x1, starting transfers between devices, on_device(): lax.all_to_all(amplitudes, 'pair', split_axis=1, concat_axis=3, tiled=True)  9.68 us
    unnamed x21, local copies, waits for them, and re-layouts  4.04 us
    pallas_call x3, Pallas kernels, stop_sums(): call(functools.partial(stop_kernel, chips, stop, owners, picks, scaled),...  3.42 us
    ppermute x1, waiting for transfers between devices, on_device(): other = lax.ppermute(other, 'aux', [(i, i ^ 1) for i in range(2 * chips)])  2.31 us
    all_to_all x1, waiting for transfers between devices, on_device(): lax.all_to_all(amplitudes, 'pair', split_axis=1, concat_axis=3, tiled=True)  1.92 us
  transfers between devices with their start and end apart: 10, of which 5 were waited for; matrix products, arithmetic and copies ran while one was open for 6% of the time, Pallas kernels for 5%

profile of v6, /device:TPU:1, one launch (start us, length us, event | category | flops | bytes accessed | tf_op | source)
XLA Modules:
  0.0 82.4 jit_solution(16428613948980437614)
XLA Ops:
  0.0 2.3 %copy.12 = bf16[24,1,84,512]{3,2,0,1:T(8,128)(2,1)S(1)} copy(bf16[24,1,84,512]{3,0,2,1:T(8,128)(2,1)} %param.8) | data formatting | bytes 4128768 | tf_op args[1]
  2.3 0.1 split_cores.1
  2.4 12.4 %collective-permute-start = (bf16[12,84,512]{2,1,0:T(8,128)(2,1)S(1)}, bf16[12,84,512]{2,1,0:T(8,128)(2,1)S(1)}, u32[]{:S(2)}, u32[]{:S(2)}) collective-permute-start(bf16[12,84,512]{2,1,0:T(8,128)(2,1)S(1)} %split_cores.1), channel_id=1, source_target_pairs={{0,1},{1,0},{2,3},{3,2},{4,5},{5,4},{6,7},{7,6},{8,9},{9,8},{10,11... | collective-permute-start | bytes 3096584 | tf_op jit(solution)/shard_map/ppermute | solution.py:224
  14.8 2.3 %collective-permute-done.other = bf16[12,84,512]{2,1,0:T(8,128)(2,1)S(1)} collective-permute-done((bf16[12,84,512]{2,1,0:T(8,128)(2,1)S(1)}, bf16[12,84,512]{2,1,0:T(8,128)(2,1)S(1)}, u32[]{:S(2)}, u32[]{:S(2)}) %collective-permute-start) | collective-permute-done | bytes 1032224 | tf_op jit(solution)/shard_map/ppermute | solution.py:224
  17.2 5.3 %collective-permute-start.2 = (bf16[4,84,512]{2,1,0:T(8,128)(2,1)S(1)}, bf16[4,84,512]{2,1,0:T(8,128)(2,1)S(1)}, u32[]{:S(2)}, u32[]{:S(2)}) collective-permute-start(bf16[4,84,512]{2,1,0:T(8,128)(2,1)S(1)} %get-tuple-element.24), channel_id=1, source_target_pairs={{0,2},{1,23},{2,4},{3,1},{4,6},{5,3},{6,8},{7,5},{8,10},{9,7},{10,... | collective-permute-start | bytes 1032200 | tf_op jit(solution)/shard_map/ppermute | solution.py:198
  22.5 2.2 %collective-permute-start.3 = (bf16[4,84,512]{2,1,0:T(8,128)(2,1)S(1)}, bf16[4,84,512]{2,1,0:T(8,128)(2,1)S(1)}, u32[]{:S(2)}, u32[]{:S(2)}) collective-permute-start(bf16[4,84,512]{2,1,0:T(8,128)(2,1)S(1)} %pack_rows.4), channel_id=1, source_target_pairs={{0,2},{1,23},{2,4},{3,1},{4,6},{5,3},{6,8},{7,5},{8,10},{9,7},{10,... | collective-permute-start | bytes 1032200 | tf_op jit(solution)/shard_map/ppermute | solution.py:198
  24.7 2.2 %collective-permute-start.1 = (bf16[2,84,512]{2,1,0:T(8,128)(2,1)S(1)}, bf16[2,84,512]{2,1,0:T(8,128)(2,1)S(1)}, u32[]{:S(2)}, u32[]{:S(2)}) collective-permute-start(bf16[2,84,512]{2,1,0:T(8,128)(2,1)S(1)} %get-tuple-element.22), channel_id=1, source_target_pairs={{0,4},{1,21},{2,6},{3,23},{4,8},{5,1},{6,10},{7,3},{8,12},{9,5},{1... | collective-permute-start | bytes 516104 | tf_op jit(solution)/shard_map/ppermute | solution.py:198
  26.9 7.7 %collective-permute-done.1.rest_0_ = bf16[2,84,512]{2,1,0:T(8,128)(2,1)S(1)} collective-permute-done((bf16[2,84,512]{2,1,0:T(8,128)(2,1)S(1)}, bf16[2,84,512]{2,1,0:T(8,128)(2,1)S(1)}, u32[]{:S(2)}, u32[]{:S(2)}) %collective-permute-start.1) | collective-permute-done | bytes 172064 | tf_op jit(solution)/shard_map/ppermute | solution.py:198
  34.5 0.0 collective-permute-done.2.rest_1_
  34.5 1.0 %stop_sums.3 = f32[2,784,128]{2,1,0:T(8,128)S(1)} custom-call(bf16[24,84,512]{2,1,0:T(8,128)(2,1)S(1)} %bitcast.64, bf16[12,84,512]{2,1,0:T(8,128)(2,1)S(1)} %collective-permute-done.other, bf16[2,84,512]{2,1,0:T(8,128)(2,1)S(1)} %collective-permute-done.1.rest_0_, bf16[4,84,512]{2,1,0:T(8,128)(2,1)S(1)} %collective-permute-done.2.rest_1_), custom_call_target="tpu_custom_call" | custom-call | tf_op jit(solution)/shard_map/stop_sums/pallas_call | solution.py:209
  35.6 0.8 convert_element_type.27
  36.4 0.0 collective-permute-done.3.rest_0_
  36.4 0.0 copy-start
  36.4 0.8 copy-done
  37.1 5.9 %collective-permute-start.4 = (f16[2,784,128]{2,1,0:T(8,128)(2,1)}, f16[2,784,128]{2,1,0:T(8,128)(2,1)}, u32[]{:S(2)}, u32[]{:S(2)}) collective-permute-start(f16[2,784,128]{2,1,0:T(8,128)(2,1)} %convert_element_type.27), channel_id=1, source_target_pairs={{0,4},{1,21},{2,6},{3,23},{4,8},{5,1},{6,10},{7,3},{8,12},{9,5},{1... | collective-permute-start | bytes 1204232 | tf_op jit(solution)/shard_map/ppermute | solution.py:198
  43.1 9.7 %all-to-all-start = ((bf16[1,32,256,8]{2,3,0,1:T(8,128)(2,1)}), bf16[1,32,256,8]{2,3,0,1:T(8,128)(2,1)S(1)}, u32[]{:S(2)}, u32[]{:S(2)}) async-start(bf16[1,32,256,8]{2,3,0,1:T(8,128)(2,1)} %bitcast.7), calls=%async_computation | async-start | bytes 262144 | tf_op jit(solution)/shard_map/all_to_all | solution.py:235
  52.8 0.6 iota_compare_fusion.2
  53.3 0.6 iota_compare_fusion
  53.9 0.8 pack_rows.5
  54.7 1.9 %collective-permute-start.5 = (bf16[2,84,512]{2,1,0:T(8,128)(2,1)}, bf16[2,84,512]{2,1,0:T(8,128)(2,1)S(1)}, u32[]{:S(2)}, u32[]{:S(2)}) collective-permute-start(bf16[2,84,512]{2,1,0:T(8,128)(2,1)} %get-tuple-element.31), channel_id=1, source_target_pairs={{0,2},{1,23},{2,4},{3,1},{4,6},{5,3},{6,8},{7,5},{8,10},{9,7},{10,... | collective-permute-start | bytes 516104 | tf_op jit(solution)/shard_map/ppermute | solution.py:198
  56.6 3.6 %collective-permute-start.6 = (bf16[2,84,512]{2,1,0:T(8,128)(2,1)}, bf16[2,84,512]{2,1,0:T(8,128)(2,1)}, u32[]{:S(2)}, u32[]{:S(2)}) collective-permute-start(bf16[2,84,512]{2,1,0:T(8,128)(2,1)} %get-tuple-element.32), channel_id=1, source_target_pairs={{0,3},{1,22},{2,5},{3,0},{4,7},{5,2},{6,9},{7,4},{8,11},{9,6},{10,... | collective-permute-start | bytes 516104 | tf_op jit(solution)/shard_map/ppermute | solution.py:198
  60.2 1.9 %all-to-all-done = bf16[1,32,256,8]{2,3,0,1:T(8,128)(2,1)S(1)} async-done(((bf16[1,32,256,8]{2,3,0,1:T(8,128)(2,1)}), bf16[1,32,256,8]{2,3,0,1:T(8,128)(2,1)S(1)}, u32[]{:S(2)}, u32[]{:S(2)}) %all-to-all-start) | async-done | bytes 131104 | tf_op jit(solution)/shard_map/all_to_all | solution.py:235
  62.1 1.0 %copy-done.1 = bf16[4,84,512]{2,1,0:T(8,128)(2,1)S(1)} copy-done((bf16[4,84,512]{2,1,0:T(8,128)(2,1)S(1)}, bf16[4,84,512]{2,1,0:T(8,128)(2,1)}, u32[]{:S(2)}) %copy-start.1) | copy-done | bytes 344088
  63.1 0.8 stop_sums.4
  63.9 0.0 collective-permute-done.4
  64.0 1.1 %slice_convert_fusion = (f32[1,784,128]{2,1,0:T(8,128)S(1)}, f32[1,784,128]{2,1,0:T(8,128)S(1)}) fusion(f16[2,784,128]{2,1,0:T(8,128)(2,1)} %collective-permute-done.4), kind=kLoop, calls=%fused_computation.19 | loop fusion | flops 200704 | bytes 1204224 | tf_op jit(solution)/shard_map/convert_element_type | solution.py:86
  65.1 0.0 copy-done.7
  65.1 0.0 copy-done.8
  65.1 0.0 copy-done.9
  65.1 1.7 %fusion.11 = (f16[784,128]{1,0:T(8,128)(2,1)S(1)}, f16[784,128]{1,0:T(8,128)(2,1)S(1)}) fusion(f32[2,784,128]{2,1,0:T(8,128)S(1)} %stop_sums.4, f32[128]{0:T(128)S(1)} %bitcast.74, f32[128]{0:T(128)S(1)} %bitcast.73, f32[128]{0:T(128)S(1)} %get-tuple-element.49, f32[128]{0:T(128)S(1)} %get-tuple-element.39, f32[128]{0:T(128)S(1)} %get-tuple-element.64, ...), kind=kLoop, calls=%fused_computation.18 | loop fusion | flops 1806336 | bytes 1614128 | tf_op jit(solution)/shard_map/squeeze | solution.py:249
  66.8 0.0 collective-permute-done.5.rest_0_
  66.8 0.0 collective-permute-done.6.rest_1_
  66.8 4.4 %collective-permute-start.8 = (f16[784,128]{1,0:T(8,128)(2,1)S(1)}, f16[784,128]{1,0:T(8,128)(2,1)S(1)}, u32[]{:S(2)}, u32[]{:S(2)}) collective-permute-start(f16[784,128]{1,0:T(8,128)(2,1)S(1)} %get-tuple-element.34), channel_id=1, source_target_pairs={{0,5},{1,20},{2,7},{3,22},{4,9},{5,0},{6,11},{7,2},{8,13},{9,4},{1... | collective-permute-start | bytes 602120 | tf_op jit(solution)/shard_map/ppermute | solution.py:198
  71.3 2.2 %collective-permute-start.7 = (f16[784,128]{1,0:T(8,128)(2,1)S(1)}, f16[784,128]{1,0:T(8,128)(2,1)S(1)}, u32[]{:S(2)}, u32[]{:S(2)}) collective-permute-start(f16[784,128]{1,0:T(8,128)(2,1)S(1)} %get-tuple-element.33), channel_id=1, source_target_pairs={{0,4},{1,21},{2,6},{3,23},{4,8},{5,1},{6,10},{7,3},{8,12},{9,5},{1... | collective-permute-start | bytes 602120 | tf_op jit(solution)/shard_map/ppermute | solution.py:198
  73.5 1.6 %stop_sums.5 = f32[1,784,128]{2,1,0:T(8,128)S(1)} custom-call(bf16[24,84,512]{2,1,0:T(8,128)(2,1)S(1)} %bitcast.67, bf16[12,84,512]{2,1,0:T(8,128)(2,1)S(1)} %collective-permute-done.other, bf16[2,84,512]{2,1,0:T(8,128)(2,1)S(1)} %collective-permute-done.5.rest_0_, bf16[2,84,512]{2,1,0:T(8,128)(2,1)} %collective-permute-done.6.rest_1_), custom_call_target="tpu_custom_call" | custom-call | tf_op jit(solution)/shard_map/stop_sums/pallas_call | solution.py:209
  75.1 0.0 copy-start.3
  75.1 0.0 copy-start.4
  75.1 0.0 copy-start.5
  75.2 0.0 copy-start.6
  75.2 4.1 %collective-permute-done.8 = f16[784,128]{1,0:T(8,128)(2,1)S(1)} collective-permute-done((f16[784,128]{1,0:T(8,128)(2,1)S(1)}, f16[784,128]{1,0:T(8,128)(2,1)S(1)}, u32[]{:S(2)}, u32[]{:S(2)}) %collective-permute-start.8) | collective-permute-done | bytes 200736 | tf_op jit(solution)/shard_map/ppermute | solution.py:198
  79.3 1.0 %collective-permute-done.7 = f16[784,128]{1,0:T(8,128)(2,1)S(1)} collective-permute-done((f16[784,128]{1,0:T(8,128)(2,1)S(1)}, f16[784,128]{1,0:T(8,128)(2,1)S(1)}, u32[]{:S(2)}, u32[]{:S(2)}) %collective-permute-start.7) | collective-permute-done | bytes 200736 | tf_op jit(solution)/shard_map/ppermute | solution.py:198
  80.4 0.2 fusion.3.sums
  80.6 0.0 copy-done.2
  80.6 0.0 copy-done.3
  80.6 0.0 copy-done.4
  80.6 0.0 copy-done.5
  80.7 0.0 copy-done.6
  80.7 1.8 %residual.1 = f32[256,256]{1,0:T(8,128)} custom-call(s32[2]{0:T(128)S(1)} %bitcast.70, s32[2]{0:T(128)S(1)} %bitcast.71, s32[2]{0:T(128)S(1)} %bitcast.72, f32[100]{0:T(128)S(1)} %copy-done.6, f32[12,128]{1,0:T(8,128)S(1)} %bitcast.69, f32[784,128]{1,0:T(8,128)S(1)} %fusion.3.sums, bf16[256,256]{1,0:T(8,128)(2,1)S(1)} %bitcast.68), custom_call_target="tpu_custom_call" | custom-call | tf_op jit(solution)/shard_map/residual/pallas_call | solution.py:259
  (12 shorter events, 0.2 us)
Async XLA Ops:
  2.4 14.7 %collective-permute-start = (bf16[12,84,512]{2,1,0:T(8,128)(2,1)S(1)}, bf16[12,84,512]{2,1,0:T(8,128)(2,1)S(1)}, u32[]{:S(2)}, u32[]{:S(2)}) collective-permute-start(bf16[12,84,512]{2,1,0:T(8,128)(2,1)S(1)} %split_cores.1), channel_id=1, source_target_pairs={{0,1},{1,0},{2,3},{3,2},{4,5},{5,4},{6,7},{7,6},{8,9},{9,8},{10,11... | collective-permute-start | bytes 3096584 | tf_op jit(solution)/shard_map/ppermute | solution.py:224
  17.2 17.4 %collective-permute-start.2 = (bf16[4,84,512]{2,1,0:T(8,128)(2,1)S(1)}, bf16[4,84,512]{2,1,0:T(8,128)(2,1)S(1)}, u32[]{:S(2)}, u32[]{:S(2)}) collective-permute-start(bf16[4,84,512]{2,1,0:T(8,128)(2,1)S(1)} %get-tuple-element.24), channel_id=1, source_target_pairs={{0,2},{1,23},{2,4},{3,1},{4,6},{5,3},{6,8},{7,5},{8,10},{9,7},{10,... | collective-permute-start | bytes 1032200 | tf_op jit(solution)/shard_map/ppermute | solution.py:198
  22.5 13.9 %collective-permute-start.3 = (bf16[4,84,512]{2,1,0:T(8,128)(2,1)S(1)}, bf16[4,84,512]{2,1,0:T(8,128)(2,1)S(1)}, u32[]{:S(2)}, u32[]{:S(2)}) collective-permute-start(bf16[4,84,512]{2,1,0:T(8,128)(2,1)S(1)} %pack_rows.4), channel_id=1, source_target_pairs={{0,2},{1,23},{2,4},{3,1},{4,6},{5,3},{6,8},{7,5},{8,10},{9,7},{10,... | collective-permute-start | bytes 1032200 | tf_op jit(solution)/shard_map/ppermute | solution.py:198
  24.7 9.8 %collective-permute-start.1 = (bf16[2,84,512]{2,1,0:T(8,128)(2,1)S(1)}, bf16[2,84,512]{2,1,0:T(8,128)(2,1)S(1)}, u32[]{:S(2)}, u32[]{:S(2)}) collective-permute-start(bf16[2,84,512]{2,1,0:T(8,128)(2,1)S(1)} %get-tuple-element.22), channel_id=1, source_target_pairs={{0,4},{1,21},{2,6},{3,23},{4,8},{5,1},{6,10},{7,3},{8,12},{9,5},{1... | collective-permute-start | bytes 516104 | tf_op jit(solution)/shard_map/ppermute | solution.py:198
  36.4 0.8 copy-start
  37.1 26.8 %collective-permute-start.4 = (f16[2,784,128]{2,1,0:T(8,128)(2,1)}, f16[2,784,128]{2,1,0:T(8,128)(2,1)}, u32[]{:S(2)}, u32[]{:S(2)}) collective-permute-start(f16[2,784,128]{2,1,0:T(8,128)(2,1)} %convert_element_type.27), channel_id=1, source_target_pairs={{0,4},{1,21},{2,6},{3,23},{4,8},{5,1},{6,10},{7,3},{8,12},{9,5},{1... | collective-permute-start | bytes 1204232 | tf_op jit(solution)/shard_map/ppermute | solution.py:198
  43.1 19.1 %all-to-all-start = ((bf16[1,32,256,8]{2,3,0,1:T(8,128)(2,1)}), bf16[1,32,256,8]{2,3,0,1:T(8,128)(2,1)S(1)}, u32[]{:S(2)}, u32[]{:S(2)}) async-start(bf16[1,32,256,8]{2,3,0,1:T(8,128)(2,1)} %bitcast.7), calls=%async_computation | async-start | bytes 262144 | tf_op jit(solution)/shard_map/all_to_all | solution.py:235
  54.7 12.1 %collective-permute-start.5 = (bf16[2,84,512]{2,1,0:T(8,128)(2,1)}, bf16[2,84,512]{2,1,0:T(8,128)(2,1)S(1)}, u32[]{:S(2)}, u32[]{:S(2)}) collective-permute-start(bf16[2,84,512]{2,1,0:T(8,128)(2,1)} %get-tuple-element.31), channel_id=1, source_target_pairs={{0,2},{1,23},{2,4},{3,1},{4,6},{5,3},{6,8},{7,5},{8,10},{9,7},{10,... | collective-permute-start | bytes 516104 | tf_op jit(solution)/shard_map/ppermute | solution.py:198
  56.6 10.2 %collective-permute-start.6 = (bf16[2,84,512]{2,1,0:T(8,128)(2,1)}, bf16[2,84,512]{2,1,0:T(8,128)(2,1)}, u32[]{:S(2)}, u32[]{:S(2)}) collective-permute-start(bf16[2,84,512]{2,1,0:T(8,128)(2,1)} %get-tuple-element.32), channel_id=1, source_target_pairs={{0,3},{1,22},{2,5},{3,0},{4,7},{5,2},{6,9},{7,4},{8,11},{9,6},{10,... | collective-permute-start | bytes 516104 | tf_op jit(solution)/shard_map/ppermute | solution.py:198
  62.1 1.0 %copy-start.1 = (bf16[4,84,512]{2,1,0:T(8,128)(2,1)S(1)}, bf16[4,84,512]{2,1,0:T(8,128)(2,1)}, u32[]{:S(2)}) copy-start(bf16[4,84,512]{2,1,0:T(8,128)(2,1)} %copy-done) | copy-start | bytes 1032196
  63.1 1.9 %copy-start.7 = (pred[784]{0:T(1024)(128)(4,1)S(1)}, pred[784]{0:T(1024)(128)(4,1)}, u32[]{:S(2)}) copy-start(pred[784]{0:T(1024)(128)(4,1)} %get-tuple-element.68) | copy-start | bytes 2356
  63.1 1.9 %copy-start.8 = (pred[784]{0:T(1024)(128)(4,1)S(1)}, pred[784]{0:T(1024)(128)(4,1)}, u32[]{:S(2)}) copy-start(pred[784]{0:T(1024)(128)(4,1)} %get-tuple-element.67) | copy-start | bytes 2356
  63.1 2.0 %copy-start.9 = (pred[784]{0:T(1024)(128)(4,1)S(1)}, pred[784]{0:T(1024)(128)(4,1)}, u32[]{:S(2)}) copy-start(pred[784]{0:T(1024)(128)(4,1)} %iota_compare_fusion.2) | copy-start | bytes 2356
  66.8 12.4 %collective-permute-start.8 = (f16[784,128]{1,0:T(8,128)(2,1)S(1)}, f16[784,128]{1,0:T(8,128)(2,1)S(1)}, u32[]{:S(2)}, u32[]{:S(2)}) collective-permute-start(f16[784,128]{1,0:T(8,128)(2,1)S(1)} %get-tuple-element.34), channel_id=1, source_target_pairs={{0,5},{1,20},{2,7},{3,22},{4,9},{5,0},{6,11},{7,2},{8,13},{9,4},{1... | collective-permute-start | bytes 602120 | tf_op jit(solution)/shard_map/ppermute | solution.py:198
  71.3 9.1 %collective-permute-start.7 = (f16[784,128]{1,0:T(8,128)(2,1)S(1)}, f16[784,128]{1,0:T(8,128)(2,1)S(1)}, u32[]{:S(2)}, u32[]{:S(2)}) collective-permute-start(f16[784,128]{1,0:T(8,128)(2,1)S(1)} %get-tuple-element.33), channel_id=1, source_target_pairs={{0,4},{1,21},{2,6},{3,23},{4,8},{5,1},{6,10},{7,3},{8,12},{9,5},{1... | collective-permute-start | bytes 602120 | tf_op jit(solution)/shard_map/ppermute | solution.py:198
  75.1 5.5 %copy-start.2 = (f32[1536]{0:T(1024)S(1)}, f32[1536]{0:T(1024)}, u32[]{:S(2)}) copy-start(f32[1536]{0:T(1024)} %param.12) | copy-start | bytes 18436
  75.1 5.5 %copy-start.3 = (s32[1,1,2]{2,1,0:T(1,128)S(1)}, s32[1,1,2]{2,1,0:T(1,128)}, u32[]{:S(2)}) copy-start(s32[1,1,2]{2,1,0:T(1,128)} %param.9) | copy-start | bytes 28
  75.1 5.5 %copy-start.4 = (s32[1,1,2]{2,1,0:T(1,128)S(1)}, s32[1,1,2]{2,1,0:T(1,128)}, u32[]{:S(2)}) copy-start(s32[1,1,2]{2,1,0:T(1,128)} %param.10) | copy-start | bytes 28
  75.1 5.5 %copy-start.5 = (s32[1,1,2]{2,1,0:T(1,128)S(1)}, s32[1,1,2]{2,1,0:T(1,128)}, u32[]{:S(2)}) copy-start(s32[1,1,2]{2,1,0:T(1,128)} %param.11) | copy-start | bytes 28
  75.2 5.5 %copy-start.6 = (f32[100]{0:T(128)S(1)}, f32[100]{0:T(128)}, u32[]{:S(2)}) copy-start(f32[100]{0:T(128)} %occ.1) | copy-start | bytes 1204

commit v7 on v5

--- a/solution.py
+++ b/solution.py
@@ -120,8 +120,11 @@
     return [ints[2 * toward(chips, distance) + (c if mine else 1 - c)], other[at]]
 
 
-def pack_kernel(chips, wanted, ints, other, *outs):
+def pack_kernel(chips, wanted, ints, other, *rest):
+    arrived, outs = rest[: -len(wanted)], rest[-len(wanted) :]
     for group, out in zip(wanted, outs):
+        if not group:
+            out[...] = arrived[0][-2:]
         for n, row in enumerate(sum((chip_rows(chips, ints, other, *w) for w in group), [])):
             out[n] = row
 
@@ -197,13 +200,13 @@
                 pairs.append((chip * 2 + core, to * 2 + (core ^ int(cross))))
         return lax.ppermute(x, "aux", pairs)
 
-    def pack(wanted, other):
+    def pack(wanted, other, *arrived):
         return call(
             functools.partial(pack_kernel, chips, wanted),
-            2,
-            [((2 * len(group), naux, wide), BF16) for group in wanted],
+            2 + len(arrived),
+            [((2 * (len(group) or 1), naux, wide), BF16) for group in wanted],
             "pack_rows",
-        )(ints, other)
+        )(ints, other, *arrived)
 
     def stop_sums(stop, owners, picks, scaled, other, received):
         return call(
@@ -213,9 +216,10 @@
             "stop_sums",
         )(ints, other, *received)[0]
 
-    def pairs_at(d):
-        return [(d, True)] if d == far else [(d, True), (d, False)]
-
+
+    owned = lax.all_to_all(amplitudes, "pair", split_axis=1, concat_axis=3, tiled=True)
+    to_second = list(range(FIRST - 1, SECOND, -1))
+    to_owner = list(range(SECOND - 1, 0, -1))
 
     ints = integrals[:, 0]
     (other,) = call(
@@ -223,17 +227,15 @@
     )(ints)
     other = lax.ppermute(other, "aux", [(i, i ^ 1) for i in range(2 * chips)])
 
-    to_first = list(range(far, FIRST, -1))
-    to_second = list(range(FIRST - 1, SECOND, -1))
-    to_owner = list(range(SECOND - 1, 0, -1))
-    sends = pack([pairs_at(d) for d in to_first], other)
-    first_rows = [permute(x, d - FIRST) for d, x in zip(to_first, sends)]
-    owned = lax.all_to_all(amplitudes, "pair", split_axis=1, concat_axis=3, tiled=True)
-    gate, owned, *first_rows = lax.optimization_barrier((other, owned, *first_rows))
-    sends = pack([pairs_at(d) for d in to_second], gate)
+    (send,) = pack([[(far - 1, True), (far - 1, False), (far, True)]], other)
+    arrived = permute(send, 1)
+    gate, owned = lax.optimization_barrier((other, owned, send))[:2]
+    sends = pack([[(d, True), (d, False)] for d in to_second], gate)
     second_rows = [permute(x, d - SECOND) for d, x in zip(to_second, sends)]
-
-    picks = [((0, None) if d == far else (0, 2), at) for at, d in enumerate(to_first)]
+    (onward,) = pack([[]], other, arrived)
+    first_rows = [arrived, permute(onward, 1)]
+
+    picks = [((0, 2), 0), ((0, None), 1)]
     x = stop_sums(FIRST, (True, False), picks, True, other, first_rows).astype(F16)
     moving = permute(x, FIRST - SECOND)
 

time: 85.7 us -> 84.4 us (0.985)
  waiting for transfers between devices: 25.6 us -> 21 us
  other arithmetic: 1.24 us -> 3.94 us
  Pallas kernels: 6.21 us -> 7.4 us
    all_to_all x1, waiting for transfers between devices: 7.17 us -> 0.01 us  [on_device(): lax.all_to_all(amplitudes, 'pair', split_axis=1, concat_axis=3, tiled=True)]
    ppermute x8, waiting for transfers between devices: 16.1 us -> 18.7 us  [permute(): return lax.ppermute(x, 'aux', pairs)]
    pallas_call x3 -> x4, Pallas kernels: 0.87 us -> 2 us  [pack(): call(functools.partial(pack_kernel, chips, wanted), 2 + len(arrived), [((...]
    convert_element_type x3, other arithmetic: 0.11 us -> 1.14 us  [decode(): x = x.astype(F32)]
    squeeze x1, other arithmetic: 0.79 us -> 1.72 us  [on_device(): last = [add_on(moving[n:n + 1], local[n:n + 1])[0] for n in range(2)]]
    unnamed x13 -> x11, local copies, waits for them, and re-layouts: 2.95 us -> 2.28 us
  transfers between devices with their start and end apart: 10 -> 10, of which waited for: 6 -> 5; matrix products, arithmetic and copies ran while one was open for 1% -> 4% of each run, Pallas kernels for 2% -> 6%
where the time goes in v7:
time: 84.4 us; the launch traced here: 83.8 us
  starting transfers between devices  48.9 us (58%)
  waiting for transfers between devices  21 us (25%)
  Pallas kernels  7.4 us (9%)
  other arithmetic  3.94 us (5%)
  local copies, waits for them, and re-layouts  2.28 us (3%)
    ppermute x8, starting transfers between devices, permute(): return lax.ppermute(x, 'aux', pairs)  26.8 us
    ppermute x8, waiting for transfers between devices, permute(): return lax.ppermute(x, 'aux', pairs)  18.7 us
    ppermute x1, starting transfers between devices, on_device(): other = lax.ppermute(other, 'aux', [(i, i ^ 1) for i in range(2 * chips)])  12.4 us
    all_to_all x1, starting transfers between devices, on_device(): lax.all_to_all(amplitudes, 'pair', split_axis=1, concat_axis=3, tiled=True)  9.68 us
    pallas_call x3, Pallas kernels, stop_sums(): call(functools.partial(stop_kernel, chips, stop, owners, picks, scaled),...  3.55 us
    ppermute x1, waiting for transfers between devices, on_device(): other = lax.ppermute(other, 'aux', [(i, i ^ 1) for i in range(2 * chips)])  2.31 us
    unnamed x11, local copies, waits for them, and re-layouts  2.28 us
    pallas_call x4, Pallas kernels, pack(): call(functools.partial(pack_kernel, chips, wanted), 2 + len(arrived), [((...  2 us
  transfers between devices with their start and end apart: 10, of which 5 were waited for; matrix products, arithmetic and copies ran while one was open for 4% of the time, Pallas kernels for 6%

profile of v7, /device:TPU:1, one launch (start us, length us, event | category | flops | bytes accessed | tf_op | source)
XLA Modules:
  0.0 83.8 jit_solution(13777670194092613196)
XLA Ops:
  0.0 2.3 %copy.12 = bf16[24,1,84,512]{3,2,0,1:T(8,128)(2,1)S(1)} copy(bf16[24,1,84,512]{3,0,2,1:T(8,128)(2,1)} %param.8) | data formatting | bytes 4128768 | tf_op args[1]
  2.3 0.1 split_cores.1
  2.4 12.4 %collective-permute-start = (bf16[12,84,512]{2,1,0:T(8,128)(2,1)S(1)}, bf16[12,84,512]{2,1,0:T(8,128)(2,1)S(1)}, u32[]{:S(2)}, u32[]{:S(2)}) collective-permute-start(bf16[12,84,512]{2,1,0:T(8,128)(2,1)S(1)} %split_cores.1), channel_id=1, source_target_pairs={{0,1},{1,0},{2,3},{3,2},{4,5},{5,4},{6,7},{7,6},{8,9},{9,8},{10,11... | collective-permute-start | bytes 3096584 | tf_op jit(solution)/shard_map/ppermute | solution.py:228
  14.8 2.3 %collective-permute-done.other = bf16[12,84,512]{2,1,0:T(8,128)(2,1)S(1)} collective-permute-done((bf16[12,84,512]{2,1,0:T(8,128)(2,1)S(1)}, bf16[12,84,512]{2,1,0:T(8,128)(2,1)S(1)}, u32[]{:S(2)}, u32[]{:S(2)}) %collective-permute-start) | collective-permute-done | bytes 1032224 | tf_op jit(solution)/shard_map/ppermute | solution.py:228
  17.1 0.9 %pack_rows.4 = bf16[6,84,512]{2,1,0:T(8,128)(2,1)} custom-call(bf16[24,84,512]{2,1,0:T(8,128)(2,1)S(1)} %bitcast.62, bf16[12,84,512]{2,1,0:T(8,128)(2,1)S(1)} %collective-permute-done.other), custom_call_target="tpu_custom_call" | custom-call | tf_op jit(solution)/shard_map/pack_rows/pallas_call | solution.py:204
  18.0 5.3 %collective-permute-start.1 = (bf16[6,84,512]{2,1,0:T(8,128)(2,1)}, bf16[6,84,512]{2,1,0:T(8,128)(2,1)}, u32[]{:S(2)}, u32[]{:S(2)}) collective-permute-start(bf16[6,84,512]{2,1,0:T(8,128)(2,1)} %pack_rows.4), channel_id=1, source_target_pairs={{0,2},{1,23},{2,4},{3,1},{4,6},{5,3},{6,8},{7,5},{8,10},{9,7},{10,... | collective-permute-start | bytes 1548296 | tf_op jit(solution)/shard_map/ppermute | solution.py:201
  23.3 9.7 %all-to-all-start = ((bf16[1,32,256,8]{2,3,0,1:T(8,128)(2,1)}), bf16[1,32,256,8]{2,3,0,1:T(8,128)(2,1)S(1)}, u32[]{:S(2)}, u32[]{:S(2)}) async-start(bf16[1,32,256,8]{2,3,0,1:T(8,128)(2,1)} %bitcast.7), calls=%async_computation | async-start | bytes 262144 | tf_op jit(solution)/shard_map/all_to_all | solution.py:220
  32.9 0.0 collective-permute-done.1.rest_0_
  33.0 1.1 %pack_rows.5 = bf16[2,84,512]{2,1,0:T(8,128)(2,1)S(1)} custom-call(bf16[24,84,512]{2,1,0:T(8,128)(2,1)S(1)} %bitcast.63, bf16[12,84,512]{2,1,0:T(8,128)(2,1)S(1)} %collective-permute-done.other, bf16[6,84,512]{2,1,0:T(8,128)(2,1)} %collective-permute-done.1.rest_0_), custom_call_target="tpu_custom_call" | custom-call | tf_op jit(solution)/shard_map/pack_rows/pallas_call | solution.py:204
  34.0 2.2 %collective-permute-start.2 = (bf16[2,84,512]{2,1,0:T(8,128)(2,1)S(1)}, bf16[2,84,512]{2,1,0:T(8,128)(2,1)S(1)}, u32[]{:S(2)}, u32[]{:S(2)}) collective-permute-start(bf16[2,84,512]{2,1,0:T(8,128)(2,1)S(1)} %pack_rows.5), channel_id=1, source_target_pairs={{0,2},{1,23},{2,4},{3,1},{4,6},{5,3},{6,8},{7,5},{8,10},{9,7},{10,... | collective-permute-start | bytes 516104 | tf_op jit(solution)/shard_map/ppermute | solution.py:201
  36.2 4.3 %collective-permute-done.2.rest_1_ = bf16[2,84,512]{2,1,0:T(8,128)(2,1)S(1)} collective-permute-done((bf16[2,84,512]{2,1,0:T(8,128)(2,1)S(1)}, bf16[2,84,512]{2,1,0:T(8,128)(2,1)S(1)}, u32[]{:S(2)}, u32[]{:S(2)}) %collective-permute-start.2) | collective-permute-done | bytes 172064 | tf_op jit(solution)/shard_map/ppermute | solution.py:201
  40.6 2.1 %stop_sums.3 = f32[2,784,128]{2,1,0:T(8,128)S(1)} custom-call(bf16[24,84,512]{2,1,0:T(8,128)(2,1)S(1)} %bitcast.64, bf16[12,84,512]{2,1,0:T(8,128)(2,1)S(1)} %collective-permute-done.other, bf16[6,84,512]{2,1,0:T(8,128)(2,1)} %collective-permute-done.1.rest_0_, bf16[2,84,512]{2,1,0:T(8,128)(2,1)S(1)} %collective-permute-done.2.rest_1_), custom_call_target="tpu_custom_call" | custom-call | tf_op jit(solution)/shard_map/stop_sums/pallas_call | solution.py:212
  42.6 0.8 convert_element_type.27
  43.4 2.2 %collective-permute-start.3 = (f16[2,784,128]{2,1,0:T(8,128)(2,1)}, f16[2,784,128]{2,1,0:T(8,128)(2,1)}, u32[]{:S(2)}, u32[]{:S(2)}) collective-permute-start(f16[2,784,128]{2,1,0:T(8,128)(2,1)} %convert_element_type.27), channel_id=1, source_target_pairs={{0,4},{1,21},{2,6},{3,23},{4,8},{5,1},{6,10},{7,3},{8,12},{9,5},{1... | collective-permute-start | bytes 1204232 | tf_op jit(solution)/shard_map/ppermute | solution.py:201
  45.6 0.0 all-to-all-done
  45.7 3.2 %collective-permute-start.4 = (bf16[4,84,512]{2,1,0:T(8,128)(2,1)S(1)}, bf16[4,84,512]{2,1,0:T(8,128)(2,1)S(1)}, u32[]{:S(2)}, u32[]{:S(2)}) collective-permute-start(bf16[4,84,512]{2,1,0:T(8,128)(2,1)S(1)} %pack_rows.6), channel_id=1, source_target_pairs={{0,2},{1,23},{2,4},{3,1},{4,6},{5,3},{6,8},{7,5},{8,10},{9,7},{10,... | collective-permute-start | bytes 1032200 | tf_op jit(solution)/shard_map/ppermute | solution.py:201
  48.9 2.4 %collective-permute-start.5 = (bf16[2,84,512]{2,1,0:T(8,128)(2,1)S(1)}, bf16[2,84,512]{2,1,0:T(8,128)(2,1)S(1)}, u32[]{:S(2)}, u32[]{:S(2)}) collective-permute-start(bf16[2,84,512]{2,1,0:T(8,128)(2,1)S(1)} %get-tuple-element.17), channel_id=1, source_target_pairs={{0,2},{1,23},{2,4},{3,1},{4,6},{5,3},{6,8},{7,5},{8,10},{9,7},{10,... | collective-permute-start | bytes 516104 | tf_op jit(solution)/shard_map/ppermute | solution.py:201
  51.3 3.4 %collective-permute-start.6 = (bf16[2,84,512]{2,1,0:T(8,128)(2,1)S(1)}, bf16[2,84,512]{2,1,0:T(8,128)(2,1)S(1)}, u32[]{:S(2)}, u32[]{:S(2)}) collective-permute-start(bf16[2,84,512]{2,1,0:T(8,128)(2,1)S(1)} %get-tuple-element.18), channel_id=1, source_target_pairs={{0,3},{1,22},{2,5},{3,0},{4,7},{5,2},{6,9},{7,4},{8,11},{9,6},{10,... | collective-permute-start | bytes 516104 | tf_op jit(solution)/shard_map/ppermute | solution.py:201
  54.7 6.9 %collective-permute-done.4.rest_0_ = bf16[4,84,512]{2,1,0:T(8,128)(2,1)S(1)} collective-permute-done((bf16[4,84,512]{2,1,0:T(8,128)(2,1)S(1)}, bf16[4,84,512]{2,1,0:T(8,128)(2,1)S(1)}, u32[]{:S(2)}, u32[]{:S(2)}) %collective-permute-start.4) | collective-permute-done | bytes 344096 | tf_op jit(solution)/shard_map/ppermute | solution.py:201
  61.6 0.8 stop_sums.4
  62.4 0.0 collective-permute-done.3
  62.4 1.1 %slice_convert_fusion = (f32[1,784,128]{2,1,0:T(8,128)S(1)}, f32[1,784,128]{2,1,0:T(8,128)S(1)}) fusion(f16[2,784,128]{2,1,0:T(8,128)(2,1)} %collective-permute-done.3), kind=kLoop, calls=%fused_computation.19 | loop fusion | flops 200704 | bytes 1204224 | tf_op jit(solution)/shard_map/convert_element_type | solution.py:86
  63.5 1.7 %fusion.11 = (f16[784,128]{1,0:T(8,128)(2,1)S(1)}, f16[784,128]{1,0:T(8,128)(2,1)S(1)}) fusion(f32[2,784,128]{2,1,0:T(8,128)S(1)} %stop_sums.4, f32[128]{0:T(128)S(1)} %bitcast.75, f32[128]{0:T(128)S(1)} %bitcast.74, f32[128]{0:T(128)S(1)} %get-tuple-element.35, f32[128]{0:T(128)S(1)} %get-tuple-element.25, f32[128]{0:T(128)S(1)} %get-tuple-element.50, ...), kind=kLoop, calls=%fused_computation.18 | loop fusion | flops 1806336 | bytes 1614128 | tf_op jit(solution)/shard_map/squeeze | solution.py:248
  65.3 0.0 collective-permute-done.5.rest_0_
  65.3 0.0 collective-permute-done.6.rest_1_
  65.3 3.8 %collective-permute-start.7 = (f16[784,128]{1,0:T(8,128)(2,1)S(1)}, f16[784,128]{1,0:T(8,128)(2,1)S(1)}, u32[]{:S(2)}, u32[]{:S(2)}) collective-permute-start(f16[784,128]{1,0:T(8,128)(2,1)S(1)} %get-tuple-element.19), channel_id=1, source_target_pairs={{0,4},{1,21},{2,6},{3,23},{4,8},{5,1},{6,10},{7,3},{8,12},{9,5},{1... | collective-permute-start | bytes 602120 | tf_op jit(solution)/shard_map/ppermute | solution.py:201
  69.1 4.3 %collective-permute-start.8 = (f16[784,128]{1,0:T(8,128)(2,1)S(1)}, f16[784,128]{1,0:T(8,128)(2,1)S(1)}, u32[]{:S(2)}, u32[]{:S(2)}) collective-permute-start(f16[784,128]{1,0:T(8,128)(2,1)S(1)} %get-tuple-element.20), channel_id=1, source_target_pairs={{0,5},{1,20},{2,7},{3,22},{4,9},{5,0},{6,11},{7,2},{8,13},{9,4},{1... | collective-permute-start | bytes 602120 | tf_op jit(solution)/shard_map/ppermute | solution.py:201
  73.4 0.7 stop_sums.5
  74.1 0.0 copy-start
  74.1 0.0 copy-start.1
  74.1 0.0 copy-start.2
  74.1 0.0 copy-start.3
  74.1 0.0 copy-start.4
  74.1 1.2 %collective-permute-done.7 = f16[784,128]{1,0:T(8,128)(2,1)S(1)} collective-permute-done((f16[784,128]{1,0:T(8,128)(2,1)S(1)}, f16[784,128]{1,0:T(8,128)(2,1)S(1)}, u32[]{:S(2)}, u32[]{:S(2)}) %collective-permute-start.7) | collective-permute-done | bytes 200736 | tf_op jit(solution)/shard_map/ppermute | solution.py:201
  75.4 6.3 %collective-permute-done.8 = f16[784,128]{1,0:T(8,128)(2,1)S(1)} collective-permute-done((f16[784,128]{1,0:T(8,128)(2,1)S(1)}, f16[784,128]{1,0:T(8,128)(2,1)S(1)}, u32[]{:S(2)}, u32[]{:S(2)}) %collective-permute-start.8) | collective-permute-done | bytes 200736 | tf_op jit(solution)/shard_map/ppermute | solution.py:201
  81.8 0.2 fusion.3.sums
  82.0 0.0 copy-done
  82.0 0.0 copy-done.1
  82.0 0.0 copy-done.2
  82.0 0.0 copy-done.3
  82.0 0.0 copy-done.4
  82.1 1.8 %residual.1 = f32[256,256]{1,0:T(8,128)} custom-call(s32[2]{0:T(128)S(1)} %bitcast.71, s32[2]{0:T(128)S(1)} %bitcast.72, s32[2]{0:T(128)S(1)} %bitcast.73, f32[100]{0:T(128)S(1)} %copy-done.4, f32[12,128]{1,0:T(8,128)S(1)} %bitcast.70, f32[784,128]{1,0:T(8,128)S(1)} %fusion.3.sums, bf16[256,256]{1,0:T(8,128)(2,1)S(1)} %bitcast.69), custom_call_target="tpu_custom_call" | custom-call | tf_op jit(solution)/shard_map/residual/pallas_call | solution.py:258
  (9 shorter events, 0.2 us)
Async XLA Ops:
  2.4 14.7 %collective-permute-start = (bf16[12,84,512]{2,1,0:T(8,128)(2,1)S(1)}, bf16[12,84,512]{2,1,0:T(8,128)(2,1)S(1)}, u32[]{:S(2)}, u32[]{:S(2)}) collective-permute-start(bf16[12,84,512]{2,1,0:T(8,128)(2,1)S(1)} %split_cores.1), channel_id=1, source_target_pairs={{0,1},{1,0},{2,3},{3,2},{4,5},{5,4},{6,7},{7,6},{8,9},{9,8},{10,11... | collective-permute-start | bytes 3096584 | tf_op jit(solution)/shard_map/ppermute | solution.py:228
  18.0 15.0 %collective-permute-start.1 = (bf16[6,84,512]{2,1,0:T(8,128)(2,1)}, bf16[6,84,512]{2,1,0:T(8,128)(2,1)}, u32[]{:S(2)}, u32[]{:S(2)}) collective-permute-start(bf16[6,84,512]{2,1,0:T(8,128)(2,1)} %pack_rows.4), channel_id=1, source_target_pairs={{0,2},{1,23},{2,4},{3,1},{4,6},{5,3},{6,8},{7,5},{8,10},{9,7},{10,... | collective-permute-start | bytes 1548296 | tf_op jit(solution)/shard_map/ppermute | solution.py:201
  23.3 22.3 %all-to-all-start = ((bf16[1,32,256,8]{2,3,0,1:T(8,128)(2,1)}), bf16[1,32,256,8]{2,3,0,1:T(8,128)(2,1)S(1)}, u32[]{:S(2)}, u32[]{:S(2)}) async-start(bf16[1,32,256,8]{2,3,0,1:T(8,128)(2,1)} %bitcast.7), calls=%async_computation | async-start | bytes 262144 | tf_op jit(solution)/shard_map/all_to_all | solution.py:220
  34.0 6.5 %collective-permute-start.2 = (bf16[2,84,512]{2,1,0:T(8,128)(2,1)S(1)}, bf16[2,84,512]{2,1,0:T(8,128)(2,1)S(1)}, u32[]{:S(2)}, u32[]{:S(2)}) collective-permute-start(bf16[2,84,512]{2,1,0:T(8,128)(2,1)S(1)} %pack_rows.5), channel_id=1, source_target_pairs={{0,2},{1,23},{2,4},{3,1},{4,6},{5,3},{6,8},{7,5},{8,10},{9,7},{10,... | collective-permute-start | bytes 516104 | tf_op jit(solution)/shard_map/ppermute | solution.py:201
  43.4 19.0 %collective-permute-start.3 = (f16[2,784,128]{2,1,0:T(8,128)(2,1)}, f16[2,784,128]{2,1,0:T(8,128)(2,1)}, u32[]{:S(2)}, u32[]{:S(2)}) collective-permute-start(f16[2,784,128]{2,1,0:T(8,128)(2,1)} %convert_element_type.27), channel_id=1, source_target_pairs={{0,4},{1,21},{2,6},{3,23},{4,8},{5,1},{6,10},{7,3},{8,12},{9,5},{1... | collective-permute-start | bytes 1204232 | tf_op jit(solution)/shard_map/ppermute | solution.py:201
  45.7 15.9 %collective-permute-start.4 = (bf16[4,84,512]{2,1,0:T(8,128)(2,1)S(1)}, bf16[4,84,512]{2,1,0:T(8,128)(2,1)S(1)}, u32[]{:S(2)}, u32[]{:S(2)}) collective-permute-start(bf16[4,84,512]{2,1,0:T(8,128)(2,1)S(1)} %pack_rows.6), channel_id=1, source_target_pairs={{0,2},{1,23},{2,4},{3,1},{4,6},{5,3},{6,8},{7,5},{8,10},{9,7},{10,... | collective-permute-start | bytes 1032200 | tf_op jit(solution)/shard_map/ppermute | solution.py:201
  48.9 16.4 %collective-permute-start.5 = (bf16[2,84,512]{2,1,0:T(8,128)(2,1)S(1)}, bf16[2,84,512]{2,1,0:T(8,128)(2,1)S(1)}, u32[]{:S(2)}, u32[]{:S(2)}) collective-permute-start(bf16[2,84,512]{2,1,0:T(8,128)(2,1)S(1)} %get-tuple-element.17), channel_id=1, source_target_pairs={{0,2},{1,23},{2,4},{3,1},{4,6},{5,3},{6,8},{7,5},{8,10},{9,7},{10,... | collective-permute-start | bytes 516104 | tf_op jit(solution)/shard_map/ppermute | solution.py:201
  51.3 14.0 %collective-permute-start.6 = (bf16[2,84,512]{2,1,0:T(8,128)(2,1)S(1)}, bf16[2,84,512]{2,1,0:T(8,128)(2,1)S(1)}, u32[]{:S(2)}, u32[]{:S(2)}) collective-permute-start(bf16[2,84,512]{2,1,0:T(8,128)(2,1)S(1)} %get-tuple-element.18), channel_id=1, source_target_pairs={{0,3},{1,22},{2,5},{3,0},{4,7},{5,2},{6,9},{7,4},{8,11},{9,6},{10,... | collective-permute-start | bytes 516104 | tf_op jit(solution)/shard_map/ppermute | solution.py:201
  65.3 10.1 %collective-permute-start.7 = (f16[784,128]{1,0:T(8,128)(2,1)S(1)}, f16[784,128]{1,0:T(8,128)(2,1)S(1)}, u32[]{:S(2)}, u32[]{:S(2)}) collective-permute-start(f16[784,128]{1,0:T(8,128)(2,1)S(1)} %get-tuple-element.19), channel_id=1, source_target_pairs={{0,4},{1,21},{2,6},{3,23},{4,8},{5,1},{6,10},{7,3},{8,12},{9,5},{1... | collective-permute-start | bytes 602120 | tf_op jit(solution)/shard_map/ppermute | solution.py:201
  69.1 12.6 %collective-permute-start.8 = (f16[784,128]{1,0:T(8,128)(2,1)S(1)}, f16[784,128]{1,0:T(8,128)(2,1)S(1)}, u32[]{:S(2)}, u32[]{:S(2)}) collective-permute-start(f16[784,128]{1,0:T(8,128)(2,1)S(1)} %get-tuple-element.20), channel_id=1, source_target_pairs={{0,5},{1,20},{2,7},{3,22},{4,9},{5,0},{6,11},{7,2},{8,13},{9,4},{1... | collective-permute-start | bytes 602120 | tf_op jit(solution)/shard_map/ppermute | solution.py:201
  74.1 7.9 %copy-start = (f32[1536]{0:T(1024)S(1)}, f32[1536]{0:T(1024)}, u32[]{:S(2)}) copy-start(f32[1536]{0:T(1024)} %param.12) | copy-start | bytes 18436
  74.1 7.9 %copy-start.1 = (s32[1,1,2]{2,1,0:T(1,128)S(1)}, s32[1,1,2]{2,1,0:T(1,128)}, u32[]{:S(2)}) copy-start(s32[1,1,2]{2,1,0:T(1,128)} %param.9) | copy-start | bytes 28
  74.1 7.9 %copy-start.2 = (s32[1,1,2]{2,1,0:T(1,128)S(1)}, s32[1,1,2]{2,1,0:T(1,128)}, u32[]{:S(2)}) copy-start(s32[1,1,2]{2,1,0:T(1,128)} %param.10) | copy-start | bytes 28
  74.1 7.9 %copy-start.3 = (s32[1,1,2]{2,1,0:T(1,128)S(1)}, s32[1,1,2]{2,1,0:T(1,128)}, u32[]{:S(2)}) copy-start(s32[1,1,2]{2,1,0:T(1,128)} %param.11) | copy-start | bytes 28
  74.1 7.9 %copy-start.4 = (f32[100]{0:T(128)S(1)}, f32[100]{0:T(128)}, u32[]{:S(2)}) copy-start(f32[100]{0:T(128)} %occ.1) | copy-start | bytes 1204

commit v8 on v5

--- a/solution.py
+++ b/solution.py
@@ -8,7 +8,7 @@
 from jax.sharding import PartitionSpec as P
 
 TILE = 128
-FIRST, SECOND = 4, 2
+STOP = 2
 H_ROWS, G_ROWS = 4 * TILE, 2 * TILE
 DIAG = H_ROWS + G_ROWS
 H_EXP, G_EXP = DIAG + 1, DIAG + 2
@@ -88,15 +88,6 @@
     return x * scales(-e_h, -e_g)[1], e_h, e_g
 
 
-def add_on(x, own):
-    x, e_h, e_g = decode(x)
-    own_h, own_g = exponents(own)
-    e_h, e_g = jnp.minimum(e_h, own_h) - 1.0, jnp.minimum(e_g, own_g) - 1.0
-    row, scale = scales(e_h, e_g)
-    tail = jnp.where(row == H_EXP, e_h, e_g)
-    return jnp.where(row <= DIAG, (x + own) * scale, tail).astype(F16)
-
-
 def split_kernel(chips, ints, out):
     z, c, _ = here()
     near = chips // 2 - 1
@@ -223,33 +214,26 @@
     )(ints)
     other = lax.ppermute(other, "aux", [(i, i ^ 1) for i in range(2 * chips)])
 
-    to_first = list(range(far, FIRST, -1))
-    to_second = list(range(FIRST - 1, SECOND, -1))
-    to_owner = list(range(SECOND - 1, 0, -1))
-    sends = pack([pairs_at(d) for d in to_first], other)
-    first_rows = [permute(x, d - FIRST) for d, x in zip(to_first, sends)]
+    to_stop = list(range(far, STOP, -1))
+    sends = pack([pairs_at(d) for d in to_stop], other)
+    rows = [permute(x, d - STOP) for d, x in zip(to_stop, sends)]
     owned = lax.all_to_all(amplitudes, "pair", split_axis=1, concat_axis=3, tiled=True)
-    gate, owned, *first_rows = lax.optimization_barrier((other, owned, *first_rows))
-    sends = pack([pairs_at(d) for d in to_second], gate)
-    second_rows = [permute(x, d - SECOND) for d, x in zip(to_second, sends)]
-
-    picks = [((0, None) if d == far else (0, 2), at) for at, d in enumerate(to_first)]
-    x = stop_sums(FIRST, (True, False), picks, True, other, first_rows).astype(F16)
-    moving = permute(x, FIRST - SECOND)
+
+    picks = [((0, None) if d == far else (0, 2), at) for at, d in enumerate(to_stop)]
+    moving = []
+    for n, mine in enumerate((True, False)):
+        x = stop_sums(STOP, (mine,), [((at[n],), ref) for at, ref in picks], True, other, rows)
+        x = x[0].astype(F16)
+        if n == 0:
+            x, owned = lax.optimization_barrier((x, owned))
+        moving.append(permute(x, STOP, n == 1))
 
     gate = lax.optimization_barrier((other, x))[0]
-    sends = pack([[(d, mine)] for d in to_owner for mine in (True, False)], gate)
-    ways = [(d, n == 1) for d in to_owner for n in range(2)]
-    owner_rows = [permute(x, *way) for way, x in zip(ways, sends)]
-    picks = [((0, 2), at) for at in range(len(to_second))]
-    local = stop_sums(SECOND, (True, False), picks, False, gate, second_rows)
-    last = [add_on(moving[n : n + 1], local[n : n + 1])[0] for n in range(2)]
-    *last, owner_rows = lax.optimization_barrier((*last, owner_rows))
-    moving = [permute(last[n], SECOND, n == 1) for n in range(2)]
-
-    gate = lax.optimization_barrier((other, last[1]))[0]
-    picks = [((0,), at) for at in range(len(owner_rows))]
-    local = stop_sums(0, (True,), picks, False, gate, owner_rows)
+    to_owner = [(d, n) for d in range(STOP - 1, 0, -1) for n in range(2)]
+    sends = pack([[(d, n == 0)] for d, n in to_owner], gate)
+    rows = [permute(x, d, n == 1) for (d, n), x in zip(to_owner, sends)]
+    picks = [((0,), at) for at in range(len(rows))]
+    local = stop_sums(0, (True,), picks, False, gate, rows)
     sums = (decode(moving[0][None])[0] + decode(moving[1][None])[0] + local)[0]
     amps_t = jnp.swapaxes(owned[0, 0], 0, 1)
 

time: 85.7 us -> 84.6 us (0.987)
  waiting for transfers between devices: 25.6 us -> 21.4 us
  starting transfers between devices: 49 us -> 51.2 us
  Pallas kernels: 6.21 us -> 7.94 us
    all_to_all x1, waiting for transfers between devices: 7.17 us -> 0.01 us  [on_device(): lax.all_to_all(amplitudes, 'pair', split_axis=1, concat_axis=3, tiled=True)]
    ppermute x8, waiting for transfers between devices: 16.1 us -> 19.1 us  [permute(): return lax.ppermute(x, 'aux', pairs)]
    ppermute x8, starting transfers between devices: 26.9 us -> 29.1 us  [permute(): return lax.ppermute(x, 'aux', pairs)]
    pallas_call x3, Pallas kernels: 3.49 us -> 4.93 us  [stop_sums(): call(functools.partial(stop_kernel, chips, stop, owners, picks, scaled),...]
    unnamed x13 -> x11, local copies, waits for them, and re-layouts: 2.95 us -> 2.28 us
  transfers between devices with their start and end apart: 10 -> 10, of which waited for: 6 -> 5; matrix products, arithmetic and copies ran while one was open for 1% -> 1% of each run, Pallas kernels for 2% -> 6%
where the time goes in v8:
time: 84.6 us; the launch traced here: 84.1 us
  starting transfers between devices  51.2 us (61%)
  waiting for transfers between devices  21.4 us (25%)
  Pallas kernels  7.94 us (9%)
  local copies, waits for them, and re-layouts  2.28 us (3%)
  other arithmetic  1.04 us (1%)
    ppermute x8, starting transfers between devices, permute(): return lax.ppermute(x, 'aux', pairs)  29.1 us
    ppermute x8, waiting for transfers between devices, permute(): return lax.ppermute(x, 'aux', pairs)  19.1 us
    ppermute x1, starting transfers between devices, on_device(): other = lax.ppermute(other, 'aux', [(i, i ^ 1) for i in range(2 * chips)])  12.4 us
    all_to_all x1, starting transfers between devices, on_device(): lax.all_to_all(amplitudes, 'pair', split_axis=1, concat_axis=3, tiled=True)  9.68 us
    pallas_call x3, Pallas kernels, stop_sums(): call(functools.partial(stop_kernel, chips, stop, owners, picks, scaled),...  4.93 us
    ppermute x1, waiting for transfers between devices, on_device(): other = lax.ppermute(other, 'aux', [(i, i ^ 1) for i in range(2 * chips)])  2.31 us
    unnamed x11, local copies, waits for them, and re-layouts  2.28 us
    pallas_call x1, Pallas kernels, on_device(): call(final_kernel, 3, [((2 * TILE, 2 * TILE), F32)], 'residual', 4)  1.75 us
  transfers between devices with their start and end apart: 10, of which 5 were waited for; matrix products, arithmetic and copies ran while one was open for 1% of the time, Pallas kernels for 6%

profile of v8, /device:TPU:1, one launch (start us, length us, event | category | flops | bytes accessed | tf_op | source)
XLA Modules:
  0.0 84.1 jit_solution(3159227433077094420)
XLA Ops:
  0.0 2.3 %copy.12 = bf16[24,1,84,512]{3,2,0,1:T(8,128)(2,1)S(1)} copy(bf16[24,1,84,512]{3,0,2,1:T(8,128)(2,1)} %param.8) | data formatting | bytes 4128768 | tf_op args[1]
  2.3 0.1 split_cores.1
  2.4 12.4 %collective-permute-start = (bf16[12,84,512]{2,1,0:T(8,128)(2,1)S(1)}, bf16[12,84,512]{2,1,0:T(8,128)(2,1)S(1)}, u32[]{:S(2)}, u32[]{:S(2)}) collective-permute-start(bf16[12,84,512]{2,1,0:T(8,128)(2,1)S(1)} %split_cores.1), channel_id=1, source_target_pairs={{0,1},{1,0},{2,3},{3,2},{4,5},{5,4},{6,7},{7,6},{8,9},{9,8},{10,11... | collective-permute-start | bytes 3096584 | tf_op jit(solution)/shard_map/ppermute | solution.py:215
  14.8 2.3 %collective-permute-done.other = bf16[12,84,512]{2,1,0:T(8,128)(2,1)S(1)} collective-permute-done((bf16[12,84,512]{2,1,0:T(8,128)(2,1)S(1)}, bf16[12,84,512]{2,1,0:T(8,128)(2,1)S(1)}, u32[]{:S(2)}, u32[]{:S(2)}) %collective-permute-start) | collective-permute-done | bytes 1032224 | tf_op jit(solution)/shard_map/ppermute | solution.py:215
  17.1 1.1 %pack_rows.2 = (bf16[2,84,512]{2,1,0:T(8,128)(2,1)}, bf16[4,84,512]{2,1,0:T(8,128)(2,1)}, bf16[4,84,512]{2,1,0:T(8,128)(2,1)}, bf16[4,84,512]{2,1,0:T(8,128)(2,1)}) custom-call(bf16[24,84,512]{2,1,0:T(8,128)(2,1)S(1)} %bitcast.42, bf16[12,84,512]{2,1,0:T(8,128)(2,1)S(1)} %collective-permute-done.other), custom_call_target="tpu_custom_call" | custom-call | tf_op jit(solution)/shard_map/pack_rows/pallas_call | solution.py:192
  18.2 5.3 %collective-permute-start.2 = (bf16[4,84,512]{2,1,0:T(8,128)(2,1)}, bf16[4,84,512]{2,1,0:T(8,128)(2,1)}, u32[]{:S(2)}, u32[]{:S(2)}) collective-permute-start(bf16[4,84,512]{2,1,0:T(8,128)(2,1)} %get-tuple-element.15), channel_id=1, source_target_pairs={{0,6},{1,19},{2,8},{3,21},{4,10},{5,23},{6,12},{7,1},{8,14},{9,3},... | collective-permute-start | bytes 1032200 | tf_op jit(solution)/shard_map/ppermute | solution.py:189
  23.5 3.4 %collective-permute-start.3 = (bf16[4,84,512]{2,1,0:T(8,128)(2,1)}, bf16[4,84,512]{2,1,0:T(8,128)(2,1)}, u32[]{:S(2)}, u32[]{:S(2)}) collective-permute-start(bf16[4,84,512]{2,1,0:T(8,128)(2,1)} %get-tuple-element.16), channel_id=1, source_target_pairs={{0,4},{1,21},{2,6},{3,23},{4,8},{5,1},{6,10},{7,3},{8,12},{9,5},{1... | collective-permute-start | bytes 1032200 | tf_op jit(solution)/shard_map/ppermute | solution.py:189
  26.9 1.9 %collective-permute-start.4 = (bf16[4,84,512]{2,1,0:T(8,128)(2,1)}, bf16[4,84,512]{2,1,0:T(8,128)(2,1)}, u32[]{:S(2)}, u32[]{:S(2)}) collective-permute-start(bf16[4,84,512]{2,1,0:T(8,128)(2,1)} %get-tuple-element.17), channel_id=1, source_target_pairs={{0,2},{1,23},{2,4},{3,1},{4,6},{5,3},{6,8},{7,5},{8,10},{9,7},{10,... | collective-permute-start | bytes 1032200 | tf_op jit(solution)/shard_map/ppermute | solution.py:189
  28.8 1.9 %collective-permute-start.1 = (bf16[2,84,512]{2,1,0:T(8,128)(2,1)}, bf16[2,84,512]{2,1,0:T(8,128)(2,1)S(1)}, u32[]{:S(2)}, u32[]{:S(2)}) collective-permute-start(bf16[2,84,512]{2,1,0:T(8,128)(2,1)} %get-tuple-element.14), channel_id=1, source_target_pairs={{0,8},{1,17},{2,10},{3,19},{4,12},{5,21},{6,14},{7,23},{8,16},{9,1... | collective-permute-start | bytes 516104 | tf_op jit(solution)/shard_map/ppermute | solution.py:189
  30.7 9.7 %all-to-all-start = ((bf16[1,32,256,8]{2,3,0,1:T(8,128)(2,1)}), bf16[1,32,256,8]{2,3,0,1:T(8,128)(2,1)S(1)}, u32[]{:S(2)}, u32[]{:S(2)}) async-start(bf16[1,32,256,8]{2,3,0,1:T(8,128)(2,1)} %bitcast.52), calls=%async_computation | async-start | bytes 262144 | tf_op jit(solution)/shard_map/all_to_all | solution.py:220
  40.4 11.0 %collective-permute-done.1.rest_0_ = bf16[2,84,512]{2,1,0:T(8,128)(2,1)S(1)} collective-permute-done((bf16[2,84,512]{2,1,0:T(8,128)(2,1)}, bf16[2,84,512]{2,1,0:T(8,128)(2,1)S(1)}, u32[]{:S(2)}, u32[]{:S(2)}) %collective-permute-start.1) | collective-permute-done | bytes 172064 | tf_op jit(solution)/shard_map/ppermute | solution.py:189
  51.4 0.0 collective-permute-done.2.rest_1_
  51.4 0.0 collective-permute-done.3.rest_2_
  51.4 2.8 %collective-permute-done.4.rest_3_ = bf16[4,84,512]{2,1,0:T(8,128)(2,1)} collective-permute-done((bf16[4,84,512]{2,1,0:T(8,128)(2,1)}, bf16[4,84,512]{2,1,0:T(8,128)(2,1)}, u32[]{:S(2)}, u32[]{:S(2)}) %collective-permute-start.4) | collective-permute-done | bytes 344096 | tf_op jit(solution)/shard_map/ppermute | solution.py:189
  54.2 2.2 %stop_sums.3 = f32[1,784,128]{2,1,0:T(8,128)S(1)} custom-call(bf16[24,84,512]{2,1,0:T(8,128)(2,1)S(1)} %bitcast.43, bf16[12,84,512]{2,1,0:T(8,128)(2,1)S(1)} %collective-permute-done.other, bf16[2,84,512]{2,1,0:T(8,128)(2,1)S(1)} %collective-permute-done.1.rest_0_, bf16[4,84,512]{2,1,0:T(8,128)(2,1)} %collective-permute-done.2.rest_1_, ...), custom_call_target="tpu_custom_call" | custom-call | tf_op jit(solution)/shard_map/stop_sums/pallas_call | solution.py:200
  56.4 0.7 convert_bitcast_fusion.3
  57.1 0.0 all-to-all-done
  57.1 5.2 %collective-permute-start.5 = (f16[784,128]{1,0:T(8,128)(2,1)}, f16[784,128]{1,0:T(8,128)(2,1)S(1)}, u32[]{:S(2)}, u32[]{:S(2)}) collective-permute-start(f16[784,128]{1,0:T(8,128)(2,1)} %convert_bitcast_fusion.3), channel_id=1, source_target_pairs={{0,4},{1,21},{2,6},{3,23},{4,8},{5,1},{6,10},{7,3},{8,12},{9,5},{1... | collective-permute-start | bytes 602120 | tf_op jit(solution)/shard_map/ppermute | solution.py:189
  62.3 2.1 %stop_sums.4 = f32[1,784,128]{2,1,0:T(8,128)S(1)} custom-call(bf16[24,84,512]{2,1,0:T(8,128)(2,1)S(1)} %bitcast.44, bf16[12,84,512]{2,1,0:T(8,128)(2,1)S(1)} %collective-permute-done.other, bf16[2,84,512]{2,1,0:T(8,128)(2,1)S(1)} %collective-permute-done.1.rest_0_, bf16[4,84,512]{2,1,0:T(8,128)(2,1)} %collective-permute-done.2.rest_1_, ...), custom_call_target="tpu_custom_call" | custom-call | tf_op jit(solution)/shard_map/stop_sums/pallas_call | solution.py:200
  64.4 4.8 %collective-permute-start.7 = (bf16[2,84,512]{2,1,0:T(8,128)(2,1)S(1)}, bf16[2,84,512]{2,1,0:T(8,128)(2,1)S(1)}, u32[]{:S(2)}, u32[]{:S(2)}) collective-permute-start(bf16[2,84,512]{2,1,0:T(8,128)(2,1)S(1)} %get-tuple-element.20), channel_id=1, source_target_pairs={{0,2},{1,23},{2,4},{3,1},{4,6},{5,3},{6,8},{7,5},{8,10},{9,7},{10,... | collective-permute-start | bytes 516104 | tf_op jit(solution)/shard_map/ppermute | solution.py:189
  69.2 2.7 %collective-permute-start.8 = (bf16[2,84,512]{2,1,0:T(8,128)(2,1)S(1)}, bf16[2,84,512]{2,1,0:T(8,128)(2,1)S(1)}, u32[]{:S(2)}, u32[]{:S(2)}) collective-permute-start(bf16[2,84,512]{2,1,0:T(8,128)(2,1)S(1)} %get-tuple-element.21), channel_id=1, source_target_pairs={{0,3},{1,22},{2,5},{3,0},{4,7},{5,2},{6,9},{7,4},{8,11},{9,6},{10,... | collective-permute-start | bytes 516104 | tf_op jit(solution)/shard_map/ppermute | solution.py:189
  71.9 4.0 %collective-permute-start.6 = (f16[784,128]{1,0:T(8,128)(2,1)S(1)}, f16[784,128]{1,0:T(8,128)(2,1)S(1)}, u32[]{:S(2)}, u32[]{:S(2)}) collective-permute-start(f16[784,128]{1,0:T(8,128)(2,1)S(1)} %convert_bitcast_fusion.2), channel_id=1, source_target_pairs={{0,5},{1,20},{2,7},{3,22},{4,9},{5,0},{6,11},{7,2},{8,13},{9,4},{1... | collective-permute-start | bytes 602120 | tf_op jit(solution)/shard_map/ppermute | solution.py:189
  75.9 0.0 collective-permute-done.7.rest_0_
  75.9 1.4 %collective-permute-done.8.rest_1_ = bf16[2,84,512]{2,1,0:T(8,128)(2,1)S(1)} collective-permute-done((bf16[2,84,512]{2,1,0:T(8,128)(2,1)S(1)}, bf16[2,84,512]{2,1,0:T(8,128)(2,1)S(1)}, u32[]{:S(2)}, u32[]{:S(2)}) %collective-permute-start.8) | collective-permute-done | bytes 172064 | tf_op jit(solution)/shard_map/ppermute | solution.py:189
  77.4 0.7 stop_sums.5
  78.1 0.0 copy-start
  78.1 0.0 copy-start.1
  78.1 0.0 copy-start.2
  78.1 0.0 copy-start.3
  78.1 0.0 copy-start.4
  78.1 0.0 collective-permute-done.5
  78.2 3.9 %collective-permute-done.6 = f16[784,128]{1,0:T(8,128)(2,1)S(1)} collective-permute-done((f16[784,128]{1,0:T(8,128)(2,1)S(1)}, f16[784,128]{1,0:T(8,128)(2,1)S(1)}, u32[]{:S(2)}, u32[]{:S(2)}) %collective-permute-start.6) | collective-permute-done | bytes 200736 | tf_op jit(solution)/shard_map/ppermute | solution.py:189
  82.1 0.2 fusion.3.sums
  82.3 0.0 copy-done
  82.4 0.0 copy-done.1
  82.4 0.0 copy-done.2
  82.4 0.0 copy-done.3
  82.4 0.0 copy-done.4
  82.4 1.8 %residual.1 = f32[256,256]{1,0:T(8,128)} custom-call(s32[2]{0:T(128)S(1)} %bitcast.49, s32[2]{0:T(128)S(1)} %bitcast.50, s32[2]{0:T(128)S(1)} %bitcast.51, f32[100]{0:T(128)S(1)} %copy-done.4, f32[12,128]{1,0:T(8,128)S(1)} %bitcast.48, f32[784,128]{1,0:T(8,128)S(1)} %fusion.3.sums, bf16[256,256]{1,0:T(8,128)(2,1)S(1)} %bitcast.47), custom_call_target="tpu_custom_call" | custom-call | tf_op jit(solution)/shard_map/residual/pallas_call | solution.py:240
  (7 shorter events, 0.2 us)
Async XLA Ops:
  2.4 14.7 %collective-permute-start = (bf16[12,84,512]{2,1,0:T(8,128)(2,1)S(1)}, bf16[12,84,512]{2,1,0:T(8,128)(2,1)S(1)}, u32[]{:S(2)}, u32[]{:S(2)}) collective-permute-start(bf16[12,84,512]{2,1,0:T(8,128)(2,1)S(1)} %split_cores.1), channel_id=1, source_target_pairs={{0,1},{1,0},{2,3},{3,2},{4,5},{5,4},{6,7},{7,6},{8,9},{9,8},{10,11... | collective-permute-start | bytes 3096584 | tf_op jit(solution)/shard_map/ppermute | solution.py:215
  18.2 33.2 %collective-permute-start.2 = (bf16[4,84,512]{2,1,0:T(8,128)(2,1)}, bf16[4,84,512]{2,1,0:T(8,128)(2,1)}, u32[]{:S(2)}, u32[]{:S(2)}) collective-permute-start(bf16[4,84,512]{2,1,0:T(8,128)(2,1)} %get-tuple-element.15), channel_id=1, source_target_pairs={{0,6},{1,19},{2,8},{3,21},{4,10},{5,23},{6,12},{7,1},{8,14},{9,3},... | collective-permute-start | bytes 1032200 | tf_op jit(solution)/shard_map/ppermute | solution.py:189
  23.5 27.9 %collective-permute-start.3 = (bf16[4,84,512]{2,1,0:T(8,128)(2,1)}, bf16[4,84,512]{2,1,0:T(8,128)(2,1)}, u32[]{:S(2)}, u32[]{:S(2)}) collective-permute-start(bf16[4,84,512]{2,1,0:T(8,128)(2,1)} %get-tuple-element.16), channel_id=1, source_target_pairs={{0,4},{1,21},{2,6},{3,23},{4,8},{5,1},{6,10},{7,3},{8,12},{9,5},{1... | collective-permute-start | bytes 1032200 | tf_op jit(solution)/shard_map/ppermute | solution.py:189
  26.9 27.3 %collective-permute-start.4 = (bf16[4,84,512]{2,1,0:T(8,128)(2,1)}, bf16[4,84,512]{2,1,0:T(8,128)(2,1)}, u32[]{:S(2)}, u32[]{:S(2)}) collective-permute-start(bf16[4,84,512]{2,1,0:T(8,128)(2,1)} %get-tuple-element.17), channel_id=1, source_target_pairs={{0,2},{1,23},{2,4},{3,1},{4,6},{5,3},{6,8},{7,5},{8,10},{9,7},{10,... | collective-permute-start | bytes 1032200 | tf_op jit(solution)/shard_map/ppermute | solution.py:189
  28.8 22.6 %collective-permute-start.1 = (bf16[2,84,512]{2,1,0:T(8,128)(2,1)}, bf16[2,84,512]{2,1,0:T(8,128)(2,1)S(1)}, u32[]{:S(2)}, u32[]{:S(2)}) collective-permute-start(bf16[2,84,512]{2,1,0:T(8,128)(2,1)} %get-tuple-element.14), channel_id=1, source_target_pairs={{0,8},{1,17},{2,10},{3,19},{4,12},{5,21},{6,14},{7,23},{8,16},{9,1... | collective-permute-start | bytes 516104 | tf_op jit(solution)/shard_map/ppermute | solution.py:189
  30.7 26.4 %all-to-all-start = ((bf16[1,32,256,8]{2,3,0,1:T(8,128)(2,1)}), bf16[1,32,256,8]{2,3,0,1:T(8,128)(2,1)S(1)}, u32[]{:S(2)}, u32[]{:S(2)}) async-start(bf16[1,32,256,8]{2,3,0,1:T(8,128)(2,1)} %bitcast.52), calls=%async_computation | async-start | bytes 262144 | tf_op jit(solution)/shard_map/all_to_all | solution.py:220
  57.1 21.0 %collective-permute-start.5 = (f16[784,128]{1,0:T(8,128)(2,1)}, f16[784,128]{1,0:T(8,128)(2,1)S(1)}, u32[]{:S(2)}, u32[]{:S(2)}) collective-permute-start(f16[784,128]{1,0:T(8,128)(2,1)} %convert_bitcast_fusion.3), channel_id=1, source_target_pairs={{0,4},{1,21},{2,6},{3,23},{4,8},{5,1},{6,10},{7,3},{8,12},{9,5},{1... | collective-permute-start | bytes 602120 | tf_op jit(solution)/shard_map/ppermute | solution.py:189
  64.4 11.5 %collective-permute-start.7 = (bf16[2,84,512]{2,1,0:T(8,128)(2,1)S(1)}, bf16[2,84,512]{2,1,0:T(8,128)(2,1)S(1)}, u32[]{:S(2)}, u32[]{:S(2)}) collective-permute-start(bf16[2,84,512]{2,1,0:T(8,128)(2,1)S(1)} %get-tuple-element.20), channel_id=1, source_target_pairs={{0,2},{1,23},{2,4},{3,1},{4,6},{5,3},{6,8},{7,5},{8,10},{9,7},{10,... | collective-permute-start | bytes 516104 | tf_op jit(solution)/shard_map/ppermute | solution.py:189
  69.2 8.2 %collective-permute-start.8 = (bf16[2,84,512]{2,1,0:T(8,128)(2,1)S(1)}, bf16[2,84,512]{2,1,0:T(8,128)(2,1)S(1)}, u32[]{:S(2)}, u32[]{:S(2)}) collective-permute-start(bf16[2,84,512]{2,1,0:T(8,128)(2,1)S(1)} %get-tuple-element.21), channel_id=1, source_target_pairs={{0,3},{1,22},{2,5},{3,0},{4,7},{5,2},{6,9},{7,4},{8,11},{9,6},{10,... | collective-permute-start | bytes 516104 | tf_op jit(solution)/shard_map/ppermute | solution.py:189
  71.9 10.1 %collective-permute-start.6 = (f16[784,128]{1,0:T(8,128)(2,1)S(1)}, f16[784,128]{1,0:T(8,128)(2,1)S(1)}, u32[]{:S(2)}, u32[]{:S(2)}) collective-permute-start(f16[784,128]{1,0:T(8,128)(2,1)S(1)} %convert_bitcast_fusion.2), channel_id=1, source_target_pairs={{0,5},{1,20},{2,7},{3,22},{4,9},{5,0},{6,11},{7,2},{8,13},{9,4},{1... | collective-permute-start | bytes 602120 | tf_op jit(solution)/shard_map/ppermute | solution.py:189
  78.1 4.3 %copy-start = (f32[1536]{0:T(1024)S(1)}, f32[1536]{0:T(1024)}, u32[]{:S(2)}) copy-start(f32[1536]{0:T(1024)} %param.12) | copy-start | bytes 18436
  78.1 4.3 %copy-start.1 = (s32[1,1,2]{2,1,0:T(1,128)S(1)}, s32[1,1,2]{2,1,0:T(1,128)}, u32[]{:S(2)}) copy-start(s32[1,1,2]{2,1,0:T(1,128)} %param.9) | copy-start | bytes 28
  78.1 4.3 %copy-start.2 = (s32[1,1,2]{2,1,0:T(1,128)S(1)}, s32[1,1,2]{2,1,0:T(1,128)}, u32[]{:S(2)}) copy-start(s32[1,1,2]{2,1,0:T(1,128)} %param.10) | copy-start | bytes 28
  78.1 4.3 %copy-start.3 = (s32[1,1,2]{2,1,0:T(1,128)S(1)}, s32[1,1,2]{2,1,0:T(1,128)}, u32[]{:S(2)}) copy-start(s32[1,1,2]{2,1,0:T(1,128)} %param.11) | copy-start | bytes 28
  78.1 4.3 %copy-start.4 = (f32[100]{0:T(128)S(1)}, f32[100]{0:T(128)}, u32[]{:S(2)}) copy-start(f32[100]{0:T(128)} %occ.1) | copy-start | bytes 1204

commit v9 on v8

--- a/solution.py
+++ b/solution.py
@@ -118,13 +118,13 @@
 
 
 def stop_kernel(chips, stop, owners, picks, scaled, ints, other, *rest):
-    received, out = rest[:-1], rest[-1]
+    received, outs = rest[: -len(owners)], rest[-len(owners) :]
     for n, mine in enumerate(owners):
         blocks = chip_rows(chips, ints, other, stop, mine)
         for at, ref in picks:
             if at[n] is not None:
                 blocks += [received[ref][at[n]], received[ref][at[n] + 1]]
-        packed_sum(blocks, out.at[n], scaled)
+        packed_sum(blocks, outs[n], scaled)
 
 
 def final_kernel(occ_at, tiles, mask, occ, virt, sums, amps_t, out):
@@ -143,7 +143,7 @@
     tt = amps_t[...]
     total = h
     rest = g
-    for _ in range(3):
+    for _ in range(2):
         piece = rest.astype(BF16)
         rest = rest - piece.astype(F32)
         total = total - lax.dot_general(
@@ -200,9 +200,9 @@
         return call(
             functools.partial(stop_kernel, chips, stop, owners, picks, scaled),
             2 + len(received),
-            [((len(owners), ROWS, TILE), F32)],
+            [((ROWS, TILE), F32)] * len(owners),
             "stop_sums",
-        )(ints, other, *received)[0]
+        )(ints, other, *received)
 
     def pairs_at(d):
         return [(d, True)] if d == far else [(d, True), (d, False)]
@@ -220,12 +220,11 @@
     owned = lax.all_to_all(amplitudes, "pair", split_axis=1, concat_axis=3, tiled=True)
 
     picks = [((0, None) if d == far else (0, 2), at) for at, d in enumerate(to_stop)]
+    both = stop_sums(STOP, (True, False), picks, True, other, rows)
+    both, owned = lax.optimization_barrier((both, owned))
     moving = []
-    for n, mine in enumerate((True, False)):
-        x = stop_sums(STOP, (mine,), [((at[n],), ref) for at, ref in picks], True, other, rows)
-        x = x[0].astype(F16)
-        if n == 0:
-            x, owned = lax.optimization_barrier((x, owned))
+    for n in range(2):
+        x = both[n].astype(F16)
         moving.append(permute(x, STOP, n == 1))
 
     gate = lax.optimization_barrier((other, x))[0]
@@ -233,8 +232,9 @@
     sends = pack([[(d, n == 0)] for d, n in to_owner], gate)
     rows = [permute(x, d, n == 1) for (d, n), x in zip(to_owner, sends)]
     picks = [((0,), at) for at in range(len(rows))]
+    gate, *moving = lax.optimization_barrier((gate, *moving))
     local = stop_sums(0, (True,), picks, False, gate, rows)
-    sums = (decode(moving[0][None])[0] + decode(moving[1][None])[0] + local)[0]
+    sums = decode(moving[0][None])[0][0] + decode(moving[1][None])[0][0] + local[0]
     amps_t = jnp.swapaxes(owned[0, 0], 0, 1)
 
     (out,) = call(final_kernel, 3, [((2 * TILE, 2 * TILE), F32)], "residual", 4)(

time: 84.6 us -> 87.4 us (1.033)
  Pallas kernels: 7.94 us -> 6.35 us
  local copies, waits for them, and re-layouts: 2.28 us -> 3.77 us
  other arithmetic: 1.04 us -> 2.37 us
  starting transfers between devices: 51.2 us -> 52.1 us
    pallas_call x3 -> x2, Pallas kernels: 4.93 us -> 3.44 us  [stop_sums(): call(functools.partial(stop_kernel, chips, stop, owners, picks, scaled),...]
    unnamed x11 -> x15, local copies, waits for them, and re-layouts: 2.28 us -> 3.77 us
    convert_element_type x2, other arithmetic: 0.74 us -> 2.06 us  [on_device(): x = both[n].astype(F16)]
    ppermute x8, starting transfers between devices: 29.1 us -> 30 us  [permute(): return lax.ppermute(x, 'aux', pairs)]
  transfers between devices with their start and end apart: 10 -> 10, of which waited for: 5 -> 5; matrix products, arithmetic and copies ran while one was open for 1% -> 1% of each run, Pallas kernels for 6% -> 3%
where the time goes in v9:
time: 87.4 us; the launch traced here: 86.9 us
  starting transfers between devices  52.1 us (60%)
  waiting for transfers between devices  22 us (25%)
  Pallas kernels  6.35 us (7%)
  local copies, waits for them, and re-layouts  3.77 us (4%)
  other arithmetic  2.37 us (3%)
    ppermute x8, starting transfers between devices, permute(): return lax.ppermute(x, 'aux', pairs)  30 us
    ppermute x8, waiting for transfers between devices, permute(): return lax.ppermute(x, 'aux', pairs)  19.7 us
    ppermute x1, starting transfers between devices, on_device(): other = lax.ppermute(other, 'aux', [(i, i ^ 1) for i in range(2 * chips)])  12.4 us
    all_to_all x1, starting transfers between devices, on_device(): lax.all_to_all(amplitudes, 'pair', split_axis=1, concat_axis=3, tiled=True)  9.68 us
    unnamed x15, local copies, waits for them, and re-layouts  3.77 us
    pallas_call x2, Pallas kernels, stop_sums(): call(functools.partial(stop_kernel, chips, stop, owners, picks, scaled),...  3.44 us
    ppermute x1, waiting for transfers between devices, on_device(): other = lax.ppermute(other, 'aux', [(i, i ^ 1) for i in range(2 * chips)])  2.31 us
    convert_element_type x2, other arithmetic, on_device(): x = both[n].astype(F16)  2.06 us
  transfers between devices with their start and end apart: 10, of which 5 were waited for; matrix products, arithmetic and copies ran while one was open for 1% of the time, Pallas kernels for 3%

profile of v9, /device:TPU:1, one launch (start us, length us, event | category | flops | bytes accessed | tf_op | source)
XLA Modules:
  0.0 86.9 jit_solution(15718277157962883425)
XLA Ops:
  0.0 2.3 %copy.12 = bf16[24,1,84,512]{3,2,0,1:T(8,128)(2,1)S(1)} copy(bf16[24,1,84,512]{3,0,2,1:T(8,128)(2,1)} %param.8) | data formatting | bytes 4128768 | tf_op args[1]
  2.3 0.1 split_cores.1
  2.4 12.4 %collective-permute-start = (bf16[12,84,512]{2,1,0:T(8,128)(2,1)S(1)}, bf16[12,84,512]{2,1,0:T(8,128)(2,1)S(1)}, u32[]{:S(2)}, u32[]{:S(2)}) collective-permute-start(bf16[12,84,512]{2,1,0:T(8,128)(2,1)S(1)} %split_cores.1), channel_id=1, source_target_pairs={{0,1},{1,0},{2,3},{3,2},{4,5},{5,4},{6,7},{7,6},{8,9},{9,8},{10,11... | collective-permute-start | bytes 3096584 | tf_op jit(solution)/shard_map/ppermute | solution.py:215
  14.8 2.3 %collective-permute-done.other = bf16[12,84,512]{2,1,0:T(8,128)(2,1)S(1)} collective-permute-done((bf16[12,84,512]{2,1,0:T(8,128)(2,1)S(1)}, bf16[12,84,512]{2,1,0:T(8,128)(2,1)S(1)}, u32[]{:S(2)}, u32[]{:S(2)}) %collective-permute-start) | collective-permute-done | bytes 1032224 | tf_op jit(solution)/shard_map/ppermute | solution.py:215
  17.1 1.1 %pack_rows.2 = (bf16[2,84,512]{2,1,0:T(8,128)(2,1)S(1)}, bf16[4,84,512]{2,1,0:T(8,128)(2,1)}, bf16[4,84,512]{2,1,0:T(8,128)(2,1)}, bf16[4,84,512]{2,1,0:T(8,128)(2,1)}) custom-call(bf16[24,84,512]{2,1,0:T(8,128)(2,1)S(1)} %bitcast.30, bf16[12,84,512]{2,1,0:T(8,128)(2,1)S(1)} %collective-permute-done.other), custom_call_target="tpu_custom_call" | custom-call | tf_op jit(solution)/shard_map/pack_rows/pallas_call | solution.py:192
  18.2 5.3 %collective-permute-start.2 = (bf16[4,84,512]{2,1,0:T(8,128)(2,1)}, bf16[4,84,512]{2,1,0:T(8,128)(2,1)}, u32[]{:S(2)}, u32[]{:S(2)}) collective-permute-start(bf16[4,84,512]{2,1,0:T(8,128)(2,1)} %get-tuple-element.21), channel_id=1, source_target_pairs={{0,6},{1,19},{2,8},{3,21},{4,10},{5,23},{6,12},{7,1},{8,14},{9,3},... | collective-permute-start | bytes 1032200 | tf_op jit(solution)/shard_map/ppermute | solution.py:189
  23.5 3.4 %collective-permute-start.3 = (bf16[4,84,512]{2,1,0:T(8,128)(2,1)}, bf16[4,84,512]{2,1,0:T(8,128)(2,1)}, u32[]{:S(2)}, u32[]{:S(2)}) collective-permute-start(bf16[4,84,512]{2,1,0:T(8,128)(2,1)} %get-tuple-element.22), channel_id=1, source_target_pairs={{0,4},{1,21},{2,6},{3,23},{4,8},{5,1},{6,10},{7,3},{8,12},{9,5},{1... | collective-permute-start | bytes 1032200 | tf_op jit(solution)/shard_map/ppermute | solution.py:189
  26.9 1.9 %collective-permute-start.4 = (bf16[4,84,512]{2,1,0:T(8,128)(2,1)}, bf16[4,84,512]{2,1,0:T(8,128)(2,1)}, u32[]{:S(2)}, u32[]{:S(2)}) collective-permute-start(bf16[4,84,512]{2,1,0:T(8,128)(2,1)} %get-tuple-element.23), channel_id=1, source_target_pairs={{0,2},{1,23},{2,4},{3,1},{4,6},{5,3},{6,8},{7,5},{8,10},{9,7},{10,... | collective-permute-start | bytes 1032200 | tf_op jit(solution)/shard_map/ppermute | solution.py:189
  28.8 9.7 %all-to-all-start = ((bf16[1,32,256,8]{2,3,0,1:T(8,128)(2,1)}), bf16[1,32,256,8]{2,3,0,1:T(8,128)(2,1)S(1)}, u32[]{:S(2)}, u32[]{:S(2)}) async-start(bf16[1,32,256,8]{2,3,0,1:T(8,128)(2,1)} %bitcast.39), calls=%async_computation | async-start | bytes 262144 | tf_op jit(solution)/shard_map/all_to_all | solution.py:220
  38.5 1.9 %collective-permute-start.1 = (bf16[2,84,512]{2,1,0:T(8,128)(2,1)S(1)}, bf16[2,84,512]{2,1,0:T(8,128)(2,1)S(1)}, u32[]{:S(2)}, u32[]{:S(2)}) collective-permute-start(bf16[2,84,512]{2,1,0:T(8,128)(2,1)S(1)} %get-tuple-element.20), channel_id=1, source_target_pairs={{0,8},{1,17},{2,10},{3,19},{4,12},{5,21},{6,14},{7,23},{8,16},{9,1... | collective-permute-start | bytes 516104 | tf_op jit(solution)/shard_map/ppermute | solution.py:189
  40.4 12.8 %collective-permute-done.1.rest_0_ = bf16[2,84,512]{2,1,0:T(8,128)(2,1)S(1)} collective-permute-done((bf16[2,84,512]{2,1,0:T(8,128)(2,1)S(1)}, bf16[2,84,512]{2,1,0:T(8,128)(2,1)S(1)}, u32[]{:S(2)}, u32[]{:S(2)}) %collective-permute-start.1) | collective-permute-done | bytes 172064 | tf_op jit(solution)/shard_map/ppermute | solution.py:189
  53.2 0.0 collective-permute-done.2.rest_1_
  53.2 0.0 collective-permute-done.3.rest_2_
  53.2 1.0 %collective-permute-done.4.rest_3_ = bf16[4,84,512]{2,1,0:T(8,128)(2,1)} collective-permute-done((bf16[4,84,512]{2,1,0:T(8,128)(2,1)}, bf16[4,84,512]{2,1,0:T(8,128)(2,1)}, u32[]{:S(2)}, u32[]{:S(2)}) %collective-permute-start.4) | collective-permute-done | bytes 344096 | tf_op jit(solution)/shard_map/ppermute | solution.py:189
  54.2 2.8 %stop_sums.2 = (f32[784,128]{1,0:T(8,128)S(1)}, f32[784,128]{1,0:T(8,128)S(1)}) custom-call(bf16[24,84,512]{2,1,0:T(8,128)(2,1)S(1)} %bitcast.31, bf16[12,84,512]{2,1,0:T(8,128)(2,1)S(1)} %collective-permute-done.other, bf16[2,84,512]{2,1,0:T(8,128)(2,1)S(1)} %collective-permute-done.1.rest_0_, bf16[4,84,512]{2,1,0:T(8,128)(2,1)} %collective-permute-done.2.rest_1_, ...), custom_call_target="tpu_custom_call" | custom-call | tf_op jit(solution)/shard_map/stop_sums/pallas_call | solution.py:200
  56.9 0.0 copy-start
  57.0 0.7 copy-done
  57.7 0.0 copy-start.1
  57.7 0.7 copy-done.1
  58.4 0.0 all-to-all-done
  58.4 1.0 %convert_element_type.19 = f16[784,128]{1,0:T(8,128)(2,1)S(1)} convert(f32[784,128]{1,0:T(8,128)} %copy-done.1) | non-fusion elementwise | flops 100352 | bytes 602112 | tf_op jit(solution)/shard_map/convert_element_type | solution.py:227
  59.5 3.4 %collective-permute-start.5 = (f16[784,128]{1,0:T(8,128)(2,1)S(1)}, f16[784,128]{1,0:T(8,128)(2,1)S(1)}, u32[]{:S(2)}, u32[]{:S(2)}) collective-permute-start(f16[784,128]{1,0:T(8,128)(2,1)S(1)} %convert_element_type.19), channel_id=1, source_target_pairs={{0,4},{1,21},{2,6},{3,23},{4,8},{5,1},{6,10},{7,3},{8,12},{9,5},{1... | collective-permute-start | bytes 602120 | tf_op jit(solution)/shard_map/ppermute | solution.py:189
  62.9 1.0 %convert_element_type.18 = f16[784,128]{1,0:T(8,128)(2,1)S(1)} convert(f32[784,128]{1,0:T(8,128)} %copy-done) | non-fusion elementwise | flops 100352 | bytes 602112 | tf_op jit(solution)/shard_map/convert_element_type | solution.py:227
  63.9 6.9 %collective-permute-start.6 = (f16[784,128]{1,0:T(8,128)(2,1)S(1)}, f16[784,128]{1,0:T(8,128)(2,1)S(1)}, u32[]{:S(2)}, u32[]{:S(2)}) collective-permute-start(f16[784,128]{1,0:T(8,128)(2,1)S(1)} %convert_element_type.18), channel_id=1, source_target_pairs={{0,5},{1,20},{2,7},{3,22},{4,9},{5,0},{6,11},{7,2},{8,13},{9,4},{1... | collective-permute-start | bytes 602120 | tf_op jit(solution)/shard_map/ppermute | solution.py:189
  70.9 5.3 %collective-permute-start.7 = (bf16[2,84,512]{2,1,0:T(8,128)(2,1)S(1)}, bf16[2,84,512]{2,1,0:T(8,128)(2,1)S(1)}, u32[]{:S(2)}, u32[]{:S(2)}) collective-permute-start(bf16[2,84,512]{2,1,0:T(8,128)(2,1)S(1)} %get-tuple-element.32), channel_id=1, source_target_pairs={{0,2},{1,23},{2,4},{3,1},{4,6},{5,3},{6,8},{7,5},{8,10},{9,7},{10,... | collective-permute-start | bytes 516104 | tf_op jit(solution)/shard_map/ppermute | solution.py:189
  76.2 1.9 %collective-permute-start.8 = (bf16[2,84,512]{2,1,0:T(8,128)(2,1)S(1)}, bf16[2,84,512]{2,1,0:T(8,128)(2,1)S(1)}, u32[]{:S(2)}, u32[]{:S(2)}) collective-permute-start(bf16[2,84,512]{2,1,0:T(8,128)(2,1)S(1)} %get-tuple-element.33), channel_id=1, source_target_pairs={{0,3},{1,22},{2,5},{3,0},{4,7},{5,2},{6,9},{7,4},{8,11},{9,6},{10,... | collective-permute-start | bytes 516104 | tf_op jit(solution)/shard_map/ppermute | solution.py:189
  78.1 0.0 collective-permute-done.5
  78.2 0.0 collective-permute-done.6
  78.2 0.1 convert_bitcast_fusion
  78.3 0.0 copy-start.2
  78.3 0.0 copy-start.3
  78.3 0.0 copy-start.4
  78.3 0.0 copy-start.5
  78.3 0.0 copy-start.6
  78.3 0.3 collective-permute-done.7.rest_0_
  78.6 5.6 %collective-permute-done.8.rest_1_ = bf16[2,84,512]{2,1,0:T(8,128)(2,1)S(1)} collective-permute-done((bf16[2,84,512]{2,1,0:T(8,128)(2,1)S(1)}, bf16[2,84,512]{2,1,0:T(8,128)(2,1)S(1)}, u32[]{:S(2)}, u32[]{:S(2)}) %collective-permute-start.8) | collective-permute-done | bytes 172064 | tf_op jit(solution)/shard_map/ppermute | solution.py:189
  84.2 0.7 stop_sums.3
  84.9 0.2 fusion.1.sums
  85.2 0.0 copy-done.2
  85.2 0.0 copy-done.3
  85.2 0.0 copy-done.4
  85.2 0.0 copy-done.5
  85.2 0.0 copy-done.6
  85.2 1.7 %residual.1 = f32[256,256]{1,0:T(8,128)} custom-call(s32[2]{0:T(128)S(1)} %bitcast.36, s32[2]{0:T(128)S(1)} %bitcast.37, s32[2]{0:T(128)S(1)} %bitcast.38, f32[100]{0:T(128)S(1)} %copy-done.6, f32[12,128]{1,0:T(8,128)S(1)} %bitcast.35, f32[784,128]{1,0:T(8,128)S(1)} %fusion.1.sums, bf16[256,256]{1,0:T(8,128)(2,1)S(1)} %bitcast.34), custom_call_target="tpu_custom_call" | custom-call | tf_op jit(solution)/shard_map/residual/pallas_call | solution.py:240
  (4 shorter events, 0.1 us)
Async XLA Ops:
  2.4 14.7 %collective-permute-start = (bf16[12,84,512]{2,1,0:T(8,128)(2,1)S(1)}, bf16[12,84,512]{2,1,0:T(8,128)(2,1)S(1)}, u32[]{:S(2)}, u32[]{:S(2)}) collective-permute-start(bf16[12,84,512]{2,1,0:T(8,128)(2,1)S(1)} %split_cores.1), channel_id=1, source_target_pairs={{0,1},{1,0},{2,3},{3,2},{4,5},{5,4},{6,7},{7,6},{8,9},{9,8},{10,11... | collective-permute-start | bytes 3096584 | tf_op jit(solution)/shard_map/ppermute | solution.py:215
  18.2 35.0 %collective-permute-start.2 = (bf16[4,84,512]{2,1,0:T(8,128)(2,1)}, bf16[4,84,512]{2,1,0:T(8,128)(2,1)}, u32[]{:S(2)}, u32[]{:S(2)}) collective-permute-start(bf16[4,84,512]{2,1,0:T(8,128)(2,1)} %get-tuple-element.21), channel_id=1, source_target_pairs={{0,6},{1,19},{2,8},{3,21},{4,10},{5,23},{6,12},{7,1},{8,14},{9,3},... | collective-permute-start | bytes 1032200 | tf_op jit(solution)/shard_map/ppermute | solution.py:189
  23.5 29.7 %collective-permute-start.3 = (bf16[4,84,512]{2,1,0:T(8,128)(2,1)}, bf16[4,84,512]{2,1,0:T(8,128)(2,1)}, u32[]{:S(2)}, u32[]{:S(2)}) collective-permute-start(bf16[4,84,512]{2,1,0:T(8,128)(2,1)} %get-tuple-element.22), channel_id=1, source_target_pairs={{0,4},{1,21},{2,6},{3,23},{4,8},{5,1},{6,10},{7,3},{8,12},{9,5},{1... | collective-permute-start | bytes 1032200 | tf_op jit(solution)/shard_map/ppermute | solution.py:189
  26.9 27.3 %collective-permute-start.4 = (bf16[4,84,512]{2,1,0:T(8,128)(2,1)}, bf16[4,84,512]{2,1,0:T(8,128)(2,1)}, u32[]{:S(2)}, u32[]{:S(2)}) collective-permute-start(bf16[4,84,512]{2,1,0:T(8,128)(2,1)} %get-tuple-element.23), channel_id=1, source_target_pairs={{0,2},{1,23},{2,4},{3,1},{4,6},{5,3},{6,8},{7,5},{8,10},{9,7},{10,... | collective-permute-start | bytes 1032200 | tf_op jit(solution)/shard_map/ppermute | solution.py:189
  28.8 29.6 %all-to-all-start = ((bf16[1,32,256,8]{2,3,0,1:T(8,128)(2,1)}), bf16[1,32,256,8]{2,3,0,1:T(8,128)(2,1)S(1)}, u32[]{:S(2)}, u32[]{:S(2)}) async-start(bf16[1,32,256,8]{2,3,0,1:T(8,128)(2,1)} %bitcast.39), calls=%async_computation | async-start | bytes 262144 | tf_op jit(solution)/shard_map/all_to_all | solution.py:220
  38.5 14.7 %collective-permute-start.1 = (bf16[2,84,512]{2,1,0:T(8,128)(2,1)S(1)}, bf16[2,84,512]{2,1,0:T(8,128)(2,1)S(1)}, u32[]{:S(2)}, u32[]{:S(2)}) collective-permute-start(bf16[2,84,512]{2,1,0:T(8,128)(2,1)S(1)} %get-tuple-element.20), channel_id=1, source_target_pairs={{0,8},{1,17},{2,10},{3,19},{4,12},{5,21},{6,14},{7,23},{8,16},{9,1... | collective-permute-start | bytes 516104 | tf_op jit(solution)/shard_map/ppermute | solution.py:189
  56.9 0.7 copy-start
  57.7 0.7 copy-start.1
  59.5 18.7 %collective-permute-start.5 = (f16[784,128]{1,0:T(8,128)(2,1)S(1)}, f16[784,128]{1,0:T(8,128)(2,1)S(1)}, u32[]{:S(2)}, u32[]{:S(2)}) collective-permute-start(f16[784,128]{1,0:T(8,128)(2,1)S(1)} %convert_element_type.19), channel_id=1, source_target_pairs={{0,4},{1,21},{2,6},{3,23},{4,8},{5,1},{6,10},{7,3},{8,12},{9,5},{1... | collective-permute-start | bytes 602120 | tf_op jit(solution)/shard_map/ppermute | solution.py:189
  63.9 14.3 %collective-permute-start.6 = (f16[784,128]{1,0:T(8,128)(2,1)S(1)}, f16[784,128]{1,0:T(8,128)(2,1)S(1)}, u32[]{:S(2)}, u32[]{:S(2)}) collective-permute-start(f16[784,128]{1,0:T(8,128)(2,1)S(1)} %convert_element_type.18), channel_id=1, source_target_pairs={{0,5},{1,20},{2,7},{3,22},{4,9},{5,0},{6,11},{7,2},{8,13},{9,4},{1... | collective-permute-start | bytes 602120 | tf_op jit(solution)/shard_map/ppermute | solution.py:189
  70.9 7.8 %collective-permute-start.7 = (bf16[2,84,512]{2,1,0:T(8,128)(2,1)S(1)}, bf16[2,84,512]{2,1,0:T(8,128)(2,1)S(1)}, u32[]{:S(2)}, u32[]{:S(2)}) collective-permute-start(bf16[2,84,512]{2,1,0:T(8,128)(2,1)S(1)} %get-tuple-element.32), channel_id=1, source_target_pairs={{0,2},{1,23},{2,4},{3,1},{4,6},{5,3},{6,8},{7,5},{8,10},{9,7},{10,... | collective-permute-start | bytes 516104 | tf_op jit(solution)/shard_map/ppermute | solution.py:189
  76.2 8.0 %collective-permute-start.8 = (bf16[2,84,512]{2,1,0:T(8,128)(2,1)S(1)}, bf16[2,84,512]{2,1,0:T(8,128)(2,1)S(1)}, u32[]{:S(2)}, u32[]{:S(2)}) collective-permute-start(bf16[2,84,512]{2,1,0:T(8,128)(2,1)S(1)} %get-tuple-element.33), channel_id=1, source_target_pairs={{0,3},{1,22},{2,5},{3,0},{4,7},{5,2},{6,9},{7,4},{8,11},{9,6},{10,... | collective-permute-start | bytes 516104 | tf_op jit(solution)/shard_map/ppermute | solution.py:189
  78.3 6.9 %copy-start.2 = (f32[1536]{0:T(1024)S(1)}, f32[1536]{0:T(1024)}, u32[]{:S(2)}) copy-start(f32[1536]{0:T(1024)} %param.12) | copy-start | bytes 18436
  78.3 6.9 %copy-start.3 = (s32[1,1,2]{2,1,0:T(1,128)S(1)}, s32[1,1,2]{2,1,0:T(1,128)}, u32[]{:S(2)}) copy-start(s32[1,1,2]{2,1,0:T(1,128)} %param.9) | copy-start | bytes 28
  78.3 6.9 %copy-start.4 = (s32[1,1,2]{2,1,0:T(1,128)S(1)}, s32[1,1,2]{2,1,0:T(1,128)}, u32[]{:S(2)}) copy-start(s32[1,1,2]{2,1,0:T(1,128)} %param.10) | copy-start | bytes 28
  78.3 6.9 %copy-start.5 = (s32[1,1,2]{2,1,0:T(1,128)S(1)}, s32[1,1,2]{2,1,0:T(1,128)}, u32[]{:S(2)}) copy-start(s32[1,1,2]{2,1,0:T(1,128)} %param.11) | copy-start | bytes 28
  78.3 6.9 %copy-start.6 = (f32[100]{0:T(128)S(1)}, f32[100]{0:T(128)}, u32[]{:S(2)}) copy-start(f32[100]{0:T(128)} %occ.1) | copy-start | bytes 1204

commit v10 on v5

--- a/solution.py
+++ b/solution.py
@@ -152,7 +152,7 @@
     tt = amps_t[...]
     total = h
     rest = g
-    for _ in range(3):
+    for _ in range(2):
         piece = rest.astype(BF16)
         rest = rest - piece.astype(F32)
         total = total - lax.dot_general(
@@ -225,29 +225,29 @@
 
     to_first = list(range(far, FIRST, -1))
     to_second = list(range(FIRST - 1, SECOND, -1))
-    to_owner = list(range(SECOND - 1, 0, -1))
+    to_owner = [(d, n) for d in range(SECOND - 1, 0, -1) for n in range(2)]
     sends = pack([pairs_at(d) for d in to_first], other)
     first_rows = [permute(x, d - FIRST) for d, x in zip(to_first, sends)]
-    owned = lax.all_to_all(amplitudes, "pair", split_axis=1, concat_axis=3, tiled=True)
-    gate, owned, *first_rows = lax.optimization_barrier((other, owned, *first_rows))
-    sends = pack([pairs_at(d) for d in to_second], gate)
+    gate = lax.optimization_barrier((other, *sends))[0]
+    sends = pack([pairs_at(d) for d in to_second] + [[(d, n == 0)] for d, n in to_owner], gate)
     second_rows = [permute(x, d - SECOND) for d, x in zip(to_second, sends)]
+    owner_rows = [permute(x, d, n == 1) for (d, n), x in zip(to_owner, sends[len(to_second) :])]
 
     picks = [((0, None) if d == far else (0, 2), at) for at, d in enumerate(to_first)]
     x = stop_sums(FIRST, (True, False), picks, True, other, first_rows).astype(F16)
+    x, second_rows, owner_rows = lax.optimization_barrier((x, second_rows, owner_rows))
     moving = permute(x, FIRST - SECOND)
 
-    gate = lax.optimization_barrier((other, x))[0]
-    sends = pack([[(d, mine)] for d in to_owner for mine in (True, False)], gate)
-    ways = [(d, n == 1) for d in to_owner for n in range(2)]
-    owner_rows = [permute(x, *way) for way, x in zip(ways, sends)]
+    gate, amplitudes = lax.optimization_barrier((other, amplitudes, x))[:2]
+    owned = lax.all_to_all(amplitudes, "pair", split_axis=1, concat_axis=3, tiled=True)
+
     picks = [((0, 2), at) for at in range(len(to_second))]
     local = stop_sums(SECOND, (True, False), picks, False, gate, second_rows)
     last = [add_on(moving[n : n + 1], local[n : n + 1])[0] for n in range(2)]
-    *last, owner_rows = lax.optimization_barrier((*last, owner_rows))
     moving = [permute(last[n], SECOND, n == 1) for n in range(2)]
 
     gate = lax.optimization_barrier((other, last[1]))[0]
+    *moving, owned = lax.optimization_barrier((*moving, owned))
     picks = [((0,), at) for at in range(len(owner_rows))]
     local = stop_sums(0, (True,), picks, False, gate, owner_rows)
     sums = (decode(moving[0][None])[0] + decode(moving[1][None])[0] + local)[0]

time: 85.7 us -> 82.6 us (0.964)
  waiting for transfers between devices: 25.6 us -> 16.3 us
  other arithmetic: 1.24 us -> 8.78 us
  local copies, waits for them, and re-layouts: 2.95 us -> 5.46 us
  starting transfers between devices: 49 us -> 46.8 us
  Pallas kernels: 6.21 us -> 4.37 us
    all_to_all x1, waiting for transfers between devices: 7.17 us -> 0.01 us  [on_device(): lax.all_to_all(amplitudes, 'pair', split_axis=1, concat_axis=3, tiled=True)]
    convert_element_type x3, other arithmetic: 0.11 us -> 3.03 us  [decode(): x = x.astype(F32)]
    unnamed x13 -> x27, local copies, waits for them, and re-layouts: 2.95 us -> 5.46 us
    ppermute x8, waiting for transfers between devices: 16.1 us -> 13.9 us  [permute(): return lax.ppermute(x, 'aux', pairs)]
    ppermute x8, starting transfers between devices: 26.9 us -> 24.7 us  [permute(): return lax.ppermute(x, 'aux', pairs)]
    squeeze x1, other arithmetic: 0.79 us -> 2.38 us  [on_device(): last = [add_on(moving[n:n + 1], local[n:n + 1])[0] for n in range(2)]]
    squeeze x1, other arithmetic: 0.23 us -> 1.38 us  [on_device(): sums = (decode(moving[0][None])[0] + decode(moving[1][None])[0] + local)[0]]
    pallas_call x3, Pallas kernels: 3.49 us -> 2.49 us  [stop_sums(): call(functools.partial(stop_kernel, chips, stop, owners, picks, scaled),...]
  transfers between devices with their start and end apart: 10 -> 10, of which waited for: 6 -> 6; matrix products, arithmetic and copies ran while one was open for 1% -> 7% of each run, Pallas kernels for 2% -> 3%
where the time goes in v10:
time: 82.6 us; the launch traced here: 82 us
  starting transfers between devices  46.8 us (57%)
  waiting for transfers between devices  16.3 us (20%)
  other arithmetic  8.78 us (11%)
  local copies, waits for them, and re-layouts  5.46 us (7%)
  Pallas kernels  4.37 us (5%)
    ppermute x8, starting transfers between devices, permute(): return lax.ppermute(x, 'aux', pairs)  24.7 us
    ppermute x8, waiting for transfers between devices, permute(): return lax.ppermute(x, 'aux', pairs)  13.9 us
    ppermute x1, starting transfers between devices, on_device(): other = lax.ppermute(other, 'aux', [(i, i ^ 1) for i in range(2 * chips)])  12.4 us
    all_to_all x1, starting transfers between devices, on_device(): lax.all_to_all(amplitudes, 'pair', split_axis=1, concat_axis=3, tiled=True)  9.67 us
    unnamed x27, local copies, waits for them, and re-layouts  5.46 us
    convert_element_type x3, other arithmetic, decode(): x = x.astype(F32)  3.03 us
    pallas_call x3, Pallas kernels, stop_sums(): call(functools.partial(stop_kernel, chips, stop, owners, picks, scaled),...  2.49 us
    squeeze x1, other arithmetic, on_device(): last = [add_on(moving[n:n + 1], local[n:n + 1])[0] for n in range(2)]  2.38 us
  transfers between devices with their start and end apart: 10, of which 6 were waited for; matrix products, arithmetic and copies ran while one was open for 7% of the time, Pallas kernels for 3%

profile of v10, /device:TPU:1, one launch (start us, length us, event | category | flops | bytes accessed | tf_op | source)
XLA Modules:
  0.0 82.0 jit_solution(12659602780706253470)
XLA Ops:
  0.0 2.3 %copy.12 = bf16[24,1,84,512]{3,2,0,1:T(8,128)(2,1)S(1)} copy(bf16[24,1,84,512]{3,0,2,1:T(8,128)(2,1)} %param.8) | data formatting | bytes 4128768 | tf_op args[1]
  2.3 0.1 split_cores.1
  2.4 12.4 %collective-permute-start = (bf16[12,84,512]{2,1,0:T(8,128)(2,1)S(1)}, bf16[12,84,512]{2,1,0:T(8,128)(2,1)S(1)}, u32[]{:S(2)}, u32[]{:S(2)}) collective-permute-start(bf16[12,84,512]{2,1,0:T(8,128)(2,1)S(1)} %split_cores.1), channel_id=1, source_target_pairs={{0,1},{1,0},{2,3},{3,2},{4,5},{5,4},{6,7},{7,6},{8,9},{9,8},{10,11... | collective-permute-start | bytes 3096584 | tf_op jit(solution)/shard_map/ppermute | solution.py:224
  14.8 2.3 %collective-permute-done.other = bf16[12,84,512]{2,1,0:T(8,128)(2,1)S(1)} collective-permute-done((bf16[12,84,512]{2,1,0:T(8,128)(2,1)S(1)}, bf16[12,84,512]{2,1,0:T(8,128)(2,1)S(1)}, u32[]{:S(2)}, u32[]{:S(2)}) %collective-permute-start) | collective-permute-done | bytes 1032224 | tf_op jit(solution)/shard_map/ppermute | solution.py:224
  17.2 5.3 %collective-permute-start.2 = (bf16[4,84,512]{2,1,0:T(8,128)(2,1)S(1)}, bf16[4,84,512]{2,1,0:T(8,128)(2,1)S(1)}, u32[]{:S(2)}, u32[]{:S(2)}) collective-permute-start(bf16[4,84,512]{2,1,0:T(8,128)(2,1)S(1)} %get-tuple-element.22), channel_id=1, source_target_pairs={{0,2},{1,23},{2,4},{3,1},{4,6},{5,3},{6,8},{7,5},{8,10},{9,7},{10,... | collective-permute-start | bytes 1032200 | tf_op jit(solution)/shard_map/ppermute | solution.py:198
  22.5 0.1 pack_rows.3
  22.5 2.2 %collective-permute-start.3 = (bf16[4,84,512]{2,1,0:T(8,128)(2,1)S(1)}, bf16[4,84,512]{2,1,0:T(8,128)(2,1)S(1)}, u32[]{:S(2)}, u32[]{:S(2)}) collective-permute-start(bf16[4,84,512]{2,1,0:T(8,128)(2,1)S(1)} %get-tuple-element.24), channel_id=1, source_target_pairs={{0,2},{1,23},{2,4},{3,1},{4,6},{5,3},{6,8},{7,5},{8,10},{9,7},{10,... | collective-permute-start | bytes 1032200 | tf_op jit(solution)/shard_map/ppermute | solution.py:198
  24.7 2.2 %collective-permute-start.1 = (bf16[2,84,512]{2,1,0:T(8,128)(2,1)S(1)}, bf16[2,84,512]{2,1,0:T(8,128)(2,1)S(1)}, u32[]{:S(2)}, u32[]{:S(2)}) collective-permute-start(bf16[2,84,512]{2,1,0:T(8,128)(2,1)S(1)} %get-tuple-element.21), channel_id=1, source_target_pairs={{0,4},{1,21},{2,6},{3,23},{4,8},{5,1},{6,10},{7,3},{8,12},{9,5},{1... | collective-permute-start | bytes 516104 | tf_op jit(solution)/shard_map/ppermute | solution.py:198
  26.9 3.4 %collective-permute-start.4 = (bf16[2,84,512]{2,1,0:T(8,128)(2,1)S(1)}, bf16[2,84,512]{2,1,0:T(8,128)(2,1)S(1)}, u32[]{:S(2)}, u32[]{:S(2)}) collective-permute-start(bf16[2,84,512]{2,1,0:T(8,128)(2,1)S(1)} %get-tuple-element.25), channel_id=1, source_target_pairs={{0,2},{1,23},{2,4},{3,1},{4,6},{5,3},{6,8},{7,5},{8,10},{9,7},{10,... | collective-permute-start | bytes 516104 | tf_op jit(solution)/shard_map/ppermute | solution.py:198
  30.3 1.9 %collective-permute-start.5 = (bf16[2,84,512]{2,1,0:T(8,128)(2,1)S(1)}, bf16[2,84,512]{2,1,0:T(8,128)(2,1)S(1)}, u32[]{:S(2)}, u32[]{:S(2)}) collective-permute-start(bf16[2,84,512]{2,1,0:T(8,128)(2,1)S(1)} %get-tuple-element.26), channel_id=1, source_target_pairs={{0,3},{1,22},{2,5},{3,0},{4,7},{5,2},{6,9},{7,4},{8,11},{9,6},{10,... | collective-permute-start | bytes 516104 | tf_op jit(solution)/shard_map/ppermute | solution.py:198
  32.2 2.3 %collective-permute-done.1.rest_0_ = bf16[2,84,512]{2,1,0:T(8,128)(2,1)S(1)} collective-permute-done((bf16[2,84,512]{2,1,0:T(8,128)(2,1)S(1)}, bf16[2,84,512]{2,1,0:T(8,128)(2,1)S(1)}, u32[]{:S(2)}, u32[]{:S(2)}) %collective-permute-start.1) | collective-permute-done | bytes 172064 | tf_op jit(solution)/shard_map/ppermute | solution.py:198
  34.5 0.0 collective-permute-done.2.rest_1_
  34.5 1.0 %stop_sums.3 = f32[2,784,128]{2,1,0:T(8,128)S(1)} custom-call(bf16[24,84,512]{2,1,0:T(8,128)(2,1)S(1)} %bitcast.64, bf16[12,84,512]{2,1,0:T(8,128)(2,1)S(1)} %collective-permute-done.other, bf16[2,84,512]{2,1,0:T(8,128)(2,1)S(1)} %collective-permute-done.1.rest_0_, bf16[4,84,512]{2,1,0:T(8,128)(2,1)S(1)} %collective-permute-done.2.rest_1_), custom_call_target="tpu_custom_call" | custom-call | tf_op jit(solution)/shard_map/stop_sums/pallas_call | solution.py:209
  35.6 0.8 convert_element_type.27
  36.4 0.5 collective-permute-done.4.rest_0_
  36.8 2.6 %collective-permute-done.5.rest_1_ = bf16[2,84,512]{2,1,0:T(8,128)(2,1)S(1)} collective-permute-done((bf16[2,84,512]{2,1,0:T(8,128)(2,1)S(1)}, bf16[2,84,512]{2,1,0:T(8,128)(2,1)S(1)}, u32[]{:S(2)}, u32[]{:S(2)}) %collective-permute-start.5) | collective-permute-done | bytes 172064 | tf_op jit(solution)/shard_map/ppermute | solution.py:198
  39.4 0.7 copy-done.3
  40.1 0.0 collective-permute-done.3.rest_0_
  40.1 0.7 copy-done.1
  40.8 3.7 %collective-permute-start.6 = (f16[2,784,128]{2,1,0:T(8,128)(2,1)}, f16[2,784,128]{2,1,0:T(8,128)(2,1)}, u32[]{:S(2)}, u32[]{:S(2)}) collective-permute-start(f16[2,784,128]{2,1,0:T(8,128)(2,1)} %convert_element_type.27), channel_id=1, source_target_pairs={{0,4},{1,21},{2,6},{3,23},{4,8},{5,1},{6,10},{7,3},{8,12},{9,5},{1... | collective-permute-start | bytes 1204232 | tf_op jit(solution)/shard_map/ppermute | solution.py:198
  44.5 0.6 iota_compare_fusion.2
  45.1 0.6 iota_compare_fusion
  45.6 9.7 %all-to-all-start = ((bf16[1,32,256,8]{2,3,0,1:T(8,128)(2,1)}), bf16[1,32,256,8]{2,3,0,1:T(8,128)(2,1)S(1)}, u32[]{:S(2)}, u32[]{:S(2)}) async-start(bf16[1,32,256,8]{2,3,0,1:T(8,128)(2,1)} %bitcast.72), calls=%async_computation | async-start | bytes 262144 | tf_op jit(solution)/shard_map/all_to_all | solution.py:242
  55.3 0.0 copy-start.2
  55.3 1.0 %copy-done.2 = bf16[4,84,512]{2,1,0:T(8,128)(2,1)S(1)} copy-done((bf16[4,84,512]{2,1,0:T(8,128)(2,1)S(1)}, bf16[4,84,512]{2,1,0:T(8,128)(2,1)}, u32[]{:S(2)}) %copy-start.2) | copy-done | bytes 344088
  56.3 0.8 stop_sums.4
  57.1 0.0 collective-permute-done.6
  57.1 1.1 %slice_convert_fusion.1 = (f32[1,784,128]{2,1,0:T(8,128)S(1)}, f32[1,784,128]{2,1,0:T(8,128)S(1)}) fusion(f16[2,784,128]{2,1,0:T(8,128)(2,1)} %collective-permute-done.6), kind=kLoop, calls=%fused_computation.20 | loop fusion | flops 200704 | bytes 1204224 | tf_op jit(solution)/shard_map/convert_element_type | solution.py:86
  58.3 0.0 copy-done.10
  58.3 0.0 copy-done.11
  58.3 0.0 copy-done.12
  58.3 2.4 %fusion.10 = (f16[784,128]{1,0:T(8,128)(2,1)}, f16[784,128]{1,0:T(8,128)(2,1)}) fusion(f32[2,784,128]{2,1,0:T(8,128)S(1)} %stop_sums.4, f32[128]{0:T(128)S(1)} %bitcast.74, f32[128]{0:T(128)S(1)} %bitcast.73, f32[128]{0:T(128)S(1)} %get-tuple-element.47, f32[128]{0:T(128)S(1)} %get-tuple-element.37, f32[128]{0:T(128)S(1)} %get-tuple-element.62, ...), kind=kLoop, calls=%fused_computation.17 | loop fusion | flops 1806336 | bytes 1614128 | tf_op jit(solution)/shard_map/squeeze | solution.py:246
  60.7 3.3 %collective-permute-start.7 = (f16[784,128]{1,0:T(8,128)(2,1)}, f16[784,128]{1,0:T(8,128)(2,1)}, u32[]{:S(2)}, u32[]{:S(2)}) collective-permute-start(f16[784,128]{1,0:T(8,128)(2,1)} %get-tuple-element.45), channel_id=1, source_target_pairs={{0,4},{1,21},{2,6},{3,23},{4,8},{5,1},{6,10},{7,3},{8,12},{9,5},{1... | collective-permute-start | bytes 602120 | tf_op jit(solution)/shard_map/ppermute | solution.py:198
  64.0 2.8 %collective-permute-start.8 = (f16[784,128]{1,0:T(8,128)(2,1)}, f16[784,128]{1,0:T(8,128)(2,1)}, u32[]{:S(2)}, u32[]{:S(2)}) collective-permute-start(f16[784,128]{1,0:T(8,128)(2,1)} %get-tuple-element.46), channel_id=1, source_target_pairs={{0,5},{1,20},{2,7},{3,22},{4,9},{5,0},{6,11},{7,2},{8,13},{9,4},{1... | collective-permute-start | bytes 602120 | tf_op jit(solution)/shard_map/ppermute | solution.py:198
  66.8 0.0 copy-done.4
  66.8 0.7 stop_sums.5
  67.5 0.8 copy-done
  68.3 0.0 copy-start.9
  68.3 0.0 all-to-all-done
  68.3 1.5 %collective-permute-done.7 = f16[784,128]{1,0:T(8,128)(2,1)} collective-permute-done((f16[784,128]{1,0:T(8,128)(2,1)}, f16[784,128]{1,0:T(8,128)(2,1)}, u32[]{:S(2)}, u32[]{:S(2)}) %collective-permute-start.7) | collective-permute-done | bytes 200736 | tf_op jit(solution)/shard_map/ppermute | solution.py:198
  69.8 7.1 %collective-permute-done.8 = f16[784,128]{1,0:T(8,128)(2,1)} collective-permute-done((f16[784,128]{1,0:T(8,128)(2,1)}, f16[784,128]{1,0:T(8,128)(2,1)}, u32[]{:S(2)}, u32[]{:S(2)}) %collective-permute-start.8) | collective-permute-done | bytes 200736 | tf_op jit(solution)/shard_map/ppermute | solution.py:198
  76.9 1.0 %convert_bitcast_fusion = f32[1,784,128]{2,1,0:T(8,128)S(1)} fusion(f16[784,128]{1,0:T(8,128)(2,1)} %collective-permute-done.8), kind=kLoop, calls=%fused_computation.2 | loop fusion | flops 100352 | bytes 602112 | tf_op jit(solution)/shard_map/convert_element_type | solution.py:86
  77.9 1.0 %convert_bitcast_fusion.1 = f32[1,784,128]{2,1,0:T(8,128)S(1)} fusion(f16[784,128]{1,0:T(8,128)(2,1)} %collective-permute-done.7), kind=kLoop, calls=%fused_computation.4 | loop fusion | flops 100352 | bytes 602112 | tf_op jit(solution)/shard_map/convert_element_type | solution.py:86
  78.9 1.4 %fusion.3.sums = f32[784,128]{1,0:T(8,128)S(1)} fusion(f32[1,784,128]{2,1,0:T(8,128)} %copy-done, f16[784,128]{1,0:T(8,128)(2,1)} %collective-permute-done.7, f16[784,128]{1,0:T(8,128)(2,1)} %collective-permute-done.8, f32[128]{0:T(128)S(1)} %get-tuple-element.60, f32[128]{0:T(128)S(1)} %get-tuple-element.59, f32[128]{0:T(128)S(1)} %get-tuple-element.58, ...), kind=kLoop, calls=%fused_computation.8 | loop fusion | flops 802816 | bytes 1207056 | tf_op jit(solution)/shard_map/squeeze | solution.py:253
  80.2 0.0 copy-done.5
  80.3 0.0 copy-done.6
  80.3 0.0 copy-done.7
  80.3 1.7 %residual.1 = f32[256,256]{1,0:T(8,128)} custom-call(s32[2]{0:T(128)S(1)} %bitcast.69, s32[2]{0:T(128)S(1)} %bitcast.70, s32[2]{0:T(128)S(1)} %bitcast.71, f32[100]{0:T(128)S(1)} %copy-done.9, f32[12,128]{1,0:T(8,128)S(1)} %bitcast.68, f32[784,128]{1,0:T(8,128)S(1)} %fusion.3.sums, bf16[256,256]{1,0:T(8,128)(2,1)S(1)} %bitcast.67), custom_call_target="tpu_custom_call" | custom-call | tf_op jit(solution)/shard_map/residual/pallas_call | solution.py:256
  (17 shorter events, 0.1 us)
Async XLA Ops:
  2.4 14.7 %collective-permute-start = (bf16[12,84,512]{2,1,0:T(8,128)(2,1)S(1)}, bf16[12,84,512]{2,1,0:T(8,128)(2,1)S(1)}, u32[]{:S(2)}, u32[]{:S(2)}) collective-permute-start(bf16[12,84,512]{2,1,0:T(8,128)(2,1)S(1)} %split_cores.1), channel_id=1, source_target_pairs={{0,1},{1,0},{2,3},{3,2},{4,5},{5,4},{6,7},{7,6},{8,9},{9,8},{10,11... | collective-permute-start | bytes 3096584 | tf_op jit(solution)/shard_map/ppermute | solution.py:224
  17.2 17.4 %collective-permute-start.2 = (bf16[4,84,512]{2,1,0:T(8,128)(2,1)S(1)}, bf16[4,84,512]{2,1,0:T(8,128)(2,1)S(1)}, u32[]{:S(2)}, u32[]{:S(2)}) collective-permute-start(bf16[4,84,512]{2,1,0:T(8,128)(2,1)S(1)} %get-tuple-element.22), channel_id=1, source_target_pairs={{0,2},{1,23},{2,4},{3,1},{4,6},{5,3},{6,8},{7,5},{8,10},{9,7},{10,... | collective-permute-start | bytes 1032200 | tf_op jit(solution)/shard_map/ppermute | solution.py:198
  22.5 17.6 %collective-permute-start.3 = (bf16[4,84,512]{2,1,0:T(8,128)(2,1)S(1)}, bf16[4,84,512]{2,1,0:T(8,128)(2,1)S(1)}, u32[]{:S(2)}, u32[]{:S(2)}) collective-permute-start(bf16[4,84,512]{2,1,0:T(8,128)(2,1)S(1)} %get-tuple-element.24), channel_id=1, source_target_pairs={{0,2},{1,23},{2,4},{3,1},{4,6},{5,3},{6,8},{7,5},{8,10},{9,7},{10,... | collective-permute-start | bytes 1032200 | tf_op jit(solution)/shard_map/ppermute | solution.py:198
  24.7 9.8 %collective-permute-start.1 = (bf16[2,84,512]{2,1,0:T(8,128)(2,1)S(1)}, bf16[2,84,512]{2,1,0:T(8,128)(2,1)S(1)}, u32[]{:S(2)}, u32[]{:S(2)}) collective-permute-start(bf16[2,84,512]{2,1,0:T(8,128)(2,1)S(1)} %get-tuple-element.21), channel_id=1, source_target_pairs={{0,4},{1,21},{2,6},{3,23},{4,8},{5,1},{6,10},{7,3},{8,12},{9,5},{1... | collective-permute-start | bytes 516104 | tf_op jit(solution)/shard_map/ppermute | solution.py:198
  26.9 9.9 %collective-permute-start.4 = (bf16[2,84,512]{2,1,0:T(8,128)(2,1)S(1)}, bf16[2,84,512]{2,1,0:T(8,128)(2,1)S(1)}, u32[]{:S(2)}, u32[]{:S(2)}) collective-permute-start(bf16[2,84,512]{2,1,0:T(8,128)(2,1)S(1)} %get-tuple-element.25), channel_id=1, source_target_pairs={{0,2},{1,23},{2,4},{3,1},{4,6},{5,3},{6,8},{7,5},{8,10},{9,7},{10,... | collective-permute-start | bytes 516104 | tf_op jit(solution)/shard_map/ppermute | solution.py:198
  30.3 9.1 %collective-permute-start.5 = (bf16[2,84,512]{2,1,0:T(8,128)(2,1)S(1)}, bf16[2,84,512]{2,1,0:T(8,128)(2,1)S(1)}, u32[]{:S(2)}, u32[]{:S(2)}) collective-permute-start(bf16[2,84,512]{2,1,0:T(8,128)(2,1)S(1)} %get-tuple-element.26), channel_id=1, source_target_pairs={{0,3},{1,22},{2,5},{3,0},{4,7},{5,2},{6,9},{7,4},{8,11},{9,6},{10,... | collective-permute-start | bytes 516104 | tf_op jit(solution)/shard_map/ppermute | solution.py:198
  39.4 0.7 copy-start.3
  40.1 0.7 copy-start.1
  40.8 16.3 %collective-permute-start.6 = (f16[2,784,128]{2,1,0:T(8,128)(2,1)}, f16[2,784,128]{2,1,0:T(8,128)(2,1)}, u32[]{:S(2)}, u32[]{:S(2)}) collective-permute-start(f16[2,784,128]{2,1,0:T(8,128)(2,1)} %convert_element_type.27), channel_id=1, source_target_pairs={{0,4},{1,21},{2,6},{3,23},{4,8},{5,1},{6,10},{7,3},{8,12},{9,5},{1... | collective-permute-start | bytes 1204232 | tf_op jit(solution)/shard_map/ppermute | solution.py:198
  45.6 22.7 %all-to-all-start = ((bf16[1,32,256,8]{2,3,0,1:T(8,128)(2,1)}), bf16[1,32,256,8]{2,3,0,1:T(8,128)(2,1)S(1)}, u32[]{:S(2)}, u32[]{:S(2)}) async-start(bf16[1,32,256,8]{2,3,0,1:T(8,128)(2,1)} %bitcast.72), calls=%async_computation | async-start | bytes 262144 | tf_op jit(solution)/shard_map/all_to_all | solution.py:242
  55.3 1.0 %copy-start.2 = (bf16[4,84,512]{2,1,0:T(8,128)(2,1)S(1)}, bf16[4,84,512]{2,1,0:T(8,128)(2,1)}, u32[]{:S(2)}) copy-start(bf16[4,84,512]{2,1,0:T(8,128)(2,1)} %copy-done.1) | copy-start | bytes 1032196
  56.3 2.0 %copy-start.10 = (pred[784]{0:T(1024)(128)(4,1)S(1)}, pred[784]{0:T(1024)(128)(4,1)}, u32[]{:S(2)}) copy-start(pred[784]{0:T(1024)(128)(4,1)} %get-tuple-element.66) | copy-start | bytes 2356
  56.3 2.0 %copy-start.11 = (pred[784]{0:T(1024)(128)(4,1)S(1)}, pred[784]{0:T(1024)(128)(4,1)}, u32[]{:S(2)}) copy-start(pred[784]{0:T(1024)(128)(4,1)} %get-tuple-element.65) | copy-start | bytes 2356
  56.3 2.0 %copy-start.12 = (pred[784]{0:T(1024)(128)(4,1)S(1)}, pred[784]{0:T(1024)(128)(4,1)}, u32[]{:S(2)}) copy-start(pred[784]{0:T(1024)(128)(4,1)} %iota_compare_fusion.2) | copy-start | bytes 2356
  57.1 9.7 %copy-start.4 = (bf16[2,84,512]{2,1,0:T(8,128)(2,1)S(1)}, bf16[2,84,512]{2,1,0:T(8,128)(2,1)}, u32[]{:S(2)}) copy-start(bf16[2,84,512]{2,1,0:T(8,128)(2,1)} %copy-done.3) | copy-start | bytes 516100
  60.7 9.1 %collective-permute-start.7 = (f16[784,128]{1,0:T(8,128)(2,1)}, f16[784,128]{1,0:T(8,128)(2,1)}, u32[]{:S(2)}, u32[]{:S(2)}) collective-permute-start(f16[784,128]{1,0:T(8,128)(2,1)} %get-tuple-element.45), channel_id=1, source_target_pairs={{0,4},{1,21},{2,6},{3,23},{4,8},{5,1},{6,10},{7,3},{8,12},{9,5},{1... | collective-permute-start | bytes 602120 | tf_op jit(solution)/shard_map/ppermute | solution.py:198
  64.0 12.9 %collective-permute-start.8 = (f16[784,128]{1,0:T(8,128)(2,1)}, f16[784,128]{1,0:T(8,128)(2,1)}, u32[]{:S(2)}, u32[]{:S(2)}) collective-permute-start(f16[784,128]{1,0:T(8,128)(2,1)} %get-tuple-element.46), channel_id=1, source_target_pairs={{0,5},{1,20},{2,7},{3,22},{4,9},{5,0},{6,11},{7,2},{8,13},{9,4},{1... | collective-permute-start | bytes 602120 | tf_op jit(solution)/shard_map/ppermute | solution.py:198
  67.5 0.8 copy-start
  68.3 11.9 %copy-start.5 = (f32[1536]{0:T(1024)S(1)}, f32[1536]{0:T(1024)}, u32[]{:S(2)}) copy-start(f32[1536]{0:T(1024)} %param.12) | copy-start | bytes 18436
  68.3 11.9 %copy-start.6 = (s32[1,1,2]{2,1,0:T(1,128)S(1)}, s32[1,1,2]{2,1,0:T(1,128)}, u32[]{:S(2)}) copy-start(s32[1,1,2]{2,1,0:T(1,128)} %param.9) | copy-start | bytes 28
  68.3 11.9 %copy-start.7 = (s32[1,1,2]{2,1,0:T(1,128)S(1)}, s32[1,1,2]{2,1,0:T(1,128)}, u32[]{:S(2)}) copy-start(s32[1,1,2]{2,1,0:T(1,128)} %param.10) | copy-start | bytes 28
  68.3 12.0 %copy-start.8 = (s32[1,1,2]{2,1,0:T(1,128)S(1)}, s32[1,1,2]{2,1,0:T(1,128)}, u32[]{:S(2)}) copy-start(s32[1,1,2]{2,1,0:T(1,128)} %param.11) | copy-start | bytes 28
  68.3 12.0 %copy-start.9 = (f32[100]{0:T(128)S(1)}, f32[100]{0:T(128)}, u32[]{:S(2)}) copy-start(f32[100]{0:T(128)} %occ.1) | copy-start | bytes 1204

commit v11 on v10

--- a/solution.py
+++ b/solution.py
@@ -247,7 +247,7 @@
     moving = [permute(last[n], SECOND, n == 1) for n in range(2)]
 
     gate = lax.optimization_barrier((other, last[1]))[0]
-    *moving, owned = lax.optimization_barrier((*moving, owned))
+    gate, owned = lax.optimization_barrier((gate, owned))
     picks = [((0,), at) for at in range(len(owner_rows))]
     local = stop_sums(0, (True,), picks, False, gate, owner_rows)
     sums = (decode(moving[0][None])[0] + decode(moving[1][None])[0] + local)[0]

time: 82.6 us -> 79.2 us (0.959)
  the two profiles are of different devices: /device:TPU:1 before, /device:TPU:4 now
where the time goes in v11:
time: 79.2 us; the launch traced here: 78.6 us
  starting transfers between devices  46.5 us (59%)
  waiting for transfers between devices  14.1 us (18%)
  other arithmetic  7.62 us (10%)
  local copies, waits for them, and re-layouts  5.61 us (7%)
  Pallas kernels  4.37 us (6%)
    ppermute x8, starting transfers between devices, permute(): return lax.ppermute(x, 'aux', pairs)  34.4 us
    ppermute x8, waiting for transfers between devices, permute(): return lax.ppermute(x, 'aux', pairs)  11.5 us
    all_to_all x1, starting transfers between devices, on_device(): lax.all_to_all(amplitudes, 'pair', split_axis=1, concat_axis=3, tiled=True)  10.2 us
    unnamed x27, local copies, waits for them, and re-layouts  5.61 us
    ppermute x1, waiting for transfers between devices, on_device(): other = lax.ppermute(other, 'aux', [(i, i ^ 1) for i in range(2 * chips)])  2.67 us
    pallas_call x3, Pallas kernels, stop_sums(): call(functools.partial(stop_kernel, chips, stop, owners, picks, scaled),...  2.49 us
    squeeze x1, other arithmetic, on_device(): last = [add_on(moving[n:n + 1], local[n:n + 1])[0] for n in range(2)]  2.37 us
    convert_element_type x3, other arithmetic, decode(): x = x.astype(F32)  2.09 us
  transfers between devices with their start and end apart: 10, of which 5 were waited for; matrix products, arithmetic and copies ran while one was open for 8% of the time, Pallas kernels for 3%

profile of v11, /device:TPU:4, one launch (start us, length us, event | category | flops | bytes accessed | tf_op | source)
XLA Modules:
  0.0 78.6 jit_solution(16221510353232681612)
XLA Ops:
  0.0 2.3 %copy.12 = bf16[24,1,84,512]{3,2,0,1:T(8,128)(2,1)S(1)} copy(bf16[24,1,84,512]{3,0,2,1:T(8,128)(2,1)} %param.8) | data formatting | bytes 4128768 | tf_op args[1]
  2.3 0.1 split_cores.1
  2.4 1.9 %collective-permute-start = (bf16[12,84,512]{2,1,0:T(8,128)(2,1)S(1)}, bf16[12,84,512]{2,1,0:T(8,128)(2,1)S(1)}, u32[]{:S(2)}, u32[]{:S(2)}) collective-permute-start(bf16[12,84,512]{2,1,0:T(8,128)(2,1)S(1)} %split_cores.1), channel_id=1, source_target_pairs={{0,1},{1,0},{2,3},{3,2},{4,5},{5,4},{6,7},{7,6},{8,9},{9,8},{10,11... | collective-permute-start | bytes 3096584 | tf_op jit(solution)/shard_map/ppermute | solution.py:224
  4.3 2.7 %collective-permute-done.other = bf16[12,84,512]{2,1,0:T(8,128)(2,1)S(1)} collective-permute-done((bf16[12,84,512]{2,1,0:T(8,128)(2,1)S(1)}, bf16[12,84,512]{2,1,0:T(8,128)(2,1)S(1)}, u32[]{:S(2)}, u32[]{:S(2)}) %collective-permute-start) | collective-permute-done | bytes 1032224 | tf_op jit(solution)/shard_map/ppermute | solution.py:224
  7.0 4.3 %collective-permute-start.2 = (bf16[4,84,512]{2,1,0:T(8,128)(2,1)S(1)}, bf16[4,84,512]{2,1,0:T(8,128)(2,1)S(1)}, u32[]{:S(2)}, u32[]{:S(2)}) collective-permute-start(bf16[4,84,512]{2,1,0:T(8,128)(2,1)S(1)} %get-tuple-element.21), channel_id=1, source_target_pairs={{0,2},{1,23},{2,4},{3,1},{4,6},{5,3},{6,8},{7,5},{8,10},{9,7},{10,... | collective-permute-start | bytes 1032200 | tf_op jit(solution)/shard_map/ppermute | solution.py:198
  11.3 0.1 pack_rows.3
  11.4 4.3 %collective-permute-start.3 = (bf16[4,84,512]{2,1,0:T(8,128)(2,1)S(1)}, bf16[4,84,512]{2,1,0:T(8,128)(2,1)S(1)}, u32[]{:S(2)}, u32[]{:S(2)}) collective-permute-start(bf16[4,84,512]{2,1,0:T(8,128)(2,1)S(1)} %get-tuple-element.23), channel_id=1, source_target_pairs={{0,2},{1,23},{2,4},{3,1},{4,6},{5,3},{6,8},{7,5},{8,10},{9,7},{10,... | collective-permute-start | bytes 1032200 | tf_op jit(solution)/shard_map/ppermute | solution.py:198
  15.7 7.3 %collective-permute-start.1 = (bf16[2,84,512]{2,1,0:T(8,128)(2,1)S(1)}, bf16[2,84,512]{2,1,0:T(8,128)(2,1)S(1)}, u32[]{:S(2)}, u32[]{:S(2)}) collective-permute-start(bf16[2,84,512]{2,1,0:T(8,128)(2,1)S(1)} %get-tuple-element.20), channel_id=1, source_target_pairs={{0,4},{1,21},{2,6},{3,23},{4,8},{5,1},{6,10},{7,3},{8,12},{9,5},{1... | collective-permute-start | bytes 516104 | tf_op jit(solution)/shard_map/ppermute | solution.py:198
  23.0 4.3 %collective-permute-start.4 = (bf16[2,84,512]{2,1,0:T(8,128)(2,1)S(1)}, bf16[2,84,512]{2,1,0:T(8,128)(2,1)S(1)}, u32[]{:S(2)}, u32[]{:S(2)}) collective-permute-start(bf16[2,84,512]{2,1,0:T(8,128)(2,1)S(1)} %get-tuple-element.24), channel_id=1, source_target_pairs={{0,2},{1,23},{2,4},{3,1},{4,6},{5,3},{6,8},{7,5},{8,10},{9,7},{10,... | collective-permute-start | bytes 516104 | tf_op jit(solution)/shard_map/ppermute | solution.py:198
  27.3 3.8 %collective-permute-start.5 = (bf16[2,84,512]{2,1,0:T(8,128)(2,1)S(1)}, bf16[2,84,512]{2,1,0:T(8,128)(2,1)S(1)}, u32[]{:S(2)}, u32[]{:S(2)}) collective-permute-start(bf16[2,84,512]{2,1,0:T(8,128)(2,1)S(1)} %get-tuple-element.25), channel_id=1, source_target_pairs={{0,3},{1,22},{2,5},{3,0},{4,7},{5,2},{6,9},{7,4},{8,11},{9,6},{10,... | collective-permute-start | bytes 516104 | tf_op jit(solution)/shard_map/ppermute | solution.py:198
  31.1 3.3 %collective-permute-done.1.rest_0_ = bf16[2,84,512]{2,1,0:T(8,128)(2,1)S(1)} collective-permute-done((bf16[2,84,512]{2,1,0:T(8,128)(2,1)S(1)}, bf16[2,84,512]{2,1,0:T(8,128)(2,1)S(1)}, u32[]{:S(2)}, u32[]{:S(2)}) %collective-permute-start.1) | collective-permute-done | bytes 172064 | tf_op jit(solution)/shard_map/ppermute | solution.py:198
  34.4 0.0 collective-permute-done.2.rest_1_
  34.4 1.0 %stop_sums.3 = f32[2,784,128]{2,1,0:T(8,128)S(1)} custom-call(bf16[24,84,512]{2,1,0:T(8,128)(2,1)S(1)} %bitcast.64, bf16[12,84,512]{2,1,0:T(8,128)(2,1)S(1)} %collective-permute-done.other, bf16[2,84,512]{2,1,0:T(8,128)(2,1)S(1)} %collective-permute-done.1.rest_0_, bf16[4,84,512]{2,1,0:T(8,128)(2,1)S(1)} %collective-permute-done.2.rest_1_), custom_call_target="tpu_custom_call" | custom-call | tf_op jit(solution)/shard_map/stop_sums/pallas_call | solution.py:209
  35.4 0.8 %convert_element_type.27 = f16[2,784,128]{2,1,0:T(8,128)(2,1)} convert(f32[2,784,128]{2,1,0:T(8,128)S(1)} %stop_sums.3) | non-fusion elementwise | flops 200704 | bytes 1204224 | tf_op jit(solution)/shard_map/convert_element_type | solution.py:237
  36.2 0.5 collective-permute-done.4.rest_0_
  36.7 1.0 %collective-permute-done.5.rest_1_ = bf16[2,84,512]{2,1,0:T(8,128)(2,1)S(1)} collective-permute-done((bf16[2,84,512]{2,1,0:T(8,128)(2,1)S(1)}, bf16[2,84,512]{2,1,0:T(8,128)(2,1)S(1)}, u32[]{:S(2)}, u32[]{:S(2)}) %collective-permute-start.5) | collective-permute-done | bytes 172064 | tf_op jit(solution)/shard_map/ppermute | solution.py:198
  37.7 0.7 copy-done.2
  38.3 0.0 collective-permute-done.3.rest_0_
  38.3 0.7 copy-done
  39.1 2.2 %collective-permute-start.6 = (f16[2,784,128]{2,1,0:T(8,128)(2,1)}, f16[2,784,128]{2,1,0:T(8,128)(2,1)}, u32[]{:S(2)}, u32[]{:S(2)}) collective-permute-start(f16[2,784,128]{2,1,0:T(8,128)(2,1)} %convert_element_type.27), channel_id=1, source_target_pairs={{0,4},{1,21},{2,6},{3,23},{4,8},{5,1},{6,10},{7,3},{8,12},{9,5},{1... | collective-permute-start | bytes 1204232 | tf_op jit(solution)/shard_map/ppermute | solution.py:198
  41.3 0.6 iota_compare_fusion.2
  41.9 0.6 iota_compare_fusion
  42.4 10.2 %all-to-all-start = ((bf16[1,32,256,8]{2,3,0,1:T(8,128)(2,1)}), bf16[1,32,256,8]{2,3,0,1:T(8,128)(2,1)S(1)}, u32[]{:S(2)}, u32[]{:S(2)}) async-start(bf16[1,32,256,8]{2,3,0,1:T(8,128)(2,1)} %bitcast.72), calls=%async_computation | async-start | bytes 262144 | tf_op jit(solution)/shard_map/all_to_all | solution.py:242
  52.7 0.0 copy-start.1
  52.7 1.0 %copy-done.1 = bf16[4,84,512]{2,1,0:T(8,128)(2,1)S(1)} copy-done((bf16[4,84,512]{2,1,0:T(8,128)(2,1)S(1)}, bf16[4,84,512]{2,1,0:T(8,128)(2,1)}, u32[]{:S(2)}) %copy-start.1) | copy-done | bytes 344088
  53.7 0.8 %stop_sums.4 = f32[2,784,128]{2,1,0:T(8,128)S(1)} custom-call(bf16[24,84,512]{2,1,0:T(8,128)(2,1)S(1)} %bitcast.65, bf16[12,84,512]{2,1,0:T(8,128)(2,1)S(1)} %collective-permute-done.other, bf16[4,84,512]{2,1,0:T(8,128)(2,1)S(1)} %copy-done.1), custom_call_target="tpu_custom_call" | custom-call | tf_op jit(solution)/shard_map/stop_sums/pallas_call | solution.py:209
  54.5 0.0 collective-permute-done.6
  54.5 1.1 %slice_convert_fusion.1 = (f32[1,784,128]{2,1,0:T(8,128)S(1)}, f32[1,784,128]{2,1,0:T(8,128)S(1)}) fusion(f16[2,784,128]{2,1,0:T(8,128)(2,1)} %collective-permute-done.6), kind=kLoop, calls=%fused_computation.20 | loop fusion | flops 200704 | bytes 1204224 | tf_op jit(solution)/shard_map/convert_element_type | solution.py:86
  55.6 0.0 copy-done.9
  55.6 0.0 copy-done.11
  55.6 0.0 copy-done.12
  55.6 2.4 %fusion.10 = (f16[784,128]{1,0:T(8,128)(2,1)}, f16[784,128]{1,0:T(8,128)(2,1)}) fusion(f32[2,784,128]{2,1,0:T(8,128)S(1)} %stop_sums.4, f32[128]{0:T(128)S(1)} %bitcast.74, f32[128]{0:T(128)S(1)} %bitcast.73, f32[128]{0:T(128)S(1)} %get-tuple-element.45, f32[128]{0:T(128)S(1)} %get-tuple-element.35, f32[128]{0:T(128)S(1)} %get-tuple-element.60, ...), kind=kLoop, calls=%fused_computation.17 | loop fusion | flops 1806336 | bytes 1614128 | tf_op jit(solution)/shard_map/squeeze | solution.py:246
  58.0 4.0 %collective-permute-start.8 = (f16[784,128]{1,0:T(8,128)(2,1)}, f16[784,128]{1,0:T(8,128)(2,1)}, u32[]{:S(2)}, u32[]{:S(2)}) collective-permute-start(f16[784,128]{1,0:T(8,128)(2,1)} %get-tuple-element.44), channel_id=1, source_target_pairs={{0,5},{1,20},{2,7},{3,22},{4,9},{5,0},{6,11},{7,2},{8,13},{9,4},{1... | collective-permute-start | bytes 602120 | tf_op jit(solution)/shard_map/ppermute | solution.py:198
  62.0 0.0 all-to-all-done
  62.1 4.2 %collective-permute-start.7 = (f16[784,128]{1,0:T(8,128)(2,1)}, f16[784,128]{1,0:T(8,128)(2,1)S(1)}, u32[]{:S(2)}, u32[]{:S(2)}) collective-permute-start(f16[784,128]{1,0:T(8,128)(2,1)} %get-tuple-element.43), channel_id=1, source_target_pairs={{0,4},{1,21},{2,6},{3,23},{4,8},{5,1},{6,10},{7,3},{8,12},{9,5},{1... | collective-permute-start | bytes 602120 | tf_op jit(solution)/shard_map/ppermute | solution.py:198
  66.2 0.0 copy-start.3
  66.3 0.9 %copy-done.3 = bf16[2,84,512]{2,1,0:T(8,128)(2,1)S(1)} copy-done((bf16[2,84,512]{2,1,0:T(8,128)(2,1)S(1)}, bf16[2,84,512]{2,1,0:T(8,128)(2,1)}, u32[]{:S(2)}) %copy-start.3) | copy-done | bytes 172056
  67.2 0.7 stop_sums.5
  67.9 0.0 copy-start.5
  67.9 0.0 copy-start.6
  67.9 0.0 copy-start.7
  67.9 0.0 copy-start.8
  67.9 0.0 collective-permute-done.8
  67.9 1.0 %convert_bitcast_fusion = f32[1,784,128]{2,1,0:T(8,128)S(1)} fusion(f16[784,128]{1,0:T(8,128)(2,1)} %collective-permute-done.8), kind=kLoop, calls=%fused_computation.2 | loop fusion | flops 100352 | bytes 602112 | tf_op jit(solution)/shard_map/convert_element_type | solution.py:86
  68.9 6.7 %collective-permute-done.7 = f16[784,128]{1,0:T(8,128)(2,1)S(1)} collective-permute-done((f16[784,128]{1,0:T(8,128)(2,1)}, f16[784,128]{1,0:T(8,128)(2,1)S(1)}, u32[]{:S(2)}, u32[]{:S(2)}) %collective-permute-start.7) | collective-permute-done | bytes 200736 | tf_op jit(solution)/shard_map/ppermute | solution.py:198
  75.7 0.0 copy-done.10
  75.7 1.2 %fusion.3.sums = f32[784,128]{1,0:T(8,128)S(1)} fusion(f32[1,784,128]{2,1,0:T(8,128)S(1)} %stop_sums.5, f16[784,128]{1,0:T(8,128)(2,1)S(1)} %collective-permute-done.7, f16[784,128]{1,0:T(8,128)(2,1)} %collective-permute-done.8, f32[128]{0:T(128)S(1)} %get-tuple-element.58, f32[128]{0:T(128)S(1)} %get-tuple-element.57, f32[128]{0:T(128)S(1)} %get-tuple-element.56, ...), kind=kLoop, calls=%fused_computation.8 | loop fusion | flops 802816 | bytes 1207056 | tf_op jit(solution)/shard_map/squeeze | solution.py:253
  76.9 1.7 %residual.1 = f32[256,256]{1,0:T(8,128)} custom-call(s32[2]{0:T(128)S(1)} %bitcast.69, s32[2]{0:T(128)S(1)} %bitcast.70, s32[2]{0:T(128)S(1)} %bitcast.71, f32[100]{0:T(128)S(1)} %copy-done.8, f32[12,128]{1,0:T(8,128)S(1)} %bitcast.68, f32[784,128]{1,0:T(8,128)S(1)} %fusion.3.sums, bf16[256,256]{1,0:T(8,128)(2,1)S(1)} %bitcast.67), custom_call_target="tpu_custom_call" | custom-call | tf_op jit(solution)/shard_map/residual/pallas_call | solution.py:256
  (17 shorter events, 0.1 us)
Async XLA Ops:
  2.4 4.6 %collective-permute-start = (bf16[12,84,512]{2,1,0:T(8,128)(2,1)S(1)}, bf16[12,84,512]{2,1,0:T(8,128)(2,1)S(1)}, u32[]{:S(2)}, u32[]{:S(2)}) collective-permute-start(bf16[12,84,512]{2,1,0:T(8,128)(2,1)S(1)} %split_cores.1), channel_id=1, source_target_pairs={{0,1},{1,0},{2,3},{3,2},{4,5},{5,4},{6,7},{7,6},{8,9},{9,8},{10,11... | collective-permute-start | bytes 3096584 | tf_op jit(solution)/shard_map/ppermute | solution.py:224
  7.0 27.4 %collective-permute-start.2 = (bf16[4,84,512]{2,1,0:T(8,128)(2,1)S(1)}, bf16[4,84,512]{2,1,0:T(8,128)(2,1)S(1)}, u32[]{:S(2)}, u32[]{:S(2)}) collective-permute-start(bf16[4,84,512]{2,1,0:T(8,128)(2,1)S(1)} %get-tuple-element.21), channel_id=1, source_target_pairs={{0,2},{1,23},{2,4},{3,1},{4,6},{5,3},{6,8},{7,5},{8,10},{9,7},{10,... | collective-permute-start | bytes 1032200 | tf_op jit(solution)/shard_map/ppermute | solution.py:198
  11.4 27.0 %collective-permute-start.3 = (bf16[4,84,512]{2,1,0:T(8,128)(2,1)S(1)}, bf16[4,84,512]{2,1,0:T(8,128)(2,1)S(1)}, u32[]{:S(2)}, u32[]{:S(2)}) collective-permute-start(bf16[4,84,512]{2,1,0:T(8,128)(2,1)S(1)} %get-tuple-element.23), channel_id=1, source_target_pairs={{0,2},{1,23},{2,4},{3,1},{4,6},{5,3},{6,8},{7,5},{8,10},{9,7},{10,... | collective-permute-start | bytes 1032200 | tf_op jit(solution)/shard_map/ppermute | solution.py:198
  15.7 18.7 %collective-permute-start.1 = (bf16[2,84,512]{2,1,0:T(8,128)(2,1)S(1)}, bf16[2,84,512]{2,1,0:T(8,128)(2,1)S(1)}, u32[]{:S(2)}, u32[]{:S(2)}) collective-permute-start(bf16[2,84,512]{2,1,0:T(8,128)(2,1)S(1)} %get-tuple-element.20), channel_id=1, source_target_pairs={{0,4},{1,21},{2,6},{3,23},{4,8},{5,1},{6,10},{7,3},{8,12},{9,5},{1... | collective-permute-start | bytes 516104 | tf_op jit(solution)/shard_map/ppermute | solution.py:198
  23.0 13.7 %collective-permute-start.4 = (bf16[2,84,512]{2,1,0:T(8,128)(2,1)S(1)}, bf16[2,84,512]{2,1,0:T(8,128)(2,1)S(1)}, u32[]{:S(2)}, u32[]{:S(2)}) collective-permute-start(bf16[2,84,512]{2,1,0:T(8,128)(2,1)S(1)} %get-tuple-element.24), channel_id=1, source_target_pairs={{0,2},{1,23},{2,4},{3,1},{4,6},{5,3},{6,8},{7,5},{8,10},{9,7},{10,... | collective-permute-start | bytes 516104 | tf_op jit(solution)/shard_map/ppermute | solution.py:198
  27.3 10.4 %collective-permute-start.5 = (bf16[2,84,512]{2,1,0:T(8,128)(2,1)S(1)}, bf16[2,84,512]{2,1,0:T(8,128)(2,1)S(1)}, u32[]{:S(2)}, u32[]{:S(2)}) collective-permute-start(bf16[2,84,512]{2,1,0:T(8,128)(2,1)S(1)} %get-tuple-element.25), channel_id=1, source_target_pairs={{0,3},{1,22},{2,5},{3,0},{4,7},{5,2},{6,9},{7,4},{8,11},{9,6},{10,... | collective-permute-start | bytes 516104 | tf_op jit(solution)/shard_map/ppermute | solution.py:198
  37.7 0.7 copy-start.2
  38.3 0.7 copy-start
  39.1 15.4 %collective-permute-start.6 = (f16[2,784,128]{2,1,0:T(8,128)(2,1)}, f16[2,784,128]{2,1,0:T(8,128)(2,1)}, u32[]{:S(2)}, u32[]{:S(2)}) collective-permute-start(f16[2,784,128]{2,1,0:T(8,128)(2,1)} %convert_element_type.27), channel_id=1, source_target_pairs={{0,4},{1,21},{2,6},{3,23},{4,8},{5,1},{6,10},{7,3},{8,12},{9,5},{1... | collective-permute-start | bytes 1204232 | tf_op jit(solution)/shard_map/ppermute | solution.py:198
  42.4 19.6 %all-to-all-start = ((bf16[1,32,256,8]{2,3,0,1:T(8,128)(2,1)}), bf16[1,32,256,8]{2,3,0,1:T(8,128)(2,1)S(1)}, u32[]{:S(2)}, u32[]{:S(2)}) async-start(bf16[1,32,256,8]{2,3,0,1:T(8,128)(2,1)} %bitcast.72), calls=%async_computation | async-start | bytes 262144 | tf_op jit(solution)/shard_map/all_to_all | solution.py:242
  52.7 1.0 %copy-start.1 = (bf16[4,84,512]{2,1,0:T(8,128)(2,1)S(1)}, bf16[4,84,512]{2,1,0:T(8,128)(2,1)}, u32[]{:S(2)}) copy-start(bf16[4,84,512]{2,1,0:T(8,128)(2,1)} %copy-done) | copy-start | bytes 1032196
  53.7 1.9 %copy-start.9 = (pred[784]{0:T(1024)(128)(4,1)S(1)}, pred[784]{0:T(1024)(128)(4,1)}, u32[]{:S(2)}) copy-start(pred[784]{0:T(1024)(128)(4,1)} %get-tuple-element.64) | copy-start | bytes 2356
  53.7 1.9 %copy-start.11 = (pred[784]{0:T(1024)(128)(4,1)S(1)}, pred[784]{0:T(1024)(128)(4,1)}, u32[]{:S(2)}) copy-start(pred[784]{0:T(1024)(128)(4,1)} %get-tuple-element.63) | copy-start | bytes 2356
  53.7 2.0 %copy-start.12 = (pred[784]{0:T(1024)(128)(4,1)S(1)}, pred[784]{0:T(1024)(128)(4,1)}, u32[]{:S(2)}) copy-start(pred[784]{0:T(1024)(128)(4,1)} %iota_compare_fusion.2) | copy-start | bytes 2356
  58.0 9.9 %collective-permute-start.8 = (f16[784,128]{1,0:T(8,128)(2,1)}, f16[784,128]{1,0:T(8,128)(2,1)}, u32[]{:S(2)}, u32[]{:S(2)}) collective-permute-start(f16[784,128]{1,0:T(8,128)(2,1)} %get-tuple-element.44), channel_id=1, source_target_pairs={{0,5},{1,20},{2,7},{3,22},{4,9},{5,0},{6,11},{7,2},{8,13},{9,4},{1... | collective-permute-start | bytes 602120 | tf_op jit(solution)/shard_map/ppermute | solution.py:198
  62.1 13.6 %collective-permute-start.7 = (f16[784,128]{1,0:T(8,128)(2,1)}, f16[784,128]{1,0:T(8,128)(2,1)S(1)}, u32[]{:S(2)}, u32[]{:S(2)}) collective-permute-start(f16[784,128]{1,0:T(8,128)(2,1)} %get-tuple-element.43), channel_id=1, source_target_pairs={{0,4},{1,21},{2,6},{3,23},{4,8},{5,1},{6,10},{7,3},{8,12},{9,5},{1... | collective-permute-start | bytes 602120 | tf_op jit(solution)/shard_map/ppermute | solution.py:198
  66.2 0.9 %copy-start.3 = (bf16[2,84,512]{2,1,0:T(8,128)(2,1)S(1)}, bf16[2,84,512]{2,1,0:T(8,128)(2,1)}, u32[]{:S(2)}) copy-start(bf16[2,84,512]{2,1,0:T(8,128)(2,1)} %copy-done.2) | copy-start | bytes 516100
  67.2 8.5 %copy-start.10 = (pred[784]{0:T(1024)(128)(4,1)S(1)}, pred[784]{0:T(1024)(128)(4,1)}, u32[]{:S(2)}) copy-start(pred[784]{0:T(1024)(128)(4,1)} %get-tuple-element.64) | copy-start | bytes 2356
  67.8 9.0 %copy-start.4 = (f32[1536]{0:T(1024)S(1)}, f32[1536]{0:T(1024)}, u32[]{:S(2)}) copy-start(f32[1536]{0:T(1024)} %param.12) | copy-start | bytes 18436
  67.9 9.0 %copy-start.5 = (s32[1,1,2]{2,1,0:T(1,128)S(1)}, s32[1,1,2]{2,1,0:T(1,128)}, u32[]{:S(2)}) copy-start(s32[1,1,2]{2,1,0:T(1,128)} %param.9) | copy-start | bytes 28
  67.9 9.0 %copy-start.6 = (s32[1,1,2]{2,1,0:T(1,128)S(1)}, s32[1,1,2]{2,1,0:T(1,128)}, u32[]{:S(2)}) copy-start(s32[1,1,2]{2,1,0:T(1,128)} %param.10) | copy-start | bytes 28
  67.9 9.0 %copy-start.7 = (s32[1,1,2]{2,1,0:T(1,128)S(1)}, s32[1,1,2]{2,1,0:T(1,128)}, u32[]{:S(2)}) copy-start(s32[1,1,2]{2,1,0:T(1,128)} %param.11) | copy-start | bytes 28
  67.9 9.0 %copy-start.8 = (f32[100]{0:T(128)S(1)}, f32[100]{0:T(128)}, u32[]{:S(2)}) copy-start(f32[100]{0:T(128)} %occ.1) | copy-start | bytes 1204

commit v12 on v11

--- a/solution.py
+++ b/solution.py
@@ -238,11 +238,11 @@
     x, second_rows, owner_rows = lax.optimization_barrier((x, second_rows, owner_rows))
     moving = permute(x, FIRST - SECOND)
 
-    gate, amplitudes = lax.optimization_barrier((other, amplitudes, x))[:2]
-    owned = lax.all_to_all(amplitudes, "pair", split_axis=1, concat_axis=3, tiled=True)
-
+    gate = lax.optimization_barrier((other, x))[0]
     picks = [((0, 2), at) for at in range(len(to_second))]
     local = stop_sums(SECOND, (True, False), picks, False, gate, second_rows)
+    amplitudes = lax.optimization_barrier((amplitudes, local))[0]
+    owned = lax.all_to_all(amplitudes, "pair", split_axis=1, concat_axis=3, tiled=True)
     last = [add_on(moving[n : n + 1], local[n : n + 1])[0] for n in range(2)]
     moving = [permute(last[n], SECOND, n == 1) for n in range(2)]
 

time: 79.2 us -> 78.8 us (level)
  the two profiles are of different devices: /device:TPU:4 before, /device:TPU:64 now
where the time goes in v12:
time: 78.8 us; the launch traced here: 78.2 us
  starting transfers between devices  43.4 us (55%)
  waiting for transfers between devices  17.5 us (22%)
  other arithmetic  8.58 us (11%)
  Pallas kernels  4.38 us (6%)
  local copies, waits for them, and re-layouts  4.1 us (5%)
    ppermute x8, starting transfers between devices, permute(): return lax.ppermute(x, 'aux', pairs)  31.5 us
    all_to_all x1, starting transfers between devices, on_device(): lax.all_to_all(amplitudes, 'pair', split_axis=1, concat_axis=3, tiled=True)  9.95 us
    ppermute x8, waiting for transfers between devices, permute(): return lax.ppermute(x, 'aux', pairs)  9.59 us
    all_to_all x1, waiting for transfers between devices, on_device(): lax.all_to_all(amplitudes, 'pair', split_axis=1, concat_axis=3, tiled=True)  5.2 us
    unnamed x19, local copies, waits for them, and re-layouts  4.1 us
    ppermute x1, waiting for transfers between devices, on_device(): other = lax.ppermute(other, 'aux', [(i, i ^ 1) for i in range(2 * chips)])  2.67 us
    squeeze x1, other arithmetic, on_device(): last = [add_on(moving[n:n + 1], local[n:n + 1])[0] for n in range(2)]  2.54 us
    pallas_call x3, Pallas kernels, stop_sums(): call(functools.partial(stop_kernel, chips, stop, owners, picks, scaled),...  2.49 us
  transfers between devices with their start and end apart: 10, of which 4 were waited for; matrix products, arithmetic and copies ran while one was open for 9% of the time, Pallas kernels for 3%

profile of v12, /device:TPU:64, one launch (start us, length us, event | category | flops | bytes accessed | tf_op | source)
XLA Modules:
  0.0 78.2 jit_solution(13532605481143429057)
XLA Ops:
  0.0 2.3 %copy.12 = bf16[24,1,84,512]{3,2,0,1:T(8,128)(2,1)S(1)} copy(bf16[24,1,84,512]{3,0,2,1:T(8,128)(2,1)} %param.8) | data formatting | bytes 4128768 | tf_op args[1]
  2.3 0.1 split_cores.1
  2.4 1.9 %collective-permute-start = (bf16[12,84,512]{2,1,0:T(8,128)(2,1)S(1)}, bf16[12,84,512]{2,1,0:T(8,128)(2,1)S(1)}, u32[]{:S(2)}, u32[]{:S(2)}) collective-permute-start(bf16[12,84,512]{2,1,0:T(8,128)(2,1)S(1)} %split_cores.1), channel_id=1, source_target_pairs={{0,1},{1,0},{2,3},{3,2},{4,5},{5,4},{6,7},{7,6},{8,9},{9,8},{10,11... | collective-permute-start | bytes 3096584 | tf_op jit(solution)/shard_map/ppermute | solution.py:224
  4.3 2.7 %collective-permute-done.other = bf16[12,84,512]{2,1,0:T(8,128)(2,1)S(1)} collective-permute-done((bf16[12,84,512]{2,1,0:T(8,128)(2,1)S(1)}, bf16[12,84,512]{2,1,0:T(8,128)(2,1)S(1)}, u32[]{:S(2)}, u32[]{:S(2)}) %collective-permute-start) | collective-permute-done | bytes 1032224 | tf_op jit(solution)/shard_map/ppermute | solution.py:224
  7.0 4.3 %collective-permute-start.2 = (bf16[4,84,512]{2,1,0:T(8,128)(2,1)S(1)}, bf16[4,84,512]{2,1,0:T(8,128)(2,1)S(1)}, u32[]{:S(2)}, u32[]{:S(2)}) collective-permute-start(bf16[4,84,512]{2,1,0:T(8,128)(2,1)S(1)} %get-tuple-element.21), channel_id=1, source_target_pairs={{0,2},{1,23},{2,4},{3,1},{4,6},{5,3},{6,8},{7,5},{8,10},{9,7},{10,... | collective-permute-start | bytes 1032200 | tf_op jit(solution)/shard_map/ppermute | solution.py:198
  11.3 0.1 pack_rows.3
  11.4 4.3 %collective-permute-start.3 = (bf16[4,84,512]{2,1,0:T(8,128)(2,1)S(1)}, bf16[4,84,512]{2,1,0:T(8,128)(2,1)S(1)}, u32[]{:S(2)}, u32[]{:S(2)}) collective-permute-start(bf16[4,84,512]{2,1,0:T(8,128)(2,1)S(1)} %get-tuple-element.23), channel_id=1, source_target_pairs={{0,2},{1,23},{2,4},{3,1},{4,6},{5,3},{6,8},{7,5},{8,10},{9,7},{10,... | collective-permute-start | bytes 1032200 | tf_op jit(solution)/shard_map/ppermute | solution.py:198
  15.7 7.3 %collective-permute-start.1 = (bf16[2,84,512]{2,1,0:T(8,128)(2,1)S(1)}, bf16[2,84,512]{2,1,0:T(8,128)(2,1)S(1)}, u32[]{:S(2)}, u32[]{:S(2)}) collective-permute-start(bf16[2,84,512]{2,1,0:T(8,128)(2,1)S(1)} %get-tuple-element.20), channel_id=1, source_target_pairs={{0,4},{1,21},{2,6},{3,23},{4,8},{5,1},{6,10},{7,3},{8,12},{9,5},{1... | collective-permute-start | bytes 516104 | tf_op jit(solution)/shard_map/ppermute | solution.py:198
  23.0 4.3 %collective-permute-start.4 = (bf16[2,84,512]{2,1,0:T(8,128)(2,1)S(1)}, bf16[2,84,512]{2,1,0:T(8,128)(2,1)S(1)}, u32[]{:S(2)}, u32[]{:S(2)}) collective-permute-start(bf16[2,84,512]{2,1,0:T(8,128)(2,1)S(1)} %get-tuple-element.24), channel_id=1, source_target_pairs={{0,2},{1,23},{2,4},{3,1},{4,6},{5,3},{6,8},{7,5},{8,10},{9,7},{10,... | collective-permute-start | bytes 516104 | tf_op jit(solution)/shard_map/ppermute | solution.py:198
  27.3 2.9 %collective-permute-start.5 = (bf16[2,84,512]{2,1,0:T(8,128)(2,1)S(1)}, bf16[2,84,512]{2,1,0:T(8,128)(2,1)S(1)}, u32[]{:S(2)}, u32[]{:S(2)}) collective-permute-start(bf16[2,84,512]{2,1,0:T(8,128)(2,1)S(1)} %get-tuple-element.25), channel_id=1, source_target_pairs={{0,3},{1,22},{2,5},{3,0},{4,7},{5,2},{6,9},{7,4},{8,11},{9,6},{10,... | collective-permute-start | bytes 516104 | tf_op jit(solution)/shard_map/ppermute | solution.py:198
  30.2 3.7 %collective-permute-done.1.rest_0_ = bf16[2,84,512]{2,1,0:T(8,128)(2,1)S(1)} collective-permute-done((bf16[2,84,512]{2,1,0:T(8,128)(2,1)S(1)}, bf16[2,84,512]{2,1,0:T(8,128)(2,1)S(1)}, u32[]{:S(2)}, u32[]{:S(2)}) %collective-permute-start.1) | collective-permute-done | bytes 172064 | tf_op jit(solution)/shard_map/ppermute | solution.py:198
  33.9 0.0 collective-permute-done.2.rest_1_
  33.9 1.0 %stop_sums.3 = f32[2,784,128]{2,1,0:T(8,128)S(1)} custom-call(bf16[24,84,512]{2,1,0:T(8,128)(2,1)S(1)} %bitcast.64, bf16[12,84,512]{2,1,0:T(8,128)(2,1)S(1)} %collective-permute-done.other, bf16[2,84,512]{2,1,0:T(8,128)(2,1)S(1)} %collective-permute-done.1.rest_0_, bf16[4,84,512]{2,1,0:T(8,128)(2,1)S(1)} %collective-permute-done.2.rest_1_), custom_call_target="tpu_custom_call" | custom-call | tf_op jit(solution)/shard_map/stop_sums/pallas_call | solution.py:209
  34.9 0.8 %convert_element_type.27 = f16[2,784,128]{2,1,0:T(8,128)(2,1)} convert(f32[2,784,128]{2,1,0:T(8,128)S(1)} %stop_sums.3) | non-fusion elementwise | flops 200704 | bytes 1204224 | tf_op jit(solution)/shard_map/convert_element_type | solution.py:237
  35.8 0.0 collective-permute-done.4.rest_0_
  35.8 0.0 collective-permute-done.5.rest_1_
  35.8 0.0 collective-permute-done.3.rest_0_
  35.8 4.4 %collective-permute-start.6 = (f16[2,784,128]{2,1,0:T(8,128)(2,1)}, f16[2,784,128]{2,1,0:T(8,128)(2,1)}, u32[]{:S(2)}, u32[]{:S(2)}) collective-permute-start(f16[2,784,128]{2,1,0:T(8,128)(2,1)} %convert_element_type.27), channel_id=1, source_target_pairs={{0,4},{1,21},{2,6},{3,23},{4,8},{5,1},{6,10},{7,3},{8,12},{9,5},{1... | collective-permute-start | bytes 1204232 | tf_op jit(solution)/shard_map/ppermute | solution.py:198
  40.2 0.6 iota_compare_fusion.2
  40.8 0.6 iota_compare_fusion
  41.4 0.8 %stop_sums.4 = f32[2,784,128]{2,1,0:T(8,128)S(1)} custom-call(bf16[24,84,512]{2,1,0:T(8,128)(2,1)S(1)} %bitcast.65, bf16[12,84,512]{2,1,0:T(8,128)(2,1)S(1)} %collective-permute-done.other, bf16[4,84,512]{2,1,0:T(8,128)(2,1)S(1)} %collective-permute-done.3.rest_0_), custom_call_target="tpu_custom_call" | custom-call | tf_op jit(solution)/shard_map/stop_sums/pallas_call | solution.py:209
  42.2 0.0 copy-done.1
  42.2 0.0 copy-start
  42.2 0.9 %copy-done = f32[2,784,128]{2,1,0:T(8,128)} copy-done((f32[2,784,128]{2,1,0:T(8,128)}, f32[2,784,128]{2,1,0:T(8,128)S(1)}, u32[]{:S(2)}) %copy-start) | copy-done | bytes 802840
  43.1 10.0 %all-to-all-start = ((bf16[1,32,256,8]{2,3,0,1:T(8,128)(2,1)}), bf16[1,32,256,8]{2,3,0,1:T(8,128)(2,1)S(1)}, u32[]{:S(2)}, u32[]{:S(2)}) async-start(bf16[1,32,256,8]{2,3,0,1:T(8,128)(2,1)} %bitcast.72), calls=%async_computation | async-start | bytes 262144 | tf_op jit(solution)/shard_map/all_to_all | solution.py:245
  53.0 0.0 collective-permute-done.6
  53.0 1.1 %slice_convert_fusion.1 = (f32[1,784,128]{2,1,0:T(8,128)S(1)}, f32[1,784,128]{2,1,0:T(8,128)S(1)}) fusion(f16[2,784,128]{2,1,0:T(8,128)(2,1)} %collective-permute-done.6), kind=kLoop, calls=%fused_computation.20 | loop fusion | flops 200704 | bytes 1204224 | tf_op jit(solution)/shard_map/convert_element_type | solution.py:86
  54.1 0.8 exponential_bitcast_fusion.5
  54.9 2.5 %fusion.10 = (f16[784,128]{1,0:T(8,128)(2,1)}, f16[784,128]{1,0:T(8,128)(2,1)}) fusion(f32[2,784,128]{2,1,0:T(8,128)} %copy-done, f32[128]{0:T(128)S(1)} %bitcast.74, f32[128]{0:T(128)S(1)} %bitcast.73, f32[128]{0:T(128)S(1)} %get-tuple-element.45, f32[128]{0:T(128)S(1)} %get-tuple-element.35, f32[128]{0:T(128)S(1)} %get-tuple-element.60, ...), kind=kLoop, calls=%fused_computation.17 | loop fusion | flops 1806336 | bytes 1614128 | tf_op jit(solution)/shard_map/squeeze | solution.py:246
  57.5 1.9 %collective-permute-start.8 = (f16[784,128]{1,0:T(8,128)(2,1)}, f16[784,128]{1,0:T(8,128)(2,1)}, u32[]{:S(2)}, u32[]{:S(2)}) collective-permute-start(f16[784,128]{1,0:T(8,128)(2,1)} %get-tuple-element.44), channel_id=1, source_target_pairs={{0,5},{1,20},{2,7},{3,22},{4,9},{5,0},{6,11},{7,2},{8,13},{9,4},{1... | collective-permute-start | bytes 602120 | tf_op jit(solution)/shard_map/ppermute | solution.py:198
  59.4 5.2 %all-to-all-done = bf16[1,32,256,8]{2,3,0,1:T(8,128)(2,1)S(1)} async-done(((bf16[1,32,256,8]{2,3,0,1:T(8,128)(2,1)}), bf16[1,32,256,8]{2,3,0,1:T(8,128)(2,1)S(1)}, u32[]{:S(2)}, u32[]{:S(2)}) %all-to-all-start) | async-done | bytes 131104 | tf_op jit(solution)/shard_map/all_to_all | solution.py:245
  64.6 2.2 %collective-permute-start.7 = (f16[784,128]{1,0:T(8,128)(2,1)}, f16[784,128]{1,0:T(8,128)(2,1)S(1)}, u32[]{:S(2)}, u32[]{:S(2)}) collective-permute-start(f16[784,128]{1,0:T(8,128)(2,1)} %get-tuple-element.43), channel_id=1, source_target_pairs={{0,4},{1,21},{2,6},{3,23},{4,8},{5,1},{6,10},{7,3},{8,12},{9,5},{1... | collective-permute-start | bytes 602120 | tf_op jit(solution)/shard_map/ppermute | solution.py:198
  66.7 0.0 copy-start.2
  66.8 0.9 %copy-done.2 = bf16[2,84,512]{2,1,0:T(8,128)(2,1)S(1)} copy-done((bf16[2,84,512]{2,1,0:T(8,128)(2,1)S(1)}, bf16[2,84,512]{2,1,0:T(8,128)(2,1)}, u32[]{:S(2)}) %copy-start.2) | copy-done | bytes 172056
  67.7 0.7 stop_sums.5
  68.4 0.0 copy-start.5
  68.4 0.0 copy-start.6
  68.4 0.0 copy-start.7
  68.4 0.0 collective-permute-done.8
  68.4 1.0 %convert_bitcast_fusion = f32[1,784,128]{2,1,0:T(8,128)S(1)} fusion(f16[784,128]{1,0:T(8,128)(2,1)} %collective-permute-done.8), kind=kLoop, calls=%fused_computation.2 | loop fusion | flops 100352 | bytes 602112 | tf_op jit(solution)/shard_map/convert_element_type | solution.py:86
  69.4 5.8 %collective-permute-done.7 = f16[784,128]{1,0:T(8,128)(2,1)S(1)} collective-permute-done((f16[784,128]{1,0:T(8,128)(2,1)}, f16[784,128]{1,0:T(8,128)(2,1)S(1)}, u32[]{:S(2)}, u32[]{:S(2)}) %collective-permute-start.7) | collective-permute-done | bytes 200736 | tf_op jit(solution)/shard_map/ppermute | solution.py:198
  75.3 1.2 %fusion.3.sums = f32[784,128]{1,0:T(8,128)S(1)} fusion(f32[1,784,128]{2,1,0:T(8,128)S(1)} %stop_sums.5, f16[784,128]{1,0:T(8,128)(2,1)S(1)} %collective-permute-done.7, f16[784,128]{1,0:T(8,128)(2,1)} %collective-permute-done.8, f32[128]{0:T(128)S(1)} %get-tuple-element.58, f32[128]{0:T(128)S(1)} %get-tuple-element.57, f32[128]{0:T(128)S(1)} %get-tuple-element.56, ...), kind=kLoop, calls=%fused_computation.8 | loop fusion | flops 802816 | bytes 1207056 | tf_op jit(solution)/shard_map/squeeze | solution.py:253
  76.5 0.0 copy-done.3
  76.5 0.0 copy-done.4
  76.5 0.0 copy-done.5
  76.5 0.0 copy-done.6
  76.5 0.0 copy-done.7
  76.5 1.7 %residual.1 = f32[256,256]{1,0:T(8,128)} custom-call(s32[2]{0:T(128)S(1)} %bitcast.69, s32[2]{0:T(128)S(1)} %bitcast.70, s32[2]{0:T(128)S(1)} %bitcast.71, f32[100]{0:T(128)S(1)} %copy-done.7, f32[12,128]{1,0:T(8,128)S(1)} %bitcast.68, f32[784,128]{1,0:T(8,128)S(1)} %fusion.3.sums, bf16[256,256]{1,0:T(8,128)(2,1)S(1)} %bitcast.67), custom_call_target="tpu_custom_call" | custom-call | tf_op jit(solution)/shard_map/residual/pallas_call | solution.py:256
  (9 shorter events, 0.1 us)
Async XLA Ops:
  2.4 4.6 %collective-permute-start = (bf16[12,84,512]{2,1,0:T(8,128)(2,1)S(1)}, bf16[12,84,512]{2,1,0:T(8,128)(2,1)S(1)}, u32[]{:S(2)}, u32[]{:S(2)}) collective-permute-start(bf16[12,84,512]{2,1,0:T(8,128)(2,1)S(1)} %split_cores.1), channel_id=1, source_target_pairs={{0,1},{1,0},{2,3},{3,2},{4,5},{5,4},{6,7},{7,6},{8,9},{9,8},{10,11... | collective-permute-start | bytes 3096584 | tf_op jit(solution)/shard_map/ppermute | solution.py:224
  7.0 26.9 %collective-permute-start.2 = (bf16[4,84,512]{2,1,0:T(8,128)(2,1)S(1)}, bf16[4,84,512]{2,1,0:T(8,128)(2,1)S(1)}, u32[]{:S(2)}, u32[]{:S(2)}) collective-permute-start(bf16[4,84,512]{2,1,0:T(8,128)(2,1)S(1)} %get-tuple-element.21), channel_id=1, source_target_pairs={{0,2},{1,23},{2,4},{3,1},{4,6},{5,3},{6,8},{7,5},{8,10},{9,7},{10,... | collective-permute-start | bytes 1032200 | tf_op jit(solution)/shard_map/ppermute | solution.py:198
  11.4 24.4 %collective-permute-start.3 = (bf16[4,84,512]{2,1,0:T(8,128)(2,1)S(1)}, bf16[4,84,512]{2,1,0:T(8,128)(2,1)S(1)}, u32[]{:S(2)}, u32[]{:S(2)}) collective-permute-start(bf16[4,84,512]{2,1,0:T(8,128)(2,1)S(1)} %get-tuple-element.23), channel_id=1, source_target_pairs={{0,2},{1,23},{2,4},{3,1},{4,6},{5,3},{6,8},{7,5},{8,10},{9,7},{10,... | collective-permute-start | bytes 1032200 | tf_op jit(solution)/shard_map/ppermute | solution.py:198
  15.7 18.3 %collective-permute-start.1 = (bf16[2,84,512]{2,1,0:T(8,128)(2,1)S(1)}, bf16[2,84,512]{2,1,0:T(8,128)(2,1)S(1)}, u32[]{:S(2)}, u32[]{:S(2)}) collective-permute-start(bf16[2,84,512]{2,1,0:T(8,128)(2,1)S(1)} %get-tuple-element.20), channel_id=1, source_target_pairs={{0,4},{1,21},{2,6},{3,23},{4,8},{5,1},{6,10},{7,3},{8,12},{9,5},{1... | collective-permute-start | bytes 516104 | tf_op jit(solution)/shard_map/ppermute | solution.py:198
  23.0 12.8 %collective-permute-start.4 = (bf16[2,84,512]{2,1,0:T(8,128)(2,1)S(1)}, bf16[2,84,512]{2,1,0:T(8,128)(2,1)S(1)}, u32[]{:S(2)}, u32[]{:S(2)}) collective-permute-start(bf16[2,84,512]{2,1,0:T(8,128)(2,1)S(1)} %get-tuple-element.24), channel_id=1, source_target_pairs={{0,2},{1,23},{2,4},{3,1},{4,6},{5,3},{6,8},{7,5},{8,10},{9,7},{10,... | collective-permute-start | bytes 516104 | tf_op jit(solution)/shard_map/ppermute | solution.py:198
  27.3 8.5 %collective-permute-start.5 = (bf16[2,84,512]{2,1,0:T(8,128)(2,1)S(1)}, bf16[2,84,512]{2,1,0:T(8,128)(2,1)S(1)}, u32[]{:S(2)}, u32[]{:S(2)}) collective-permute-start(bf16[2,84,512]{2,1,0:T(8,128)(2,1)S(1)} %get-tuple-element.25), channel_id=1, source_target_pairs={{0,3},{1,22},{2,5},{3,0},{4,7},{5,2},{6,9},{7,4},{8,11},{9,6},{10,... | collective-permute-start | bytes 516104 | tf_op jit(solution)/shard_map/ppermute | solution.py:198
  35.8 6.4 %copy-start.1 = (bf16[2,84,512]{2,1,0:T(8,128)(2,1)}, bf16[2,84,512]{2,1,0:T(8,128)(2,1)S(1)}, u32[]{:S(2)}) copy-start(bf16[2,84,512]{2,1,0:T(8,128)(2,1)S(1)} %collective-permute-done.5.rest_1_) | copy-start | bytes 516100
  35.8 17.3 %collective-permute-start.6 = (f16[2,784,128]{2,1,0:T(8,128)(2,1)}, f16[2,784,128]{2,1,0:T(8,128)(2,1)}, u32[]{:S(2)}, u32[]{:S(2)}) collective-permute-start(f16[2,784,128]{2,1,0:T(8,128)(2,1)} %convert_element_type.27), channel_id=1, source_target_pairs={{0,4},{1,21},{2,6},{3,23},{4,8},{5,1},{6,10},{7,3},{8,12},{9,5},{1... | collective-permute-start | bytes 1204232 | tf_op jit(solution)/shard_map/ppermute | solution.py:198
  42.2 0.9 %copy-start = (f32[2,784,128]{2,1,0:T(8,128)}, f32[2,784,128]{2,1,0:T(8,128)S(1)}, u32[]{:S(2)}) copy-start(f32[2,784,128]{2,1,0:T(8,128)S(1)} %stop_sums.4) | copy-start | bytes 2408452
  43.1 21.5 %all-to-all-start = ((bf16[1,32,256,8]{2,3,0,1:T(8,128)(2,1)}), bf16[1,32,256,8]{2,3,0,1:T(8,128)(2,1)S(1)}, u32[]{:S(2)}, u32[]{:S(2)}) async-start(bf16[1,32,256,8]{2,3,0,1:T(8,128)(2,1)} %bitcast.72), calls=%async_computation | async-start | bytes 262144 | tf_op jit(solution)/shard_map/all_to_all | solution.py:245
  57.5 10.9 %collective-permute-start.8 = (f16[784,128]{1,0:T(8,128)(2,1)}, f16[784,128]{1,0:T(8,128)(2,1)}, u32[]{:S(2)}, u32[]{:S(2)}) collective-permute-start(f16[784,128]{1,0:T(8,128)(2,1)} %get-tuple-element.44), channel_id=1, source_target_pairs={{0,5},{1,20},{2,7},{3,22},{4,9},{5,0},{6,11},{7,2},{8,13},{9,4},{1... | collective-permute-start | bytes 602120 | tf_op jit(solution)/shard_map/ppermute | solution.py:198
  64.6 10.7 %collective-permute-start.7 = (f16[784,128]{1,0:T(8,128)(2,1)}, f16[784,128]{1,0:T(8,128)(2,1)S(1)}, u32[]{:S(2)}, u32[]{:S(2)}) collective-permute-start(f16[784,128]{1,0:T(8,128)(2,1)} %get-tuple-element.43), channel_id=1, source_target_pairs={{0,4},{1,21},{2,6},{3,23},{4,8},{5,1},{6,10},{7,3},{8,12},{9,5},{1... | collective-permute-start | bytes 602120 | tf_op jit(solution)/shard_map/ppermute | solution.py:198
  66.7 0.9 %copy-start.2 = (bf16[2,84,512]{2,1,0:T(8,128)(2,1)S(1)}, bf16[2,84,512]{2,1,0:T(8,128)(2,1)}, u32[]{:S(2)}) copy-start(bf16[2,84,512]{2,1,0:T(8,128)(2,1)} %copy-done.1) | copy-start | bytes 516100
  67.7 7.6 %copy-start.8 = (pred[784]{0:T(1024)(128)(4,1)S(1)}, pred[784]{0:T(1024)(128)(4,1)}, u32[]{:S(2)}) copy-start(pred[784]{0:T(1024)(128)(4,1)} %get-tuple-element.64) | copy-start | bytes 2356
  68.4 8.1 %copy-start.3 = (f32[1536]{0:T(1024)S(1)}, f32[1536]{0:T(1024)}, u32[]{:S(2)}) copy-start(f32[1536]{0:T(1024)} %param.12) | copy-start | bytes 18436
  68.4 8.1 %copy-start.4 = (s32[1,1,2]{2,1,0:T(1,128)S(1)}, s32[1,1,2]{2,1,0:T(1,128)}, u32[]{:S(2)}) copy-start(s32[1,1,2]{2,1,0:T(1,128)} %param.9) | copy-start | bytes 28
  68.4 8.1 %copy-start.5 = (s32[1,1,2]{2,1,0:T(1,128)S(1)}, s32[1,1,2]{2,1,0:T(1,128)}, u32[]{:S(2)}) copy-start(s32[1,1,2]{2,1,0:T(1,128)} %param.10) | copy-start | bytes 28
  68.4 8.1 %copy-start.6 = (s32[1,1,2]{2,1,0:T(1,128)S(1)}, s32[1,1,2]{2,1,0:T(1,128)}, u32[]{:S(2)}) copy-start(s32[1,1,2]{2,1,0:T(1,128)} %param.11) | copy-start | bytes 28
  68.4 8.1 %copy-start.7 = (f32[100]{0:T(128)S(1)}, f32[100]{0:T(128)}, u32[]{:S(2)}) copy-start(f32[100]{0:T(128)} %occ.1) | copy-start | bytes 1204
